TPU v7x, 32 devices: a whole 2x2x4 slice. The times are simulated.
32 devices in a mesh: groups: 2 (over x), lib: 16 (over z, y, core).
Axes of the slice: x: 2, y: 2, z: 4, core: 2. Of those that a mesh axis runs over, the one named last changes fastest.
Arguments:
- spectra: bfloat16 [512, 4096], P(('groups', 'lib')), parts along dimension 0, may hold values from -6 to 6
- library: bfloat16 [8192, 4096], P('lib'), may hold values from -6 to 6
- cand_block: int32 [512, 8], P(('groups', 'lib')), parts along dimension 0, may hold values from 0 to 15, all different within a row; in each aligned block of 16 rows (0 to 15, 16 to 31, ...) at most 12 rows name the same one
- cand_local: int32 [512, 8, 8], P(('groups', 'lib')), parts along dimension 0, may hold values from 0 to 511
Outputs:
- profiles: float32 [512, 64, 1024], P(('groups', 'lib')), parts along dimension 0
There are 2 independent parts, one for each index of `groups`. A program takes and returns all parts, laid end to end along the dimension named above; an argument that names none is the same for every part. Nothing has to cross between parts.
Inputs may be any that keep to these rules, and one draw needn't show every extreme that they name: `cand_block`: each query names 8 different blocks; among the 16 queries of one device no block is named by more than 12 of them, and 12 is reached.
All inputs are finite; a program needn't handle non-finite values.
Results may differ from a plain program's by a relative error of at most 0.0029.
Values may be sent and summed in bfloat16 or wider, within the bound.
No kernel may reach another device: no remote copies, remote signals or barrier semaphores. Data moves between devices by JAX's collectives and lax.ppermute only.
A program may use at most 128 MiB of HBM per device.

v0:
```python
import functools

import jax
import jax.numpy as jnp
from jax import lax
from jax.experimental import pallas as pl
from jax.experimental.pallas import tpu as pltpu
from jax.sharding import PartitionSpec as P

SHIFTS = 1024
BG = 32
EPSILON = 1e-06
LANES = 128
VMEM_LIMIT = 48 * 1024 * 1024
NEAR = 4
ROW_SLOTS = 4
SLOT_LANES = LANES // ROW_SLOTS
PER_TOUCH = 8
CHAINS = 1
GROUPS = 4
WIDTH = LANES // GROUPS


def rounded(value, unit):
    return -(-value // unit) * unit


def depth_of(num_query, touches, devices):
    return min(num_query, max(3, 3 * num_query * touches // (2 * devices)))


def record_values(found):
    lane = lax.broadcasted_iota(jnp.int32, found.shape, 1) % SLOT_LANES
    low = pltpu.roll(found, LANES - PER_TOUCH, 1)
    return jnp.where(lane < PER_TOUCH, found * 16 + low, found).astype(jnp.int32)


def prepare_kernel(depth, spectra_ref, named_ref, wanted_ref, out_ref, table_ref, rows_ref):
    num_query, num_bins = spectra_ref.shape
    blocks = num_bins // LANES
    values = spectra_ref[...].astype(jnp.float32)
    zeros = jnp.zeros((num_query, LANES), jnp.float32)
    wide = jnp.concatenate([values, zeros], axis=1)
    total, length = wide, 1
    while length < 2 * BG:
        total = total + pltpu.roll(total, length, 1)
        length *= 2
    total = total + pltpu.roll(wide, length, 1)
    total = pltpu.roll(total, total.shape[1] - BG, 1)[:, :num_bins]
    centered = values - total / (2 * BG + 1)
    factor = lax.rsqrt(jnp.mean(centered * centered, axis=1, keepdims=True) + EPSILON)
    prepared = (centered * factor).astype(jnp.bfloat16)
    row = lax.broadcasted_iota(jnp.int32, (LANES, LANES), 0)
    col = lax.broadcasted_iota(jnp.int32, (LANES, LANES), 1)
    flip = jnp.where(row + col == LANES - 1, 1.0, 0.0).astype(jnp.bfloat16)
    for block in range(blocks):
        piece = prepared[:, block * LANES : (block + 1) * LANES]
        turned = jnp.dot(piece, flip, preferred_element_type=jnp.float32)
        rows_ref[pl.ds(blocks - 1 - block, num_query, stride=blocks), :] = turned
    out_ref[0 : num_query * blocks, :] = rows_ref[...].astype(jnp.bfloat16)

    touches = named_ref.shape[1]
    touched = num_query * touches
    records = table_ref.shape[0]
    per_block = rounded(depth, ROW_SLOTS) // ROW_SLOTS
    touch = lax.broadcasted_iota(jnp.int32, (touched, num_query), 0)
    query = lax.broadcasted_iota(jnp.int32, (touched, num_query), 1)
    owner = jnp.where(touch // touches == query, 1.0, 0.0).astype(jnp.bfloat16)
    named = named_ref[...].astype(jnp.float32).astype(jnp.bfloat16)
    spread = jnp.dot(owner, named, preferred_element_type=jnp.float32)
    touch = lax.broadcasted_iota(jnp.int32, (touched, touches), 0)
    which = lax.broadcasted_iota(jnp.int32, (touched, touches), 1)
    block_col = jnp.sum(
        jnp.where(touch % touches == which, spread, 0.0), axis=1, keepdims=True
    )
    row = lax.broadcasted_iota(jnp.int32, (touched, touched), 0)
    col = lax.broadcasted_iota(jnp.int32, (touched, touched), 1)
    block_row = jnp.sum(jnp.where(row == col, block_col, 0.0), axis=0, keepdims=True)
    earlier = (block_col == block_row) & (row < col)
    rank = jnp.sum(jnp.where(earlier, 1.0, 0.0), axis=0, keepdims=True).astype(jnp.int32)
    place = block_row.astype(jnp.int32) * per_block + rank // ROW_SLOTS
    wanted = wanted_ref[...]
    high = (wanted // 16).astype(jnp.float32).astype(jnp.bfloat16)
    low = (wanted % 16).astype(jnp.float32).astype(jnp.bfloat16)
    unit = lax.broadcasted_iota(jnp.int32, (PER_TOUCH, LANES), 0)
    lane = lax.broadcasted_iota(jnp.int32, (PER_TOUCH, LANES), 1)
    row = lax.broadcasted_iota(jnp.int32, (records, touched), 0)
    touch = lax.broadcasted_iota(jnp.int32, (touched, LANES), 0)
    wide_lane = lax.broadcasted_iota(jnp.int32, (touched, LANES), 1)
    found = jnp.zeros((records, LANES), jnp.float32)
    for group in range(ROW_SLOTS):
        start = group * SLOT_LANES
        to_high = jnp.where(lane == start + unit, 1.0, 0.0).astype(jnp.bfloat16)
        to_low = jnp.where(lane == start + PER_TOUCH + unit, 1.0, 0.0).astype(jnp.bfloat16)
        data = jnp.dot(high, to_high, preferred_element_type=jnp.float32)
        data = data + jnp.dot(low, to_low, preferred_element_type=jnp.float32)
        data = jnp.where(
            wide_lane == start + 2 * PER_TOUCH, (touch + 1).astype(jnp.float32), data
        ).astype(jnp.bfloat16)
        pick = jnp.where((row == place) & (rank % ROW_SLOTS == group), 1.0, 0.0)
        found = found + jnp.dot(
            pick.astype(jnp.bfloat16), data, preferred_element_type=jnp.float32
        )
    out_ref[num_query * blocks :, :] = found.astype(jnp.bfloat16)
    table_ref[...] = record_values(found)


def prepare(spectra, named, wanted, depth, records):
    num_query, num_bins = spectra.shape
    rows = num_query * num_bins // LANES
    return pl.pallas_call(
        functools.partial(prepare_kernel, depth),
        out_shape=(
            jax.ShapeDtypeStruct((rows + records, LANES), jnp.bfloat16),
            jax.ShapeDtypeStruct((records, LANES), jnp.int32),
        ),
        scratch_shapes=[pltpu.VMEM((rows, LANES), jnp.float32)],
        compiler_params=pltpu.CompilerParams(vmem_limit_bytes=VMEM_LIMIT),
        name="prepare",
    )(spectra, named, wanted)


def profile_kernel(depth, num_query, touches, me_ref, *refs):
    shards, library_ref, refs = refs[:NEAR], refs[NEAR], refs[NEAR + 1 :]
    outs, refs = refs[:NEAR], refs[NEAR:]
    (
        query_ref, record_ref, found_ref, table_ref, answer_ref,
        cand_ref, packed_ref, spectrum_ref, left_ref, right_ref, product_ref, sem_ref,
    ) = refs
    per_touch = PER_TOUCH
    rows = 2 * per_touch
    blocks = library_ref.shape[1]
    offsets = SHIFTS // LANES
    first = offsets // 2 + 1
    tiles = blocks // GROUPS
    query_rows = num_query * blocks
    per_block = rounded(depth, ROW_SLOTS) // ROW_SLOTS
    row = lax.broadcasted_iota(jnp.int32, (8, LANES), 0)
    lane = lax.broadcasted_iota(jnp.int32, (8, LANES), 1)
    lane16 = lax.broadcasted_iota(jnp.int32, (rows, LANES), 1)

    copies = [
        pltpu.make_async_copy(shards[e], query_ref.at[e], sem_ref.at[e]) for e in range(NEAR)
    ]
    for copy in copies:
        copy.start()
    cand_ref[...] = jnp.zeros(cand_ref.shape, cand_ref.dtype)
    right_ref[...] = jnp.zeros(right_ref.shape, right_ref.dtype)
    found_ref[...] = jnp.zeros(found_ref.shape, found_ref.dtype)
    for e in range(NEAR):
        copies[e].wait()
        record_ref[...] = query_ref[e, query_rows:, :].astype(jnp.float32)
        found_ref[e * per_block : (e + 1) * per_block, :] = record_values(
            record_ref[pl.ds(me_ref[0] * per_block, per_block), :]
        )
    to_scalars = pltpu.make_async_copy(found_ref, table_ref, sem_ref.at[NEAR])
    to_scalars.start()
    to_scalars.wait()

    def entry(slot):
        e = slot // depth
        s = slot % depth
        return e, e * per_block + s // ROW_SLOTS, s % ROW_SLOTS * SLOT_LANES

    def touch_of(slot):
        _, line, start = entry(slot)
        return table_ref[line, start + 2 * per_touch] - 1

    def choose(pieces):
        value = pieces[0]
        for group in range(1, GROUPS):
            value = jnp.where(lane16 < group * WIDTH, value, pieces[group])
        return value

    def gather(slot, half):
        _, line, start = entry(slot)
        for k in range(per_touch):
            wanted = table_ref[line, start + k]
            cand_ref[pl.ds(first * rows + half * per_touch + k, blocks, stride=rows), :] = (
                library_ref[wanted].astype(jnp.float32)
            )
        square = jnp.zeros((per_touch, LANES), jnp.float32)
        for b in range(blocks):
            piece = cand_ref[pl.ds((first + b) * rows + half * per_touch, per_touch), :]
            square = square + piece * piece
        mean = jnp.sum(square, axis=1, keepdims=True) / (blocks * LANES)
        return lax.rsqrt(mean + EPSILON)

    def make_left():
        for b in range(blocks + offsets + 1):
            packed_ref[pl.ds(rows * b, rows), :] = cand_ref[pl.ds(rows * b, rows), :].astype(
                jnp.bfloat16
            )
        for t in range(tiles + offsets + 1):
            given = [packed_ref[pl.ds(rows * (t + tiles * g), rows), :] for g in range(GROUPS)]
            turned = []
            for c in range(GROUPS):
                mixed = choose([given[(a + c) % GROUPS] for a in range(GROUPS)])
                turned.append(pltpu.roll(mixed, WIDTH * c, 1) if c else mixed)
            for a in range(GROUPS):
                left_ref[a, pl.ds(rows * t, rows), :] = choose(
                    [turned[(g - a) % GROUPS] for g in range(GROUPS)]
                )

    def make_right(slot, half):
        query = jnp.maximum(touch_of(slot), 0) // touches
        spectrum_ref[half] = query_ref[
            entry(slot)[0], pl.ds(pl.multiple_of(query * blocks, blocks), blocks), :
        ].astype(jnp.float32)
        zero = jnp.zeros((8, LANES), jnp.float32)
        before = (zero, zero)
        before_shifted = jnp.zeros((16, LANES), jnp.bfloat16)
        columns = slice(half * LANES, (half + 1) * LANES)
        for b in range(blocks + 1):
            if b < blocks:
                wide = jnp.broadcast_to(spectrum_ref[half, pl.ds(b, 1), :], (8, LANES))
                now = tuple(
                    pltpu.roll(wide, 1 + 8 * h, 1, stride=1, stride_axis=0) for h in range(2)
                )
            else:
                now = (zero, zero)
            shifted = jnp.concatenate(
                [jnp.where(lane > row + 8 * h, now[h], before[h]) for h in range(2)], axis=0
            ).astype(jnp.bfloat16)
            j = blocks - 1 - b
            place = 0 if j < 0 else (j % tiles + 1) * LANES + j // tiles * WIDTH
            right_ref[pl.ds(place, 16), columns] = shifted
            for c in range(16, WIDTH, 16):
                right_ref[pl.ds(place + c, 16), columns] = pltpu.roll(
                    jnp.where(lane16 < LANES - c, shifted, before_shifted), c, 1
                )
            before, before_shifted = now, shifted

    def sums(low, high):
        left = jnp.concatenate(
            [
                jnp.concatenate(
                    [
                        left_ref[a, pl.ds(rows * t, rows * (offsets + 1)), :]
                        for t in range(tiles + 1)
                    ],
                    axis=1,
                )
                for a in range(low, high)
            ],
            axis=0,
        )
        return jnp.dot(left, right_ref[...], preferred_element_type=jnp.float32)

    slots = NEAR * depth
    height = GROUPS // CHAINS * (offsets + 1) * rows

    @pl.loop(0, slots // 2)
    def _(pair):
        @pl.when((touch_of(2 * pair) >= 0) | (touch_of(2 * pair + 1) >= 0))
        def _():
            scales = [gather(2 * pair + half, half) for half in range(2)]
            make_left()
            for half in range(2):
                make_right(2 * pair + half, half)
            step = GROUPS // CHAINS
            for c in range(CHAINS):
                product_ref[c * height : (c + 1) * height, :] = sums(step * c, step * (c + 1))

            def found(a, o, half):
                at = (a * (offsets + 1) + o) * rows + half * per_touch
                return product_ref[at : at + per_touch, half * LANES : (half + 1) * LANES]

            for o in range(offsets):
                both = []
                for half in range(2):
                    total = found(0, o + 1, half)
                    for a in range(1, GROUPS):
                        shift = WIDTH * a
                        total = total + pltpu.roll(
                            jnp.where(
                                lane < LANES - shift, found(a, o + 1, half), found(a, o, half)
                            ),
                            shift,
                            1,
                        )
                    both.append(total * scales[half])
                answer_ref[
                    pl.ds(pl.multiple_of(16 * pair, 16), 16), o * LANES : (o + 1) * LANES
                ] = jnp.concatenate(both, axis=0).astype(jnp.bfloat16)

    back = [
        pltpu.make_async_copy(
            answer_ref.at[pl.ds(e * depth * per_touch, depth * per_touch), :],
            outs[e],
            sem_ref.at[e],
        )
        for e in range(NEAR)
    ]
    for copy in back:
        copy.start()
    for copy in back:
        copy.wait()


def profile(part, depth, num_query, touches, me, shards, library):
    blocks = library.shape[1]
    offsets = SHIFTS // LANES
    tiles = blocks // GROUPS
    records = shards[0].shape[0] - num_query * blocks
    per_block = rounded(depth, ROW_SLOTS) // ROW_SLOTS
    table = (rounded(NEAR * per_block, 8), LANES)
    smem = pl.BlockSpec(memory_space=pltpu.SMEM)
    vmem = pl.BlockSpec(memory_space=pltpu.VMEM)
    hbm = pl.BlockSpec(memory_space=pl.ANY)
    answers = NEAR * depth * PER_TOUCH
    flops = answers * 2 * (offsets + 1) * (blocks + 4) * LANES * LANES
    return pl.pallas_call(
        functools.partial(profile_kernel, depth, num_query, touches),
        out_shape=[
            jax.ShapeDtypeStruct((depth * PER_TOUCH, SHIFTS), jnp.bfloat16)
            for _ in range(NEAR)
        ],
        in_specs=[smem] + [hbm] * NEAR + [vmem],
        out_specs=[hbm] * NEAR,
        scratch_shapes=[
            pltpu.VMEM((NEAR, *shards[0].shape), jnp.bfloat16),
            pltpu.VMEM((records, LANES), jnp.float32),
            pltpu.VMEM(table, jnp.int32),
            pltpu.SMEM(table, jnp.int32),
            pltpu.VMEM((answers, SHIFTS), jnp.bfloat16),
            pltpu.VMEM(((blocks + offsets + 1) * 16, LANES), jnp.float32),
            pltpu.VMEM(((blocks + offsets + 1) * 16, LANES), jnp.bfloat16),
            pltpu.VMEM((2, blocks, LANES), jnp.float32),
            pltpu.VMEM((GROUPS, (tiles + offsets + 1) * 16, LANES), jnp.bfloat16),
            pltpu.VMEM(((tiles + 1) * LANES, 2 * LANES), jnp.bfloat16),
            pltpu.VMEM((GROUPS * (offsets + 1) * 16, 2 * LANES), jnp.float32),
            pltpu.SemaphoreType.DMA((NEAR + 1,)),
        ],
        compiler_params=pltpu.CompilerParams(vmem_limit_bytes=VMEM_LIMIT),
        cost_estimate=pl.CostEstimate(
            flops=8 * flops, bytes_accessed=8 * 1024 * 1024, transcendentals=0
        ),
        name=f"profile_{part}",
    )(me, *shards, library)


def unpack_kernel(part, depth, me_ref, table_ref, *refs):
    got, refs = refs[:NEAR], refs[-3:]
    out_ref, stage_ref, sem_ref = refs
    per_block = rounded(depth, ROW_SLOTS) // ROW_SLOTS

    def copy(slot, touch):
        return pltpu.make_async_copy(stage_ref.at[slot], out_ref.at[touch], sem_ref.at[slot])

    def touch_of(e, s):
        block = jnp.bitwise_xor(me_ref[0], NEAR * part + e)
        line = block * per_block + s // ROW_SLOTS
        return table_ref[line, s % ROW_SLOTS * SLOT_LANES + 2 * PER_TOUCH] - 1

    for e in range(NEAR):
        for s in range(depth):
            touch = touch_of(e, s)
            slot = e * depth + s

            @pl.when(touch >= 0)
            def _():
                stage_ref[slot] = got[e][s * PER_TOUCH : (s + 1) * PER_TOUCH, :].astype(
                    jnp.float32
                )
                copy(slot, touch).start()

    for e in range(NEAR):
        for s in range(depth):
            touch = touch_of(e, s)

            @pl.when(touch >= 0)
            def _():
                copy(e * depth + s, touch).wait()


def unpack(part, depth, touched, me, table, got, out):
    shifts = got[0].shape[1]
    smem = pl.BlockSpec(memory_space=pltpu.SMEM)
    vmem = pl.BlockSpec(memory_space=pltpu.VMEM)
    hbm = pl.BlockSpec(memory_space=pl.ANY)
    more = () if out is None else (out,)
    return pl.pallas_call(
        functools.partial(unpack_kernel, part, depth),
        out_shape=jax.ShapeDtypeStruct((touched, PER_TOUCH, shifts), jnp.float32),
        in_specs=[smem] * 2 + [vmem] * NEAR + [hbm] * len(more),
        out_specs=hbm,
        scratch_shapes=[
            pltpu.VMEM((NEAR * depth, PER_TOUCH, shifts), jnp.float32),
            pltpu.SemaphoreType.DMA((NEAR * depth,)),
        ],
        input_output_aliases={2 + NEAR: 0} if more else {},
        compiler_params=pltpu.CompilerParams(vmem_limit_bytes=VMEM_LIMIT),
        cost_estimate=pl.CostEstimate(
            flops=0, bytes_accessed=NEAR * got[0].size * 6, transcendentals=0
        ),
        name=f"unpack_{part}",
    )(me, table, *got, *more)


def local(spectra, library, cand_block, cand_local):
    devices = lax.axis_size("lib")
    num_query, num_bins = spectra.shape
    touches, per_touch = cand_local.shape[1], cand_local.shape[2]
    depth = rounded(depth_of(num_query, touches, devices), 2)
    blocks = num_bins // LANES
    records = rounded(devices * (rounded(depth, ROW_SLOTS) // ROW_SLOTS), 16)
    me = lax.axis_index("lib").astype(jnp.int32).reshape(1)

    def across(value, distance):
        if distance == 0:
            return value
        pairs = [(i, i ^ distance) for i in range(devices)]
        return lax.ppermute(value, "lib", pairs)

    shard, table = prepare(
        spectra, cand_block, cand_local.reshape(-1, per_touch), depth, records
    )
    far = devices // NEAR
    order = [0] + list(range(far - 1, 0, -1))
    heads = {part: across(shard, NEAR * part) for part in order}
    shards = {
        part: [across(heads[part], e) for e in range(NEAR)] for part in order
    }
    rows = library.reshape(-1, blocks, LANES)
    got = {}
    for part in order:
        answers = profile(part, depth, num_query, touches, me, shards[part], rows)
        got[part] = [across(answers[e], NEAR * part + e) for e in range(NEAR)]
    out = None
    for part in order:
        out = unpack(part, depth, num_query * touches, me, table, got[part], out)
    return out.reshape(num_query, touches * per_touch, SHIFTS)


def solution(mesh):
    placed = (
        P(("groups", "lib"), None),
        P("lib", None),
        P(("groups", "lib"), None),
        P(("groups", "lib"), None, None),
    )
    return jax.shard_map(
        local,
        mesh=mesh,
        in_specs=placed,
        out_specs=P(("groups", "lib"), None, None),
        check_vma=False,
    )
```

profile of v0, /device:TPU:0, one launch (start us, length us, event | category | flops | bytes accessed | tf_op | source)
XLA Modules:
  0.0 178.6 jit_solution(1109962411054815890)
XLA Ops:
  1.6 0.9 copy-done
  2.5 1.7 prepare.1
  4.2 2.5 %collective-permute-start.26 = (bf16[560,128]{1,0:T(8,128)(2,1)S(1)}, bf16[560,128]{1,0:T(8,128)(2,1)S(1)}, u32[]{:S(2)}, u32[]{:S(2)}) collective-permute-start(bf16[560,128]{1,0:T(8,128)(2,1)S(1)} %get-tuple-element.24.refs_0_), channel_id=1, source_target_pairs={{0,3},{1,2},{2,1},{3,0},{4,7},{5,6},{6,5},{7,4},{8,11},{9,10},{10,... | collective-permute-start | bytes 430088 | tf_op jit(solution)/shard_map/ppermute | solution.py:414
  6.7 3.6 %collective-permute-start.16 = (bf16[560,128]{1,0:T(8,128)(2,1)S(1)}, bf16[560,128]{1,0:T(8,128)(2,1)S(1)}, u32[]{:S(2)}, u32[]{:S(2)}) collective-permute-start(bf16[560,128]{1,0:T(8,128)(2,1)S(1)} %get-tuple-element.24.refs_0_), channel_id=1, source_target_pairs={{0,12},{1,13},{2,14},{3,15},{4,8},{5,9},{6,10},{7,11},{8,4},{9,5},... | collective-permute-start | bytes 430088 | tf_op jit(solution)/shard_map/ppermute | solution.py:414
  10.9 3.5 %copy.10 = bf16[64,8,32,128]{3,2,1,0:T(8,128)(2,1)S(1)} copy(bf16[64,8,32,128]{3,1,2,0:T(8,128)(2,1)} %bitcast.10) | data formatting | bytes 8388608
  15.3 0.9 collective-permute-start.19
  17.2 6.2 %collective-permute-done.8.refs_0_ = bf16[560,128]{1,0:T(8,128)(2,1)S(1)} collective-permute-done((bf16[560,128]{1,0:T(8,128)(2,1)S(1)}, bf16[560,128]{1,0:T(8,128)(2,1)S(1)}, u32[]{:S(2)}, u32[]{:S(2)}) %collective-permute-start.8) | collective-permute-done | bytes 143392 | tf_op jit(solution)/shard_map/ppermute | solution.py:414
  23.4 13.8 %profile_0.1 = (bf16[96,1024]{1,0:T(8,128)(2,1)S(1)}, bf16[96,1024]{1,0:T(8,128)(2,1)S(1)}, bf16[96,1024]{1,0:T(8,128)(2,1)S(1)}, bf16[96,1024]{1,0:T(8,128)(2,1)S(1)}) custom-call(s32[1]{0:T(128)} %bitcast.me_ref, bf16[560,128]{1,0:T(8,128)(2,1)S(1)} %get-tuple-element.24.refs_0_, bf16[560,128]{1,0:T(8,128)(2,1)S(1)} %collective-permute-done.24.refs_1_, ...), custom_call_target="tpu_custom_call" | custom-call | flops 32614907904 | bytes 8388608 | tf_op jit(solution)/shard_map/profile_0/pallas_call | solution.py:313
  37.2 1.4 collective-permute-start.10
  38.7 1.5 collective-permute-start.9
  40.1 1.2 collective-permute-start.3
  42.0 15.8 %profile_3.1 = (bf16[96,1024]{1,0:T(8,128)(2,1)S(1)}, bf16[96,1024]{1,0:T(8,128)(2,1)S(1)}, bf16[96,1024]{1,0:T(8,128)(2,1)S(1)}, bf16[96,1024]{1,0:T(8,128)(2,1)S(1)}) custom-call(s32[1]{0:T(128)} %bitcast.me_ref, bf16[560,128]{1,0:T(8,128)(2,1)S(1)} %collective-permute-done.16.refs_0_, bf16[560,128]{1,0:T(8,128)(2,1)S(1)} %collective-permute-done.17.refs_1_, ...), custom_call_target="tpu_custom_call" | custom-call | flops 32614907904 | bytes 8388608 | tf_op jit(solution)/shard_map/profile_3/pallas_call | solution.py:313
  57.9 2.4 %collective-permute-start.27 = (bf16[96,1024]{1,0:T(8,128)(2,1)S(1)}, bf16[96,1024]{1,0:T(8,128)(2,1)S(1)}, u32[]{:S(2)}, u32[]{:S(2)}) collective-permute-start(bf16[96,1024]{1,0:T(8,128)(2,1)S(1)} %get-tuple-element.38), channel_id=1, source_target_pairs={{0,1},{1,0},{2,3},{3,2},{4,5},{5,4},{6,7},{7,6},{8,9},{9,8},{10,11... | collective-permute-start | bytes 589832 | tf_op jit(solution)/shard_map/ppermute | solution.py:414
  60.3 1.4 collective-permute-start.29
  61.7 22.9 %collective-permute-start.20 = (bf16[96,1024]{1,0:T(8,128)(2,1)S(1)}, bf16[96,1024]{1,0:T(8,128)(2,1)S(1)}, u32[]{:S(2)}, u32[]{:S(2)}) collective-permute-start(bf16[96,1024]{1,0:T(8,128)(2,1)S(1)} %get-tuple-element.33), channel_id=1, source_target_pairs={{0,12},{1,13},{2,14},{3,15},{4,8},{5,9},{6,10},{7,11},{8,4},{9,5},... | collective-permute-start | bytes 589832 | tf_op jit(solution)/shard_map/ppermute | solution.py:414
  84.6 14.8 %profile_2.1 = (bf16[96,1024]{1,0:T(8,128)(2,1)S(1)}, bf16[96,1024]{1,0:T(8,128)(2,1)S(1)}, bf16[96,1024]{1,0:T(8,128)(2,1)S(1)}, bf16[96,1024]{1,0:T(8,128)(2,1)S(1)}) custom-call(s32[1]{0:T(128)} %bitcast.me_ref, bf16[560,128]{1,0:T(8,128)(2,1)S(1)} %collective-permute-done.8.refs_0_, bf16[560,128]{1,0:T(8,128)(2,1)S(1)} %collective-permute-done.9.refs_1_, ...), custom_call_target="tpu_custom_call" | custom-call | flops 32614907904 | bytes 8388608 | tf_op jit(solution)/shard_map/profile_2/pallas_call | solution.py:313
  99.4 15.6 %collective-permute-start.22 = (bf16[96,1024]{1,0:T(8,128)(2,1)S(1)}, bf16[96,1024]{1,0:T(8,128)(2,1)S(1)}, u32[]{:S(2)}, u32[]{:S(2)}) collective-permute-start(bf16[96,1024]{1,0:T(8,128)(2,1)S(1)} %get-tuple-element.35), channel_id=1, source_target_pairs={{0,14},{1,15},{2,12},{3,13},{4,10},{5,11},{6,8},{7,9},{8,6},{9,7},... | collective-permute-start | bytes 589832 | tf_op jit(solution)/shard_map/ppermute | solution.py:414
  115.1 1.1 collective-permute-start.12
  116.2 1.4 collective-permute-start.13
  117.6 1.3 collective-permute-start.14
  118.8 11.8 %profile_1.1 = (bf16[96,1024]{1,0:T(8,128)(2,1)S(1)}, bf16[96,1024]{1,0:T(8,128)(2,1)S(1)}, bf16[96,1024]{1,0:T(8,128)(2,1)S(1)}, bf16[96,1024]{1,0:T(8,128)(2,1)S(1)}) custom-call(s32[1]{0:T(128)} %bitcast.me_ref, bf16[560,128]{1,0:T(8,128)(2,1)S(1)} %collective-permute-done.refs_0_, bf16[560,128]{1,0:T(8,128)(2,1)S(1)} %collective-permute-done.1.refs_1_, ...), custom_call_target="tpu_custom_call" | custom-call | flops 32614907904 | bytes 8388608 | tf_op jit(solution)/shard_map/profile_1/pallas_call | solution.py:313
  130.7 8.6 %collective-permute-start.15 = (bf16[96,1024]{1,0:T(8,128)(2,1)S(1)}, bf16[96,1024]{1,0:T(8,128)(2,1)S(1)}, u32[]{:S(2)}, u32[]{:S(2)}) collective-permute-start(bf16[96,1024]{1,0:T(8,128)(2,1)S(1)} %get-tuple-element.32), channel_id=1, source_target_pairs={{0,11},{1,10},{2,9},{3,8},{4,15},{5,14},{6,13},{7,12},{8,3},{9,2},... | collective-permute-start | bytes 589832 | tf_op jit(solution)/shard_map/ppermute | solution.py:414
  139.2 11.5 %collective-permute-start.4 = (bf16[96,1024]{1,0:T(8,128)(2,1)S(1)}, bf16[96,1024]{1,0:T(8,128)(2,1)S(1)}, u32[]{:S(2)}, u32[]{:S(2)}) collective-permute-start(bf16[96,1024]{1,0:T(8,128)(2,1)S(1)} %get-tuple-element.25), channel_id=1, source_target_pairs={{0,4},{1,5},{2,6},{3,7},{4,0},{5,1},{6,2},{7,3},{8,12},{9,13},{10,... | collective-permute-start | bytes 589832 | tf_op jit(solution)/shard_map/ppermute | solution.py:414
  150.7 2.5 %collective-permute-start.6 = (bf16[96,1024]{1,0:T(8,128)(2,1)S(1)}, bf16[96,1024]{1,0:T(8,128)(2,1)S(1)}, u32[]{:S(2)}, u32[]{:S(2)}) collective-permute-start(bf16[96,1024]{1,0:T(8,128)(2,1)S(1)} %get-tuple-element.27), channel_id=1, source_target_pairs={{0,6},{1,7},{2,4},{3,5},{4,2},{5,3},{6,0},{7,1},{8,14},{9,15},{10,... | collective-permute-start | bytes 589832 | tf_op jit(solution)/shard_map/ppermute | solution.py:414
  153.2 2.1 %collective-permute-done.14.refs_2_ = bf16[96,1024]{1,0:T(8,128)(2,1)S(1)} collective-permute-done((bf16[96,1024]{1,0:T(8,128)(2,1)S(1)}, bf16[96,1024]{1,0:T(8,128)(2,1)S(1)}, u32[]{:S(2)}, u32[]{:S(2)}) %collective-permute-start.14) | collective-permute-done | bytes 196640 | tf_op jit(solution)/shard_map/ppermute | solution.py:414
  155.3 2.1 %collective-permute-start.7 = (bf16[96,1024]{1,0:T(8,128)(2,1)S(1)}, bf16[96,1024]{1,0:T(8,128)(2,1)S(1)}, u32[]{:S(2)}, u32[]{:S(2)}) collective-permute-start(bf16[96,1024]{1,0:T(8,128)(2,1)S(1)} %get-tuple-element.28), channel_id=1, source_target_pairs={{0,7},{1,6},{2,5},{3,4},{4,3},{5,2},{6,1},{7,0},{8,15},{9,14},{10,... | collective-permute-start | bytes 589832 | tf_op jit(solution)/shard_map/ppermute | solution.py:414
  157.4 2.6 %unpack_0.1.refs_4_ = f32[128,8,1024]{2,1,0:T(8,128)} custom-call(s32[1]{0:T(128)} %bitcast.me_ref, s32[48,128]{1,0:T(8,128)S(1)} %get-tuple-element.23.table_ref, bf16[96,1024]{1,0:T(8,128)(2,1)S(1)} %get-tuple-element.37.refs_0_, bf16[96,1024]{1,0:T(8,128)(2,1)S(1)} %collective-permute-done.27.refs_1_, ...), custom_call_target="tpu_custom_call" | custom-call | bytes 2359296 | tf_op jit(solution)/shard_map/unpack_0/pallas_call | solution.py:383
  160.0 2.6 %unpack_3.1.refs_4_ = f32[128,8,1024]{2,1,0:T(8,128)} custom-call(s32[1]{0:T(128)} %bitcast.me_ref, s32[48,128]{1,0:T(8,128)S(1)} %get-tuple-element.23.table_ref, bf16[96,1024]{1,0:T(8,128)(2,1)S(1)} %collective-permute-done.20.refs_0_, bf16[96,1024]{1,0:T(8,128)(2,1)S(1)} %collective-permute-done.21.refs_1_, ...), custom_call_target="tpu_custom_call", output_to_operand_aliasing={{}: (6, {})} | custom-call | bytes 2359296 | tf_op jit(solution)/shard_map/unpack_3/pallas_call | solution.py:383
  163.4 2.6 %unpack_2.1.refs_4_ = f32[128,8,1024]{2,1,0:T(8,128)} custom-call(s32[1]{0:T(128)} %bitcast.me_ref, s32[48,128]{1,0:T(8,128)S(1)} %get-tuple-element.23.table_ref, bf16[96,1024]{1,0:T(8,128)(2,1)S(1)} %collective-permute-done.12.refs_0_, bf16[96,1024]{1,0:T(8,128)(2,1)S(1)} %collective-permute-done.13.refs_1_, ...), custom_call_target="tpu_custom_call", output_to_operand_aliasing={{}: (6, {})} | custom-call | bytes 2359296 | tf_op jit(solution)/shard_map/unpack_2/pallas_call | solution.py:383
  166.0 5.8 %collective-permute-done.6.refs_2_ = bf16[96,1024]{1,0:T(8,128)(2,1)S(1)} collective-permute-done((bf16[96,1024]{1,0:T(8,128)(2,1)S(1)}, bf16[96,1024]{1,0:T(8,128)(2,1)S(1)}, u32[]{:S(2)}, u32[]{:S(2)}) %collective-permute-start.6) | collective-permute-done | bytes 196640 | tf_op jit(solution)/shard_map/ppermute | solution.py:414
  171.8 4.1 %collective-permute-done.7.refs_3_ = bf16[96,1024]{1,0:T(8,128)(2,1)S(1)} collective-permute-done((bf16[96,1024]{1,0:T(8,128)(2,1)S(1)}, bf16[96,1024]{1,0:T(8,128)(2,1)S(1)}, u32[]{:S(2)}, u32[]{:S(2)}) %collective-permute-start.7) | collective-permute-done | bytes 196640 | tf_op jit(solution)/shard_map/ppermute | solution.py:414
  175.9 2.7 %unpack_1.1 = f32[128,8,1024]{2,1,0:T(8,128)} custom-call(s32[1]{0:T(128)} %bitcast.me_ref, s32[48,128]{1,0:T(8,128)S(1)} %get-tuple-element.23.table_ref, bf16[96,1024]{1,0:T(8,128)(2,1)S(1)} %collective-permute-done.4.refs_0_, bf16[96,1024]{1,0:T(8,128)(2,1)S(1)} %collective-permute-done.5.refs_1_, ...), custom_call_target="tpu_custom_call", output_to_operand_aliasing={{}: (6, {})} | custom-call | bytes 2359296 | tf_op jit(solution)/shard_map/unpack_1/pallas_call | solution.py:383
  (42 shorter events, 5.7 us)
Async XLA Ops:
  1.6 0.9 copy-start
  4.2 10.2 %collective-permute-start.26 = (bf16[560,128]{1,0:T(8,128)(2,1)S(1)}, bf16[560,128]{1,0:T(8,128)(2,1)S(1)}, u32[]{:S(2)}, u32[]{:S(2)}) collective-permute-start(bf16[560,128]{1,0:T(8,128)(2,1)S(1)} %get-tuple-element.24.refs_0_), channel_id=1, source_target_pairs={{0,3},{1,2},{2,1},{3,0},{4,7},{5,6},{6,5},{7,4},{8,11},{9,10},{10,... | collective-permute-start | bytes 430088 | tf_op jit(solution)/shard_map/ppermute | solution.py:414
  6.7 8.6 %collective-permute-start.16 = (bf16[560,128]{1,0:T(8,128)(2,1)S(1)}, bf16[560,128]{1,0:T(8,128)(2,1)S(1)}, u32[]{:S(2)}, u32[]{:S(2)}) collective-permute-start(bf16[560,128]{1,0:T(8,128)(2,1)S(1)} %get-tuple-element.24.refs_0_), channel_id=1, source_target_pairs={{0,12},{1,13},{2,14},{3,15},{4,8},{5,9},{6,10},{7,11},{8,4},{9,5},... | collective-permute-start | bytes 430088 | tf_op jit(solution)/shard_map/ppermute | solution.py:414
  10.3 6.1 %collective-permute-start.25 = (bf16[560,128]{1,0:T(8,128)(2,1)S(1)}, bf16[560,128]{1,0:T(8,128)(2,1)S(1)}, u32[]{:S(2)}, u32[]{:S(2)}) collective-permute-start(bf16[560,128]{1,0:T(8,128)(2,1)S(1)} %get-tuple-element.24.refs_0_), channel_id=1, source_target_pairs={{0,2},{1,3},{2,0},{3,1},{4,6},{5,7},{6,4},{7,5},{8,10},{9,11},{10,... | collective-permute-start | bytes 430088 | tf_op jit(solution)/shard_map/ppermute | solution.py:414
  10.9 6.0 %collective-permute-start.24 = (bf16[560,128]{1,0:T(8,128)(2,1)S(1)}, bf16[560,128]{1,0:T(8,128)(2,1)S(1)}, u32[]{:S(2)}, u32[]{:S(2)}) collective-permute-start(bf16[560,128]{1,0:T(8,128)(2,1)S(1)} %get-tuple-element.24.refs_0_), channel_id=1, source_target_pairs={{0,1},{1,0},{2,3},{3,2},{4,5},{5,4},{6,7},{7,6},{8,9},{9,8},{10,11... | collective-permute-start | bytes 430088 | tf_op jit(solution)/shard_map/ppermute | solution.py:414
  10.9 12.4 %collective-permute-start.8 = (bf16[560,128]{1,0:T(8,128)(2,1)S(1)}, bf16[560,128]{1,0:T(8,128)(2,1)S(1)}, u32[]{:S(2)}, u32[]{:S(2)}) collective-permute-start(bf16[560,128]{1,0:T(8,128)(2,1)S(1)} %get-tuple-element.24.refs_0_), channel_id=1, source_target_pairs={{0,8},{1,9},{2,10},{3,11},{4,12},{5,13},{6,14},{7,15},{8,0},{9,1},... | collective-permute-start | bytes 430088 | tf_op jit(solution)/shard_map/ppermute | solution.py:414
  14.4 22.8 %collective-permute-start = (bf16[560,128]{1,0:T(8,128)(2,1)S(1)}, bf16[560,128]{1,0:T(8,128)(2,1)S(1)}, u32[]{:S(2)}, u32[]{:S(2)}) collective-permute-start(bf16[560,128]{1,0:T(8,128)(2,1)S(1)} %get-tuple-element.24.refs_0_), channel_id=1, source_target_pairs={{0,4},{1,5},{2,6},{3,7},{4,0},{5,1},{6,2},{7,3},{8,12},{9,13},{10,... | collective-permute-start | bytes 430088 | tf_op jit(solution)/shard_map/ppermute | solution.py:414
  15.3 23.4 %collective-permute-start.19 = (bf16[560,128]{1,0:T(8,128)(2,1)S(1)}, bf16[560,128]{1,0:T(8,128)(2,1)S(1)}, u32[]{:S(2)}, u32[]{:S(2)}) collective-permute-start(bf16[560,128]{1,0:T(8,128)(2,1)S(1)} %collective-permute-done.16.refs_0_), channel_id=1, source_target_pairs={{0,3},{1,2},{2,1},{3,0},{4,7},{5,6},{6,5},{7,4},{8,11},{9,10},{10,... | collective-permute-start | bytes 430088 | tf_op jit(solution)/shard_map/ppermute | solution.py:414
  16.4 23.8 %collective-permute-start.18 = (bf16[560,128]{1,0:T(8,128)(2,1)S(1)}, bf16[560,128]{1,0:T(8,128)(2,1)S(1)}, u32[]{:S(2)}, u32[]{:S(2)}) collective-permute-start(bf16[560,128]{1,0:T(8,128)(2,1)S(1)} %collective-permute-done.16.refs_0_), channel_id=1, source_target_pairs={{0,2},{1,3},{2,0},{3,1},{4,6},{5,7},{6,4},{7,5},{8,10},{9,11},{10,... | collective-permute-start | bytes 430088 | tf_op jit(solution)/shard_map/ppermute | solution.py:414
  16.9 24.4 %collective-permute-start.17 = (bf16[560,128]{1,0:T(8,128)(2,1)S(1)}, bf16[560,128]{1,0:T(8,128)(2,1)S(1)}, u32[]{:S(2)}, u32[]{:S(2)}) collective-permute-start(bf16[560,128]{1,0:T(8,128)(2,1)S(1)} %collective-permute-done.16.refs_0_), channel_id=1, source_target_pairs={{0,1},{1,0},{2,3},{3,2},{4,5},{5,4},{6,7},{7,6},{8,9},{9,8},{10,11... | collective-permute-start | bytes 430088 | tf_op jit(solution)/shard_map/ppermute | solution.py:414
  23.4 18.5 %collective-permute-start.11 = (bf16[560,128]{1,0:T(8,128)(2,1)S(1)}, bf16[560,128]{1,0:T(8,128)(2,1)S(1)}, u32[]{:S(2)}, u32[]{:S(2)}) collective-permute-start(bf16[560,128]{1,0:T(8,128)(2,1)S(1)} %collective-permute-done.8.refs_0_), channel_id=1, source_target_pairs={{0,3},{1,2},{2,1},{3,0},{4,7},{5,6},{6,5},{7,4},{8,11},{9,10},{10,... | collective-permute-start | bytes 430088 | tf_op jit(solution)/shard_map/ppermute | solution.py:414
  37.2 20.6 %collective-permute-start.10 = (bf16[560,128]{1,0:T(8,128)(2,1)S(1)}, bf16[560,128]{1,0:T(8,128)(2,1)S(1)}, u32[]{:S(2)}, u32[]{:S(2)}) collective-permute-start(bf16[560,128]{1,0:T(8,128)(2,1)S(1)} %collective-permute-done.8.refs_0_), channel_id=1, source_target_pairs={{0,2},{1,3},{2,0},{3,1},{4,6},{5,7},{6,4},{7,5},{8,10},{9,11},{10,... | collective-permute-start | bytes 430088 | tf_op jit(solution)/shard_map/ppermute | solution.py:414
  38.7 21.6 %collective-permute-start.9 = (bf16[560,128]{1,0:T(8,128)(2,1)S(1)}, bf16[560,128]{1,0:T(8,128)(2,1)S(1)}, u32[]{:S(2)}, u32[]{:S(2)}) collective-permute-start(bf16[560,128]{1,0:T(8,128)(2,1)S(1)} %collective-permute-done.8.refs_0_), channel_id=1, source_target_pairs={{0,1},{1,0},{2,3},{3,2},{4,5},{5,4},{6,7},{7,6},{8,9},{9,8},{10,11... | collective-permute-start | bytes 430088 | tf_op jit(solution)/shard_map/ppermute | solution.py:414
  40.1 20.1 %collective-permute-start.3 = (bf16[560,128]{1,0:T(8,128)(2,1)S(1)}, bf16[560,128]{1,0:T(8,128)(2,1)S(1)}, u32[]{:S(2)}, u32[]{:S(2)}) collective-permute-start(bf16[560,128]{1,0:T(8,128)(2,1)S(1)} %collective-permute-done.refs_0_), channel_id=1, source_target_pairs={{0,3},{1,2},{2,1},{3,0},{4,7},{5,6},{6,5},{7,4},{8,11},{9,10},{10,... | collective-permute-start | bytes 430088 | tf_op jit(solution)/shard_map/ppermute | solution.py:414
  41.3 20.4 %collective-permute-start.2 = (bf16[560,128]{1,0:T(8,128)(2,1)S(1)}, bf16[560,128]{1,0:T(8,128)(2,1)S(1)}, u32[]{:S(2)}, u32[]{:S(2)}) collective-permute-start(bf16[560,128]{1,0:T(8,128)(2,1)S(1)} %collective-permute-done.refs_0_), channel_id=1, source_target_pairs={{0,2},{1,3},{2,0},{3,1},{4,6},{5,7},{6,4},{7,5},{8,10},{9,11},{10,... | collective-permute-start | bytes 430088 | tf_op jit(solution)/shard_map/ppermute | solution.py:414
  41.8 42.7 %collective-permute-start.1 = (bf16[560,128]{1,0:T(8,128)(2,1)S(1)}, bf16[560,128]{1,0:T(8,128)(2,1)S(1)}, u32[]{:S(2)}, u32[]{:S(2)}) collective-permute-start(bf16[560,128]{1,0:T(8,128)(2,1)S(1)} %collective-permute-done.refs_0_), channel_id=1, source_target_pairs={{0,1},{1,0},{2,3},{3,2},{4,5},{5,4},{6,7},{7,6},{8,9},{9,8},{10,11... | collective-permute-start | bytes 430088 | tf_op jit(solution)/shard_map/ppermute | solution.py:414
  57.9 41.6 %collective-permute-start.27 = (bf16[96,1024]{1,0:T(8,128)(2,1)S(1)}, bf16[96,1024]{1,0:T(8,128)(2,1)S(1)}, u32[]{:S(2)}, u32[]{:S(2)}) collective-permute-start(bf16[96,1024]{1,0:T(8,128)(2,1)S(1)} %get-tuple-element.38), channel_id=1, source_target_pairs={{0,1},{1,0},{2,3},{3,2},{4,5},{5,4},{6,7},{7,6},{8,9},{9,8},{10,11... | collective-permute-start | bytes 589832 | tf_op jit(solution)/shard_map/ppermute | solution.py:414
  60.3 54.8 %collective-permute-start.28 = (bf16[96,1024]{1,0:T(8,128)(2,1)S(1)}, bf16[96,1024]{1,0:T(8,128)(2,1)S(1)}, u32[]{:S(2)}, u32[]{:S(2)}) collective-permute-start(bf16[96,1024]{1,0:T(8,128)(2,1)S(1)} %get-tuple-element.39), channel_id=1, source_target_pairs={{0,2},{1,3},{2,0},{3,1},{4,6},{5,7},{6,4},{7,5},{8,10},{9,11},{10,... | collective-permute-start | bytes 589832 | tf_op jit(solution)/shard_map/ppermute | solution.py:414
  60.3 54.8 %collective-permute-start.29 = (bf16[96,1024]{1,0:T(8,128)(2,1)S(1)}, bf16[96,1024]{1,0:T(8,128)(2,1)S(1)}, u32[]{:S(2)}, u32[]{:S(2)}) collective-permute-start(bf16[96,1024]{1,0:T(8,128)(2,1)S(1)} %get-tuple-element.40), channel_id=1, source_target_pairs={{0,3},{1,2},{2,1},{3,0},{4,7},{5,6},{6,5},{7,4},{8,11},{9,10},{10,... | collective-permute-start | bytes 589832 | tf_op jit(solution)/shard_map/ppermute | solution.py:414
  61.7 54.5 %collective-permute-start.20 = (bf16[96,1024]{1,0:T(8,128)(2,1)S(1)}, bf16[96,1024]{1,0:T(8,128)(2,1)S(1)}, u32[]{:S(2)}, u32[]{:S(2)}) collective-permute-start(bf16[96,1024]{1,0:T(8,128)(2,1)S(1)} %get-tuple-element.33), channel_id=1, source_target_pairs={{0,12},{1,13},{2,14},{3,15},{4,8},{5,9},{6,10},{7,11},{8,4},{9,5},... | collective-permute-start | bytes 589832 | tf_op jit(solution)/shard_map/ppermute | solution.py:414
  84.6 33.0 %collective-permute-start.21 = (bf16[96,1024]{1,0:T(8,128)(2,1)S(1)}, bf16[96,1024]{1,0:T(8,128)(2,1)S(1)}, u32[]{:S(2)}, u32[]{:S(2)}) collective-permute-start(bf16[96,1024]{1,0:T(8,128)(2,1)S(1)} %get-tuple-element.34), channel_id=1, source_target_pairs={{0,13},{1,12},{2,15},{3,14},{4,9},{5,8},{6,11},{7,10},{8,5},{9,4},... | collective-permute-start | bytes 589832 | tf_op jit(solution)/shard_map/ppermute | solution.py:414
  99.4 31.2 %collective-permute-start.22 = (bf16[96,1024]{1,0:T(8,128)(2,1)S(1)}, bf16[96,1024]{1,0:T(8,128)(2,1)S(1)}, u32[]{:S(2)}, u32[]{:S(2)}) collective-permute-start(bf16[96,1024]{1,0:T(8,128)(2,1)S(1)} %get-tuple-element.35), channel_id=1, source_target_pairs={{0,14},{1,15},{2,12},{3,13},{4,10},{5,11},{6,8},{7,9},{8,6},{9,7},... | collective-permute-start | bytes 589832 | tf_op jit(solution)/shard_map/ppermute | solution.py:414
  115.1 24.1 %collective-permute-start.23 = (bf16[96,1024]{1,0:T(8,128)(2,1)S(1)}, bf16[96,1024]{1,0:T(8,128)(2,1)S(1)}, u32[]{:S(2)}, u32[]{:S(2)}) collective-permute-start(bf16[96,1024]{1,0:T(8,128)(2,1)S(1)} %get-tuple-element.36), channel_id=1, source_target_pairs={{0,15},{1,14},{2,13},{3,12},{4,11},{5,10},{6,9},{7,8},{8,7},{9,6},... | collective-permute-start | bytes 589832 | tf_op jit(solution)/shard_map/ppermute | solution.py:414
  115.1 35.6 %collective-permute-start.12 = (bf16[96,1024]{1,0:T(8,128)(2,1)S(1)}, bf16[96,1024]{1,0:T(8,128)(2,1)S(1)}, u32[]{:S(2)}, u32[]{:S(2)}) collective-permute-start(bf16[96,1024]{1,0:T(8,128)(2,1)S(1)} %get-tuple-element.29), channel_id=1, source_target_pairs={{0,8},{1,9},{2,10},{3,11},{4,12},{5,13},{6,14},{7,15},{8,0},{9,1},... | collective-permute-start | bytes 589832 | tf_op jit(solution)/shard_map/ppermute | solution.py:414
  116.2 34.6 %collective-permute-start.13 = (bf16[96,1024]{1,0:T(8,128)(2,1)S(1)}, bf16[96,1024]{1,0:T(8,128)(2,1)S(1)}, u32[]{:S(2)}, u32[]{:S(2)}) collective-permute-start(bf16[96,1024]{1,0:T(8,128)(2,1)S(1)} %get-tuple-element.30), channel_id=1, source_target_pairs={{0,9},{1,8},{2,11},{3,10},{4,13},{5,12},{6,15},{7,14},{8,1},{9,0},... | collective-permute-start | bytes 589832 | tf_op jit(solution)/shard_map/ppermute | solution.py:414
  117.6 37.8 %collective-permute-start.14 = (bf16[96,1024]{1,0:T(8,128)(2,1)S(1)}, bf16[96,1024]{1,0:T(8,128)(2,1)S(1)}, u32[]{:S(2)}, u32[]{:S(2)}) collective-permute-start(bf16[96,1024]{1,0:T(8,128)(2,1)S(1)} %get-tuple-element.31), channel_id=1, source_target_pairs={{0,10},{1,11},{2,8},{3,9},{4,14},{5,15},{6,12},{7,13},{8,2},{9,3},... | collective-permute-start | bytes 589832 | tf_op jit(solution)/shard_map/ppermute | solution.py:414
  130.7 32.7 %collective-permute-start.15 = (bf16[96,1024]{1,0:T(8,128)(2,1)S(1)}, bf16[96,1024]{1,0:T(8,128)(2,1)S(1)}, u32[]{:S(2)}, u32[]{:S(2)}) collective-permute-start(bf16[96,1024]{1,0:T(8,128)(2,1)S(1)} %get-tuple-element.32), channel_id=1, source_target_pairs={{0,11},{1,10},{2,9},{3,8},{4,15},{5,14},{6,13},{7,12},{8,3},{9,2},... | collective-permute-start | bytes 589832 | tf_op jit(solution)/shard_map/ppermute | solution.py:414
  139.2 26.8 %collective-permute-start.4 = (bf16[96,1024]{1,0:T(8,128)(2,1)S(1)}, bf16[96,1024]{1,0:T(8,128)(2,1)S(1)}, u32[]{:S(2)}, u32[]{:S(2)}) collective-permute-start(bf16[96,1024]{1,0:T(8,128)(2,1)S(1)} %get-tuple-element.25), channel_id=1, source_target_pairs={{0,4},{1,5},{2,6},{3,7},{4,0},{5,1},{6,2},{7,3},{8,12},{9,13},{10,... | collective-permute-start | bytes 589832 | tf_op jit(solution)/shard_map/ppermute | solution.py:414
  150.7 15.3 %collective-permute-start.5 = (bf16[96,1024]{1,0:T(8,128)(2,1)S(1)}, bf16[96,1024]{1,0:T(8,128)(2,1)S(1)}, u32[]{:S(2)}, u32[]{:S(2)}) collective-permute-start(bf16[96,1024]{1,0:T(8,128)(2,1)S(1)} %get-tuple-element.26), channel_id=1, source_target_pairs={{0,5},{1,4},{2,7},{3,6},{4,1},{5,0},{6,3},{7,2},{8,13},{9,12},{10,... | collective-permute-start | bytes 589832 | tf_op jit(solution)/shard_map/ppermute | solution.py:414
  150.7 21.1 %collective-permute-start.6 = (bf16[96,1024]{1,0:T(8,128)(2,1)S(1)}, bf16[96,1024]{1,0:T(8,128)(2,1)S(1)}, u32[]{:S(2)}, u32[]{:S(2)}) collective-permute-start(bf16[96,1024]{1,0:T(8,128)(2,1)S(1)} %get-tuple-element.27), channel_id=1, source_target_pairs={{0,6},{1,7},{2,4},{3,5},{4,2},{5,3},{6,0},{7,1},{8,14},{9,15},{10,... | collective-permute-start | bytes 589832 | tf_op jit(solution)/shard_map/ppermute | solution.py:414
  155.3 20.6 %collective-permute-start.7 = (bf16[96,1024]{1,0:T(8,128)(2,1)S(1)}, bf16[96,1024]{1,0:T(8,128)(2,1)S(1)}, u32[]{:S(2)}, u32[]{:S(2)}) collective-permute-start(bf16[96,1024]{1,0:T(8,128)(2,1)S(1)} %get-tuple-element.28), channel_id=1, source_target_pairs={{0,7},{1,6},{2,5},{3,4},{4,3},{5,2},{6,1},{7,0},{8,15},{9,14},{10,... | collective-permute-start | bytes 589832 | tf_op jit(solution)/shard_map/ppermute | solution.py:414
where the time goes:
time: 180 us; the launch traced here: 179 us
  starting transfers between devices  84.7 us (47%)
  Pallas kernels  68.4 us (38%)
  waiting for transfers between devices  19.3 us (11%)
  local copies, waits for them, and re-layouts  5.95 us (3%)
    ppermute x30, starting transfers between devices, across(): return lax.ppermute(value, 'lib', pairs)  84.7 us
    pallas_call x4, Pallas kernels, profile(): pl.pallas_call(functools.partial(profile_kernel, depth, num_query, touche...  56.3 us
    ppermute x30, waiting for transfers between devices, across(): return lax.ppermute(value, 'lib', pairs)  19.3 us
    pallas_call x4, Pallas kernels, unpack(): pl.pallas_call(functools.partial(unpack_kernel, part, depth), out_shape=j...  10.4 us
    unnamed x5, local copies, waits for them, and re-layouts  5.95 us
  transfers between devices with their start and end apart: 30, of which 6 were waited for; matrix products, arithmetic and copies ran while one was open for 2% of the time, Pallas kernels for 36%

commit v1 on v0

--- a/solution.py
+++ b/solution.py
@@ -202,34 +202,47 @@
                     [turned[(g - a) % GROUPS] for g in range(GROUPS)]
                 )
 
-    def make_right(slot, half):
+    def shifter(slot, half):
         query = jnp.maximum(touch_of(slot), 0) // touches
         spectrum_ref[half] = query_ref[
             entry(slot)[0], pl.ds(pl.multiple_of(query * blocks, blocks), blocks), :
         ].astype(jnp.float32)
         zero = jnp.zeros((8, LANES), jnp.float32)
-        before = (zero, zero)
-        before_shifted = jnp.zeros((16, LANES), jnp.bfloat16)
-        columns = slice(half * LANES, (half + 1) * LANES)
-        for b in range(blocks + 1):
-            if b < blocks:
+        turned = {-1: (zero, zero), blocks: (zero, zero)}
+        shifted = {-1: jnp.zeros((16, LANES), jnp.bfloat16)}
+
+        def turned_of(b):
+            if b not in turned:
                 wide = jnp.broadcast_to(spectrum_ref[half, pl.ds(b, 1), :], (8, LANES))
-                now = tuple(
+                turned[b] = tuple(
                     pltpu.roll(wide, 1 + 8 * h, 1, stride=1, stride_axis=0) for h in range(2)
                 )
-            else:
-                now = (zero, zero)
-            shifted = jnp.concatenate(
-                [jnp.where(lane > row + 8 * h, now[h], before[h]) for h in range(2)], axis=0
-            ).astype(jnp.bfloat16)
-            j = blocks - 1 - b
-            place = 0 if j < 0 else (j % tiles + 1) * LANES + j // tiles * WIDTH
-            right_ref[pl.ds(place, 16), columns] = shifted
-            for c in range(16, WIDTH, 16):
-                right_ref[pl.ds(place + c, 16), columns] = pltpu.roll(
-                    jnp.where(lane16 < LANES - c, shifted, before_shifted), c, 1
-                )
-            before, before_shifted = now, shifted
+            return turned[b]
+
+        def shifted_of(b):
+            if b not in shifted:
+                now, before = turned_of(b), turned_of(b - 1)
+                shifted[b] = jnp.concatenate(
+                    [jnp.where(lane > row + 8 * h, now[h], before[h]) for h in range(2)], axis=0
+                ).astype(jnp.bfloat16)
+            return shifted[b]
+
+        return shifted_of
+
+    def make_right(slots):
+        shifters = [shifter(slot, half) for half, slot in enumerate(slots)]
+        for t in range(tiles + 1):
+            for half in range(2):
+                columns = slice(half * LANES, (half + 1) * LANES)
+                for g in range(GROUPS if t else 1):
+                    b = blocks - t - tiles * g
+                    place = t * LANES + g * WIDTH
+                    now, before = shifters[half](b), shifters[half](b - 1)
+                    right_ref[pl.ds(place, 16), columns] = now
+                    for c in range(16, WIDTH, 16):
+                        right_ref[pl.ds(place + c, 16), columns] = pltpu.roll(
+                            jnp.where(lane16 < LANES - c, now, before), c, 1
+                        )
 
     def sums(low, high):
         left = jnp.concatenate(
@@ -256,8 +269,7 @@
         def _():
             scales = [gather(2 * pair + half, half) for half in range(2)]
             make_left()
-            for half in range(2):
-                make_right(2 * pair + half, half)
+            make_right([2 * pair, 2 * pair + 1])
             step = GROUPS // CHAINS
             for c in range(CHAINS):
                 product_ref[c * height : (c + 1) * height, :] = sums(step * c, step * (c + 1))

time: 180 us -> 180 us (level)
  the two profiles are of different devices: /device:TPU:0 before, /device:TPU:3 now
where the time goes in v1:
time: 180 us; the launch traced here: 178 us
  starting transfers between devices  77.6 us (43%)
  Pallas kernels  77.2 us (43%)
  waiting for transfers between devices  16.9 us (9%)
  local copies, waits for them, and re-layouts  5.95 us (3%)
    ppermute x30, starting transfers between devices, across(): return lax.ppermute(value, 'lib', pairs)  77.6 us
    pallas_call x4, Pallas kernels, profile(): pl.pallas_call(functools.partial(profile_kernel, depth, num_query, touche...  64.9 us
    ppermute x30, waiting for transfers between devices, across(): return lax.ppermute(value, 'lib', pairs)  16.9 us
    pallas_call x4, Pallas kernels, unpack(): pl.pallas_call(functools.partial(unpack_kernel, part, depth), out_shape=j...  10.6 us
    unnamed x5, local copies, waits for them, and re-layouts  5.95 us
  transfers between devices with their start and end apart: 30, of which 5 were waited for; matrix products, arithmetic and copies ran while one was open for 2% of the time, Pallas kernels for 41%

profile of v1, /device:TPU:3, one launch (start us, length us, event | category | flops | bytes accessed | tf_op | source)
XLA Modules:
  0.0 177.8 jit_solution(11705068056382547339)
XLA Ops:
  1.6 0.9 copy-done
  2.5 1.7 prepare.1
  4.2 1.9 %collective-permute-start.26 = (bf16[560,128]{1,0:T(8,128)(2,1)S(1)}, bf16[560,128]{1,0:T(8,128)(2,1)S(1)}, u32[]{:S(2)}, u32[]{:S(2)}) collective-permute-start(bf16[560,128]{1,0:T(8,128)(2,1)S(1)} %get-tuple-element.24.refs_0_), channel_id=1, source_target_pairs={{0,3},{1,2},{2,1},{3,0},{4,7},{5,6},{6,5},{7,4},{8,11},{9,10},{10,... | collective-permute-start | bytes 430088 | tf_op jit(solution)/shard_map/ppermute | solution.py:426
  6.1 3.3 %collective-permute-start.16 = (bf16[560,128]{1,0:T(8,128)(2,1)S(1)}, bf16[560,128]{1,0:T(8,128)(2,1)S(1)}, u32[]{:S(2)}, u32[]{:S(2)}) collective-permute-start(bf16[560,128]{1,0:T(8,128)(2,1)S(1)} %get-tuple-element.24.refs_0_), channel_id=1, source_target_pairs={{0,12},{1,13},{2,14},{3,15},{4,8},{5,9},{6,10},{7,11},{8,4},{9,5},... | collective-permute-start | bytes 430088 | tf_op jit(solution)/shard_map/ppermute | solution.py:426
  10.2 3.5 %copy.10 = bf16[64,8,32,128]{3,2,1,0:T(8,128)(2,1)S(1)} copy(bf16[64,8,32,128]{3,1,2,0:T(8,128)(2,1)} %bitcast.10) | data formatting | bytes 8388608
  13.9 1.7 collective-permute-start.19
  16.1 5.7 %collective-permute-done.8.refs_0_ = bf16[560,128]{1,0:T(8,128)(2,1)S(1)} collective-permute-done((bf16[560,128]{1,0:T(8,128)(2,1)S(1)}, bf16[560,128]{1,0:T(8,128)(2,1)S(1)}, u32[]{:S(2)}, u32[]{:S(2)}) %collective-permute-start.8) | collective-permute-done | bytes 143392 | tf_op jit(solution)/shard_map/ppermute | solution.py:426
  21.8 0.9 collective-permute-start.11
  22.7 16.0 %profile_0.1 = (bf16[96,1024]{1,0:T(8,128)(2,1)S(1)}, bf16[96,1024]{1,0:T(8,128)(2,1)S(1)}, bf16[96,1024]{1,0:T(8,128)(2,1)S(1)}, bf16[96,1024]{1,0:T(8,128)(2,1)S(1)}) custom-call(s32[1]{0:T(128)} %bitcast.me_ref, bf16[560,128]{1,0:T(8,128)(2,1)S(1)} %get-tuple-element.24.refs_0_, bf16[560,128]{1,0:T(8,128)(2,1)S(1)} %collective-permute-done.24.refs_1_, ...), custom_call_target="tpu_custom_call" | custom-call | flops 32614907904 | bytes 8388608 | tf_op jit(solution)/shard_map/profile_0/pallas_call | solution.py:325
  38.8 4.0 %collective-permute-start.9 = (bf16[560,128]{1,0:T(8,128)(2,1)S(1)}, bf16[560,128]{1,0:T(8,128)(2,1)S(1)}, u32[]{:S(2)}, u32[]{:S(2)}) collective-permute-start(bf16[560,128]{1,0:T(8,128)(2,1)S(1)} %collective-permute-done.8.refs_0_), channel_id=1, source_target_pairs={{0,1},{1,0},{2,3},{3,2},{4,5},{5,4},{6,7},{7,6},{8,9},{9,8},{10,11... | collective-permute-start | bytes 430088 | tf_op jit(solution)/shard_map/ppermute | solution.py:426
  42.8 1.6 collective-permute-start.3
  45.0 17.0 %profile_3.1 = (bf16[96,1024]{1,0:T(8,128)(2,1)S(1)}, bf16[96,1024]{1,0:T(8,128)(2,1)S(1)}, bf16[96,1024]{1,0:T(8,128)(2,1)S(1)}, bf16[96,1024]{1,0:T(8,128)(2,1)S(1)}) custom-call(s32[1]{0:T(128)} %bitcast.me_ref, bf16[560,128]{1,0:T(8,128)(2,1)S(1)} %collective-permute-done.16.refs_0_, bf16[560,128]{1,0:T(8,128)(2,1)S(1)} %collective-permute-done.17.refs_1_, ...), custom_call_target="tpu_custom_call" | custom-call | flops 32614907904 | bytes 8388608 | tf_op jit(solution)/shard_map/profile_3/pallas_call | solution.py:325
  61.9 6.2 %collective-permute-start.27 = (bf16[96,1024]{1,0:T(8,128)(2,1)S(1)}, bf16[96,1024]{1,0:T(8,128)(2,1)S(1)}, u32[]{:S(2)}, u32[]{:S(2)}) collective-permute-start(bf16[96,1024]{1,0:T(8,128)(2,1)S(1)} %get-tuple-element.38), channel_id=1, source_target_pairs={{0,1},{1,0},{2,3},{3,2},{4,5},{5,4},{6,7},{7,6},{8,9},{9,8},{10,11... | collective-permute-start | bytes 589832 | tf_op jit(solution)/shard_map/ppermute | solution.py:426
  68.1 1.7 collective-permute-start.29
  69.9 15.9 %collective-permute-start.20 = (bf16[96,1024]{1,0:T(8,128)(2,1)S(1)}, bf16[96,1024]{1,0:T(8,128)(2,1)S(1)}, u32[]{:S(2)}, u32[]{:S(2)}) collective-permute-start(bf16[96,1024]{1,0:T(8,128)(2,1)S(1)} %get-tuple-element.33), channel_id=1, source_target_pairs={{0,12},{1,13},{2,14},{3,15},{4,8},{5,9},{6,10},{7,11},{8,4},{9,5},... | collective-permute-start | bytes 589832 | tf_op jit(solution)/shard_map/ppermute | solution.py:426
  85.8 16.0 %profile_2.1 = (bf16[96,1024]{1,0:T(8,128)(2,1)S(1)}, bf16[96,1024]{1,0:T(8,128)(2,1)S(1)}, bf16[96,1024]{1,0:T(8,128)(2,1)S(1)}, bf16[96,1024]{1,0:T(8,128)(2,1)S(1)}) custom-call(s32[1]{0:T(128)} %bitcast.me_ref, bf16[560,128]{1,0:T(8,128)(2,1)S(1)} %collective-permute-done.8.refs_0_, bf16[560,128]{1,0:T(8,128)(2,1)S(1)} %collective-permute-done.9.refs_1_, ...), custom_call_target="tpu_custom_call" | custom-call | flops 32614907904 | bytes 8388608 | tf_op jit(solution)/shard_map/profile_2/pallas_call | solution.py:325
  101.8 6.4 %collective-permute-start.22 = (bf16[96,1024]{1,0:T(8,128)(2,1)S(1)}, bf16[96,1024]{1,0:T(8,128)(2,1)S(1)}, u32[]{:S(2)}, u32[]{:S(2)}) collective-permute-start(bf16[96,1024]{1,0:T(8,128)(2,1)S(1)} %get-tuple-element.35), channel_id=1, source_target_pairs={{0,14},{1,15},{2,12},{3,13},{4,10},{5,11},{6,8},{7,9},{8,6},{9,7},... | collective-permute-start | bytes 589832 | tf_op jit(solution)/shard_map/ppermute | solution.py:426
  108.2 6.9 %collective-permute-start.23 = (bf16[96,1024]{1,0:T(8,128)(2,1)S(1)}, bf16[96,1024]{1,0:T(8,128)(2,1)S(1)}, u32[]{:S(2)}, u32[]{:S(2)}) collective-permute-start(bf16[96,1024]{1,0:T(8,128)(2,1)S(1)} %get-tuple-element.36), channel_id=1, source_target_pairs={{0,15},{1,14},{2,13},{3,12},{4,11},{5,10},{6,9},{7,8},{8,7},{9,6},... | collective-permute-start | bytes 589832 | tf_op jit(solution)/shard_map/ppermute | solution.py:426
  115.1 2.9 %collective-permute-start.13 = (bf16[96,1024]{1,0:T(8,128)(2,1)S(1)}, bf16[96,1024]{1,0:T(8,128)(2,1)S(1)}, u32[]{:S(2)}, u32[]{:S(2)}) collective-permute-start(bf16[96,1024]{1,0:T(8,128)(2,1)S(1)} %get-tuple-element.30), channel_id=1, source_target_pairs={{0,9},{1,8},{2,11},{3,10},{4,13},{5,12},{6,15},{7,14},{8,1},{9,0},... | collective-permute-start | bytes 589832 | tf_op jit(solution)/shard_map/ppermute | solution.py:426
  118.0 2.9 %collective-permute-start.14 = (bf16[96,1024]{1,0:T(8,128)(2,1)S(1)}, bf16[96,1024]{1,0:T(8,128)(2,1)S(1)}, u32[]{:S(2)}, u32[]{:S(2)}) collective-permute-start(bf16[96,1024]{1,0:T(8,128)(2,1)S(1)} %get-tuple-element.31), channel_id=1, source_target_pairs={{0,10},{1,11},{2,8},{3,9},{4,14},{5,15},{6,12},{7,13},{8,2},{9,3},... | collective-permute-start | bytes 589832 | tf_op jit(solution)/shard_map/ppermute | solution.py:426
  120.9 16.0 %profile_1.1 = (bf16[96,1024]{1,0:T(8,128)(2,1)S(1)}, bf16[96,1024]{1,0:T(8,128)(2,1)S(1)}, bf16[96,1024]{1,0:T(8,128)(2,1)S(1)}, bf16[96,1024]{1,0:T(8,128)(2,1)S(1)}) custom-call(s32[1]{0:T(128)} %bitcast.me_ref, bf16[560,128]{1,0:T(8,128)(2,1)S(1)} %collective-permute-done.refs_0_, bf16[560,128]{1,0:T(8,128)(2,1)S(1)} %collective-permute-done.1.refs_1_, ...), custom_call_target="tpu_custom_call" | custom-call | flops 32614907904 | bytes 8388608 | tf_op jit(solution)/shard_map/profile_1/pallas_call | solution.py:325
  136.9 12.5 %collective-permute-start.15 = (bf16[96,1024]{1,0:T(8,128)(2,1)S(1)}, bf16[96,1024]{1,0:T(8,128)(2,1)S(1)}, u32[]{:S(2)}, u32[]{:S(2)}) collective-permute-start(bf16[96,1024]{1,0:T(8,128)(2,1)S(1)} %get-tuple-element.32), channel_id=1, source_target_pairs={{0,11},{1,10},{2,9},{3,8},{4,15},{5,14},{6,13},{7,12},{8,3},{9,2},... | collective-permute-start | bytes 589832 | tf_op jit(solution)/shard_map/ppermute | solution.py:426
  149.4 3.5 %collective-permute-start.4 = (bf16[96,1024]{1,0:T(8,128)(2,1)S(1)}, bf16[96,1024]{1,0:T(8,128)(2,1)S(1)}, u32[]{:S(2)}, u32[]{:S(2)}) collective-permute-start(bf16[96,1024]{1,0:T(8,128)(2,1)S(1)} %get-tuple-element.25), channel_id=1, source_target_pairs={{0,4},{1,5},{2,6},{3,7},{4,0},{5,1},{6,2},{7,3},{8,12},{9,13},{10,... | collective-permute-start | bytes 589832 | tf_op jit(solution)/shard_map/ppermute | solution.py:426
  153.0 2.7 %collective-permute-start.6 = (bf16[96,1024]{1,0:T(8,128)(2,1)S(1)}, bf16[96,1024]{1,0:T(8,128)(2,1)S(1)}, u32[]{:S(2)}, u32[]{:S(2)}) collective-permute-start(bf16[96,1024]{1,0:T(8,128)(2,1)S(1)} %get-tuple-element.27), channel_id=1, source_target_pairs={{0,6},{1,7},{2,4},{3,5},{4,2},{5,3},{6,0},{7,1},{8,14},{9,15},{10,... | collective-permute-start | bytes 589832 | tf_op jit(solution)/shard_map/ppermute | solution.py:426
  156.0 2.6 %unpack_0.1.refs_4_ = f32[128,8,1024]{2,1,0:T(8,128)} custom-call(s32[1]{0:T(128)} %bitcast.me_ref, s32[48,128]{1,0:T(8,128)S(1)} %get-tuple-element.23.table_ref, bf16[96,1024]{1,0:T(8,128)(2,1)S(1)} %get-tuple-element.37.refs_0_, bf16[96,1024]{1,0:T(8,128)(2,1)S(1)} %collective-permute-done.27.refs_1_, ...), custom_call_target="tpu_custom_call" | custom-call | bytes 2359296 | tf_op jit(solution)/shard_map/unpack_0/pallas_call | solution.py:395
  158.6 2.7 %unpack_3.1.refs_4_ = f32[128,8,1024]{2,1,0:T(8,128)} custom-call(s32[1]{0:T(128)} %bitcast.me_ref, s32[48,128]{1,0:T(8,128)S(1)} %get-tuple-element.23.table_ref, bf16[96,1024]{1,0:T(8,128)(2,1)S(1)} %collective-permute-done.20.refs_0_, bf16[96,1024]{1,0:T(8,128)(2,1)S(1)} %collective-permute-done.21.refs_1_, ...), custom_call_target="tpu_custom_call", output_to_operand_aliasing={{}: (6, {})} | custom-call | bytes 2359296 | tf_op jit(solution)/shard_map/unpack_3/pallas_call | solution.py:395
  161.3 1.1 collective-permute-done.15.refs_3_
  162.4 2.7 %unpack_2.1.refs_4_ = f32[128,8,1024]{2,1,0:T(8,128)} custom-call(s32[1]{0:T(128)} %bitcast.me_ref, s32[48,128]{1,0:T(8,128)S(1)} %get-tuple-element.23.table_ref, bf16[96,1024]{1,0:T(8,128)(2,1)S(1)} %collective-permute-done.12.refs_0_, bf16[96,1024]{1,0:T(8,128)(2,1)S(1)} %collective-permute-done.13.refs_1_, ...), custom_call_target="tpu_custom_call", output_to_operand_aliasing={{}: (6, {})} | custom-call | bytes 2359296 | tf_op jit(solution)/shard_map/unpack_2/pallas_call | solution.py:395
  165.1 1.8 %collective-permute-done.5.refs_1_ = bf16[96,1024]{1,0:T(8,128)(2,1)S(1)} collective-permute-done((bf16[96,1024]{1,0:T(8,128)(2,1)S(1)}, bf16[96,1024]{1,0:T(8,128)(2,1)S(1)}, u32[]{:S(2)}, u32[]{:S(2)}) %collective-permute-start.5) | collective-permute-done | bytes 196640 | tf_op jit(solution)/shard_map/ppermute | solution.py:426
  166.9 3.0 %collective-permute-done.6.refs_2_ = bf16[96,1024]{1,0:T(8,128)(2,1)S(1)} collective-permute-done((bf16[96,1024]{1,0:T(8,128)(2,1)S(1)}, bf16[96,1024]{1,0:T(8,128)(2,1)S(1)}, u32[]{:S(2)}, u32[]{:S(2)}) %collective-permute-start.6) | collective-permute-done | bytes 196640 | tf_op jit(solution)/shard_map/ppermute | solution.py:426
  169.9 5.2 %collective-permute-done.7.refs_3_ = bf16[96,1024]{1,0:T(8,128)(2,1)S(1)} collective-permute-done((bf16[96,1024]{1,0:T(8,128)(2,1)S(1)}, bf16[96,1024]{1,0:T(8,128)(2,1)S(1)}, u32[]{:S(2)}, u32[]{:S(2)}) %collective-permute-start.7) | collective-permute-done | bytes 196640 | tf_op jit(solution)/shard_map/ppermute | solution.py:426
  175.1 2.7 %unpack_1.1 = f32[128,8,1024]{2,1,0:T(8,128)} custom-call(s32[1]{0:T(128)} %bitcast.me_ref, s32[48,128]{1,0:T(8,128)S(1)} %get-tuple-element.23.table_ref, bf16[96,1024]{1,0:T(8,128)(2,1)S(1)} %collective-permute-done.4.refs_0_, bf16[96,1024]{1,0:T(8,128)(2,1)S(1)} %collective-permute-done.5.refs_1_, ...), custom_call_target="tpu_custom_call", output_to_operand_aliasing={{}: (6, {})} | custom-call | bytes 2359296 | tf_op jit(solution)/shard_map/unpack_1/pallas_call | solution.py:395
  (42 shorter events, 4.1 us)
Async XLA Ops:
  1.6 0.9 copy-start
  4.2 9.4 %collective-permute-start.26 = (bf16[560,128]{1,0:T(8,128)(2,1)S(1)}, bf16[560,128]{1,0:T(8,128)(2,1)S(1)}, u32[]{:S(2)}, u32[]{:S(2)}) collective-permute-start(bf16[560,128]{1,0:T(8,128)(2,1)S(1)} %get-tuple-element.24.refs_0_), channel_id=1, source_target_pairs={{0,3},{1,2},{2,1},{3,0},{4,7},{5,6},{6,5},{7,4},{8,11},{9,10},{10,... | collective-permute-start | bytes 430088 | tf_op jit(solution)/shard_map/ppermute | solution.py:426
  6.1 7.8 %collective-permute-start.16 = (bf16[560,128]{1,0:T(8,128)(2,1)S(1)}, bf16[560,128]{1,0:T(8,128)(2,1)S(1)}, u32[]{:S(2)}, u32[]{:S(2)}) collective-permute-start(bf16[560,128]{1,0:T(8,128)(2,1)S(1)} %get-tuple-element.24.refs_0_), channel_id=1, source_target_pairs={{0,12},{1,13},{2,14},{3,15},{4,8},{5,9},{6,10},{7,11},{8,4},{9,5},... | collective-permute-start | bytes 430088 | tf_op jit(solution)/shard_map/ppermute | solution.py:426
  9.4 6.2 %collective-permute-start.25 = (bf16[560,128]{1,0:T(8,128)(2,1)S(1)}, bf16[560,128]{1,0:T(8,128)(2,1)S(1)}, u32[]{:S(2)}, u32[]{:S(2)}) collective-permute-start(bf16[560,128]{1,0:T(8,128)(2,1)S(1)} %get-tuple-element.24.refs_0_), channel_id=1, source_target_pairs={{0,2},{1,3},{2,0},{3,1},{4,6},{5,7},{6,4},{7,5},{8,10},{9,11},{10,... | collective-permute-start | bytes 430088 | tf_op jit(solution)/shard_map/ppermute | solution.py:426
  9.6 6.3 %collective-permute-start.24 = (bf16[560,128]{1,0:T(8,128)(2,1)S(1)}, bf16[560,128]{1,0:T(8,128)(2,1)S(1)}, u32[]{:S(2)}, u32[]{:S(2)}) collective-permute-start(bf16[560,128]{1,0:T(8,128)(2,1)S(1)} %get-tuple-element.24.refs_0_), channel_id=1, source_target_pairs={{0,1},{1,0},{2,3},{3,2},{4,5},{5,4},{6,7},{7,6},{8,9},{9,8},{10,11... | collective-permute-start | bytes 430088 | tf_op jit(solution)/shard_map/ppermute | solution.py:426
  10.2 11.7 %collective-permute-start.8 = (bf16[560,128]{1,0:T(8,128)(2,1)S(1)}, bf16[560,128]{1,0:T(8,128)(2,1)S(1)}, u32[]{:S(2)}, u32[]{:S(2)}) collective-permute-start(bf16[560,128]{1,0:T(8,128)(2,1)S(1)} %get-tuple-element.24.refs_0_), channel_id=1, source_target_pairs={{0,8},{1,9},{2,10},{3,11},{4,12},{5,13},{6,14},{7,15},{8,0},{9,1},... | collective-permute-start | bytes 430088 | tf_op jit(solution)/shard_map/ppermute | solution.py:426
  13.6 25.0 %collective-permute-start = (bf16[560,128]{1,0:T(8,128)(2,1)S(1)}, bf16[560,128]{1,0:T(8,128)(2,1)S(1)}, u32[]{:S(2)}, u32[]{:S(2)}) collective-permute-start(bf16[560,128]{1,0:T(8,128)(2,1)S(1)} %get-tuple-element.24.refs_0_), channel_id=1, source_target_pairs={{0,4},{1,5},{2,6},{3,7},{4,0},{5,1},{6,2},{7,3},{8,12},{9,13},{10,... | collective-permute-start | bytes 430088 | tf_op jit(solution)/shard_map/ppermute | solution.py:426
  13.9 24.8 %collective-permute-start.19 = (bf16[560,128]{1,0:T(8,128)(2,1)S(1)}, bf16[560,128]{1,0:T(8,128)(2,1)S(1)}, u32[]{:S(2)}, u32[]{:S(2)}) collective-permute-start(bf16[560,128]{1,0:T(8,128)(2,1)S(1)} %collective-permute-done.16.refs_0_), channel_id=1, source_target_pairs={{0,3},{1,2},{2,1},{3,0},{4,7},{5,6},{6,5},{7,4},{8,11},{9,10},{10,... | collective-permute-start | bytes 430088 | tf_op jit(solution)/shard_map/ppermute | solution.py:426
  15.6 27.1 %collective-permute-start.18 = (bf16[560,128]{1,0:T(8,128)(2,1)S(1)}, bf16[560,128]{1,0:T(8,128)(2,1)S(1)}, u32[]{:S(2)}, u32[]{:S(2)}) collective-permute-start(bf16[560,128]{1,0:T(8,128)(2,1)S(1)} %collective-permute-done.16.refs_0_), channel_id=1, source_target_pairs={{0,2},{1,3},{2,0},{3,1},{4,6},{5,7},{6,4},{7,5},{8,10},{9,11},{10,... | collective-permute-start | bytes 430088 | tf_op jit(solution)/shard_map/ppermute | solution.py:426
  15.9 28.5 %collective-permute-start.17 = (bf16[560,128]{1,0:T(8,128)(2,1)S(1)}, bf16[560,128]{1,0:T(8,128)(2,1)S(1)}, u32[]{:S(2)}, u32[]{:S(2)}) collective-permute-start(bf16[560,128]{1,0:T(8,128)(2,1)S(1)} %collective-permute-done.16.refs_0_), channel_id=1, source_target_pairs={{0,1},{1,0},{2,3},{3,2},{4,5},{5,4},{6,7},{7,6},{8,9},{9,8},{10,11... | collective-permute-start | bytes 430088 | tf_op jit(solution)/shard_map/ppermute | solution.py:426
  21.8 22.7 %collective-permute-start.11 = (bf16[560,128]{1,0:T(8,128)(2,1)S(1)}, bf16[560,128]{1,0:T(8,128)(2,1)S(1)}, u32[]{:S(2)}, u32[]{:S(2)}) collective-permute-start(bf16[560,128]{1,0:T(8,128)(2,1)S(1)} %collective-permute-done.8.refs_0_), channel_id=1, source_target_pairs={{0,3},{1,2},{2,1},{3,0},{4,7},{5,6},{6,5},{7,4},{8,11},{9,10},{10,... | collective-permute-start | bytes 430088 | tf_op jit(solution)/shard_map/ppermute | solution.py:426
  38.7 23.3 %collective-permute-start.10 = (bf16[560,128]{1,0:T(8,128)(2,1)S(1)}, bf16[560,128]{1,0:T(8,128)(2,1)S(1)}, u32[]{:S(2)}, u32[]{:S(2)}) collective-permute-start(bf16[560,128]{1,0:T(8,128)(2,1)S(1)} %collective-permute-done.8.refs_0_), channel_id=1, source_target_pairs={{0,2},{1,3},{2,0},{3,1},{4,6},{5,7},{6,4},{7,5},{8,10},{9,11},{10,... | collective-permute-start | bytes 430088 | tf_op jit(solution)/shard_map/ppermute | solution.py:426
  38.8 29.4 %collective-permute-start.9 = (bf16[560,128]{1,0:T(8,128)(2,1)S(1)}, bf16[560,128]{1,0:T(8,128)(2,1)S(1)}, u32[]{:S(2)}, u32[]{:S(2)}) collective-permute-start(bf16[560,128]{1,0:T(8,128)(2,1)S(1)} %collective-permute-done.8.refs_0_), channel_id=1, source_target_pairs={{0,1},{1,0},{2,3},{3,2},{4,5},{5,4},{6,7},{7,6},{8,9},{9,8},{10,11... | collective-permute-start | bytes 430088 | tf_op jit(solution)/shard_map/ppermute | solution.py:426
  42.8 25.4 %collective-permute-start.3 = (bf16[560,128]{1,0:T(8,128)(2,1)S(1)}, bf16[560,128]{1,0:T(8,128)(2,1)S(1)}, u32[]{:S(2)}, u32[]{:S(2)}) collective-permute-start(bf16[560,128]{1,0:T(8,128)(2,1)S(1)} %collective-permute-done.refs_0_), channel_id=1, source_target_pairs={{0,3},{1,2},{2,1},{3,0},{4,7},{5,6},{6,5},{7,4},{8,11},{9,10},{10,... | collective-permute-start | bytes 430088 | tf_op jit(solution)/shard_map/ppermute | solution.py:426
  44.4 25.5 %collective-permute-start.2 = (bf16[560,128]{1,0:T(8,128)(2,1)S(1)}, bf16[560,128]{1,0:T(8,128)(2,1)S(1)}, u32[]{:S(2)}, u32[]{:S(2)}) collective-permute-start(bf16[560,128]{1,0:T(8,128)(2,1)S(1)} %collective-permute-done.refs_0_), channel_id=1, source_target_pairs={{0,2},{1,3},{2,0},{3,1},{4,6},{5,7},{6,4},{7,5},{8,10},{9,11},{10,... | collective-permute-start | bytes 430088 | tf_op jit(solution)/shard_map/ppermute | solution.py:426
  44.5 41.3 %collective-permute-start.1 = (bf16[560,128]{1,0:T(8,128)(2,1)S(1)}, bf16[560,128]{1,0:T(8,128)(2,1)S(1)}, u32[]{:S(2)}, u32[]{:S(2)}) collective-permute-start(bf16[560,128]{1,0:T(8,128)(2,1)S(1)} %collective-permute-done.refs_0_), channel_id=1, source_target_pairs={{0,1},{1,0},{2,3},{3,2},{4,5},{5,4},{6,7},{7,6},{8,9},{9,8},{10,11... | collective-permute-start | bytes 430088 | tf_op jit(solution)/shard_map/ppermute | solution.py:426
  61.9 39.9 %collective-permute-start.27 = (bf16[96,1024]{1,0:T(8,128)(2,1)S(1)}, bf16[96,1024]{1,0:T(8,128)(2,1)S(1)}, u32[]{:S(2)}, u32[]{:S(2)}) collective-permute-start(bf16[96,1024]{1,0:T(8,128)(2,1)S(1)} %get-tuple-element.38), channel_id=1, source_target_pairs={{0,1},{1,0},{2,3},{3,2},{4,5},{5,4},{6,7},{7,6},{8,9},{9,8},{10,11... | collective-permute-start | bytes 589832 | tf_op jit(solution)/shard_map/ppermute | solution.py:426
  68.1 40.1 %collective-permute-start.28 = (bf16[96,1024]{1,0:T(8,128)(2,1)S(1)}, bf16[96,1024]{1,0:T(8,128)(2,1)S(1)}, u32[]{:S(2)}, u32[]{:S(2)}) collective-permute-start(bf16[96,1024]{1,0:T(8,128)(2,1)S(1)} %get-tuple-element.39), channel_id=1, source_target_pairs={{0,2},{1,3},{2,0},{3,1},{4,6},{5,7},{6,4},{7,5},{8,10},{9,11},{10,... | collective-permute-start | bytes 589832 | tf_op jit(solution)/shard_map/ppermute | solution.py:426
  68.1 46.9 %collective-permute-start.29 = (bf16[96,1024]{1,0:T(8,128)(2,1)S(1)}, bf16[96,1024]{1,0:T(8,128)(2,1)S(1)}, u32[]{:S(2)}, u32[]{:S(2)}) collective-permute-start(bf16[96,1024]{1,0:T(8,128)(2,1)S(1)} %get-tuple-element.40), channel_id=1, source_target_pairs={{0,3},{1,2},{2,1},{3,0},{4,7},{5,6},{6,5},{7,4},{8,11},{9,10},{10,... | collective-permute-start | bytes 589832 | tf_op jit(solution)/shard_map/ppermute | solution.py:426
  69.9 45.2 %collective-permute-start.20 = (bf16[96,1024]{1,0:T(8,128)(2,1)S(1)}, bf16[96,1024]{1,0:T(8,128)(2,1)S(1)}, u32[]{:S(2)}, u32[]{:S(2)}) collective-permute-start(bf16[96,1024]{1,0:T(8,128)(2,1)S(1)} %get-tuple-element.33), channel_id=1, source_target_pairs={{0,12},{1,13},{2,14},{3,15},{4,8},{5,9},{6,10},{7,11},{8,4},{9,5},... | collective-permute-start | bytes 589832 | tf_op jit(solution)/shard_map/ppermute | solution.py:426
  85.8 32.2 %collective-permute-start.21 = (bf16[96,1024]{1,0:T(8,128)(2,1)S(1)}, bf16[96,1024]{1,0:T(8,128)(2,1)S(1)}, u32[]{:S(2)}, u32[]{:S(2)}) collective-permute-start(bf16[96,1024]{1,0:T(8,128)(2,1)S(1)} %get-tuple-element.34), channel_id=1, source_target_pairs={{0,13},{1,12},{2,15},{3,14},{4,9},{5,8},{6,11},{7,10},{8,5},{9,4},... | collective-permute-start | bytes 589832 | tf_op jit(solution)/shard_map/ppermute | solution.py:426
  101.8 35.1 %collective-permute-start.22 = (bf16[96,1024]{1,0:T(8,128)(2,1)S(1)}, bf16[96,1024]{1,0:T(8,128)(2,1)S(1)}, u32[]{:S(2)}, u32[]{:S(2)}) collective-permute-start(bf16[96,1024]{1,0:T(8,128)(2,1)S(1)} %get-tuple-element.35), channel_id=1, source_target_pairs={{0,14},{1,15},{2,12},{3,13},{4,10},{5,11},{6,8},{7,9},{8,6},{9,7},... | collective-permute-start | bytes 589832 | tf_op jit(solution)/shard_map/ppermute | solution.py:426
  108.2 41.2 %collective-permute-start.23 = (bf16[96,1024]{1,0:T(8,128)(2,1)S(1)}, bf16[96,1024]{1,0:T(8,128)(2,1)S(1)}, u32[]{:S(2)}, u32[]{:S(2)}) collective-permute-start(bf16[96,1024]{1,0:T(8,128)(2,1)S(1)} %get-tuple-element.36), channel_id=1, source_target_pairs={{0,15},{1,14},{2,13},{3,12},{4,11},{5,10},{6,9},{7,8},{8,7},{9,6},... | collective-permute-start | bytes 589832 | tf_op jit(solution)/shard_map/ppermute | solution.py:426
  115.1 37.9 %collective-permute-start.12 = (bf16[96,1024]{1,0:T(8,128)(2,1)S(1)}, bf16[96,1024]{1,0:T(8,128)(2,1)S(1)}, u32[]{:S(2)}, u32[]{:S(2)}) collective-permute-start(bf16[96,1024]{1,0:T(8,128)(2,1)S(1)} %get-tuple-element.29), channel_id=1, source_target_pairs={{0,8},{1,9},{2,10},{3,11},{4,12},{5,13},{6,14},{7,15},{8,0},{9,1},... | collective-permute-start | bytes 589832 | tf_op jit(solution)/shard_map/ppermute | solution.py:426
  115.1 37.9 %collective-permute-start.13 = (bf16[96,1024]{1,0:T(8,128)(2,1)S(1)}, bf16[96,1024]{1,0:T(8,128)(2,1)S(1)}, u32[]{:S(2)}, u32[]{:S(2)}) collective-permute-start(bf16[96,1024]{1,0:T(8,128)(2,1)S(1)} %get-tuple-element.30), channel_id=1, source_target_pairs={{0,9},{1,8},{2,11},{3,10},{4,13},{5,12},{6,15},{7,14},{8,1},{9,0},... | collective-permute-start | bytes 589832 | tf_op jit(solution)/shard_map/ppermute | solution.py:426
  118.0 37.7 %collective-permute-start.14 = (bf16[96,1024]{1,0:T(8,128)(2,1)S(1)}, bf16[96,1024]{1,0:T(8,128)(2,1)S(1)}, u32[]{:S(2)}, u32[]{:S(2)}) collective-permute-start(bf16[96,1024]{1,0:T(8,128)(2,1)S(1)} %get-tuple-element.31), channel_id=1, source_target_pairs={{0,10},{1,11},{2,8},{3,9},{4,14},{5,15},{6,12},{7,13},{8,2},{9,3},... | collective-permute-start | bytes 589832 | tf_op jit(solution)/shard_map/ppermute | solution.py:426
  136.9 25.5 %collective-permute-start.15 = (bf16[96,1024]{1,0:T(8,128)(2,1)S(1)}, bf16[96,1024]{1,0:T(8,128)(2,1)S(1)}, u32[]{:S(2)}, u32[]{:S(2)}) collective-permute-start(bf16[96,1024]{1,0:T(8,128)(2,1)S(1)} %get-tuple-element.32), channel_id=1, source_target_pairs={{0,11},{1,10},{2,9},{3,8},{4,15},{5,14},{6,13},{7,12},{8,3},{9,2},... | collective-permute-start | bytes 589832 | tf_op jit(solution)/shard_map/ppermute | solution.py:426
  149.4 15.6 %collective-permute-start.4 = (bf16[96,1024]{1,0:T(8,128)(2,1)S(1)}, bf16[96,1024]{1,0:T(8,128)(2,1)S(1)}, u32[]{:S(2)}, u32[]{:S(2)}) collective-permute-start(bf16[96,1024]{1,0:T(8,128)(2,1)S(1)} %get-tuple-element.25), channel_id=1, source_target_pairs={{0,4},{1,5},{2,6},{3,7},{4,0},{5,1},{6,2},{7,3},{8,12},{9,13},{10,... | collective-permute-start | bytes 589832 | tf_op jit(solution)/shard_map/ppermute | solution.py:426
  153.0 13.9 %collective-permute-start.5 = (bf16[96,1024]{1,0:T(8,128)(2,1)S(1)}, bf16[96,1024]{1,0:T(8,128)(2,1)S(1)}, u32[]{:S(2)}, u32[]{:S(2)}) collective-permute-start(bf16[96,1024]{1,0:T(8,128)(2,1)S(1)} %get-tuple-element.26), channel_id=1, source_target_pairs={{0,5},{1,4},{2,7},{3,6},{4,1},{5,0},{6,3},{7,2},{8,13},{9,12},{10,... | collective-permute-start | bytes 589832 | tf_op jit(solution)/shard_map/ppermute | solution.py:426
  153.0 16.9 %collective-permute-start.6 = (bf16[96,1024]{1,0:T(8,128)(2,1)S(1)}, bf16[96,1024]{1,0:T(8,128)(2,1)S(1)}, u32[]{:S(2)}, u32[]{:S(2)}) collective-permute-start(bf16[96,1024]{1,0:T(8,128)(2,1)S(1)} %get-tuple-element.27), channel_id=1, source_target_pairs={{0,6},{1,7},{2,4},{3,5},{4,2},{5,3},{6,0},{7,1},{8,14},{9,15},{10,... | collective-permute-start | bytes 589832 | tf_op jit(solution)/shard_map/ppermute | solution.py:426
  155.7 19.4 %collective-permute-start.7 = (bf16[96,1024]{1,0:T(8,128)(2,1)S(1)}, bf16[96,1024]{1,0:T(8,128)(2,1)S(1)}, u32[]{:S(2)}, u32[]{:S(2)}) collective-permute-start(bf16[96,1024]{1,0:T(8,128)(2,1)S(1)} %get-tuple-element.28), channel_id=1, source_target_pairs={{0,7},{1,6},{2,5},{3,4},{4,3},{5,2},{6,1},{7,0},{8,15},{9,14},{10,... | collective-permute-start | bytes 589832 | tf_op jit(solution)/shard_map/ppermute | solution.py:426

commit v2 on v0

--- a/solution.py
+++ b/solution.py
@@ -124,12 +124,13 @@
     shards, library_ref, refs = refs[:NEAR], refs[NEAR], refs[NEAR + 1 :]
     outs, refs = refs[:NEAR], refs[NEAR:]
     (
-        query_ref, record_ref, found_ref, table_ref, answer_ref,
-        cand_ref, packed_ref, spectrum_ref, left_ref, right_ref, product_ref, sem_ref,
+        query_ref, record_ref, line_ref, found_ref, table_ref, answer_ref,
+        pick_ref, cand_ref, scale_ref, spectrum_ref, left_ref, right_ref, product_ref, sem_ref,
     ) = refs
     per_touch = PER_TOUCH
     rows = 2 * per_touch
-    blocks = library_ref.shape[1]
+    lines, num_bins = library_ref.shape
+    blocks = num_bins // LANES
     offsets = SHIFTS // LANES
     first = offsets // 2 + 1
     tiles = blocks // GROUPS
@@ -144,18 +145,47 @@
     ]
     for copy in copies:
         copy.start()
-    cand_ref[...] = jnp.zeros(cand_ref.shape, cand_ref.dtype)
+    line_ref[...] = jnp.zeros(line_ref.shape, line_ref.dtype)
+    scale_ref[...] = jnp.zeros(scale_ref.shape, scale_ref.dtype)
     right_ref[...] = jnp.zeros(right_ref.shape, right_ref.dtype)
-    found_ref[...] = jnp.zeros(found_ref.shape, found_ref.dtype)
     for e in range(NEAR):
         copies[e].wait()
         record_ref[...] = query_ref[e, query_rows:, :].astype(jnp.float32)
-        found_ref[e * per_block : (e + 1) * per_block, :] = record_values(
-            record_ref[pl.ds(me_ref[0] * per_block, per_block), :]
-        )
+        line_ref[e * per_block : (e + 1) * per_block, :] = record_ref[
+            pl.ds(me_ref[0] * per_block, per_block), :
+        ]
+    found_ref[...] = record_values(line_ref[...])
     to_scalars = pltpu.make_async_copy(found_ref, table_ref, sem_ref.at[NEAR])
     to_scalars.start()
     to_scalars.wait()
+
+    picked = pick_ref.shape[0]
+    at = lax.broadcasted_iota(jnp.int32, (picked, line_ref.shape[0]), 0)
+    line = lax.broadcasted_iota(jnp.int32, (picked, line_ref.shape[0]), 1)
+    own = jnp.where(at // (PER_TOUCH * ROW_SLOTS) == line, 1.0, 0.0).astype(jnp.bfloat16)
+    spread = jnp.dot(own, line_ref[...].astype(jnp.bfloat16), preferred_element_type=jnp.float32)
+    at = lax.broadcasted_iota(jnp.int32, (picked, LANES), 0)
+    high = at // PER_TOUCH % ROW_SLOTS * SLOT_LANES + at % PER_TOUCH
+    wide_lane = lax.broadcasted_iota(jnp.int32, (picked, LANES), 1)
+    weight = jnp.where(
+        wide_lane == high, 16.0, jnp.where(wide_lane == high + PER_TOUCH, 1.0, 0.0)
+    )
+    wanted = jnp.sum(spread * weight, axis=1, keepdims=True).astype(jnp.int32)
+    which = lax.broadcasted_iota(jnp.int32, (picked, lines), 1)
+    pick_ref[...] = jnp.where(which == wanted, 1.0, 0.0).astype(jnp.bfloat16)
+
+    @pl.loop(0, num_bins // (2 * LANES))
+    def _(n):
+        columns = pl.ds(pl.multiple_of(n * 2 * LANES, 2 * LANES), 2 * LANES)
+        piece = jnp.dot(
+            pick_ref[...], library_ref[:, columns], preferred_element_type=jnp.float32
+        )
+        cand_ref[:, columns] = piece.astype(jnp.bfloat16)
+        low, top = piece[:, :LANES], piece[:, LANES:]
+        scale_ref[...] += low * low + top * top
+
+    mean = jnp.sum(scale_ref[...], axis=1, keepdims=True) / num_bins
+    scale_ref[...] = jnp.broadcast_to(lax.rsqrt(mean + EPSILON), scale_ref.shape)
 
     def entry(slot):
         e = slot // depth
@@ -172,27 +202,16 @@
             value = jnp.where(lane16 < group * WIDTH, value, pieces[group])
         return value
 
-    def gather(slot, half):
-        _, line, start = entry(slot)
-        for k in range(per_touch):
-            wanted = table_ref[line, start + k]
-            cand_ref[pl.ds(first * rows + half * per_touch + k, blocks, stride=rows), :] = (
-                library_ref[wanted].astype(jnp.float32)
-            )
-        square = jnp.zeros((per_touch, LANES), jnp.float32)
-        for b in range(blocks):
-            piece = cand_ref[pl.ds((first + b) * rows + half * per_touch, per_touch), :]
-            square = square + piece * piece
-        mean = jnp.sum(square, axis=1, keepdims=True) / (blocks * LANES)
-        return lax.rsqrt(mean + EPSILON)
-
-    def make_left():
-        for b in range(blocks + offsets + 1):
-            packed_ref[pl.ds(rows * b, rows), :] = cand_ref[pl.ds(rows * b, rows), :].astype(
-                jnp.bfloat16
-            )
+    def make_left(pair):
+        def block_of(b):
+            if not 0 <= b < blocks:
+                return jnp.zeros((rows, LANES), jnp.bfloat16)
+            return cand_ref[
+                pl.ds(pl.multiple_of(rows * pair, rows), rows), b * LANES : (b + 1) * LANES
+            ]
+
         for t in range(tiles + offsets + 1):
-            given = [packed_ref[pl.ds(rows * (t + tiles * g), rows), :] for g in range(GROUPS)]
+            given = [block_of(t + tiles * g - first) for g in range(GROUPS)]
             turned = []
             for c in range(GROUPS):
                 mixed = choose([given[(a + c) % GROUPS] for a in range(GROUPS)])
@@ -254,8 +273,7 @@
     def _(pair):
         @pl.when((touch_of(2 * pair) >= 0) | (touch_of(2 * pair + 1) >= 0))
         def _():
-            scales = [gather(2 * pair + half, half) for half in range(2)]
-            make_left()
+            make_left(pair)
             for half in range(2):
                 make_right(2 * pair + half, half)
             step = GROUPS // CHAINS
@@ -279,7 +297,8 @@
                             shift,
                             1,
                         )
-                    both.append(total * scales[half])
+                    scale_row = pl.multiple_of(rows * pair + per_touch * half, per_touch)
+                    both.append(total * scale_ref[pl.ds(scale_row, per_touch), :])
                 answer_ref[
                     pl.ds(pl.multiple_of(16 * pair, 16), 16), o * LANES : (o + 1) * LANES
                 ] = jnp.concatenate(both, axis=0).astype(jnp.bfloat16)
@@ -299,7 +318,7 @@
 
 
 def profile(part, depth, num_query, touches, me, shards, library):
-    blocks = library.shape[1]
+    blocks = library.shape[1] // LANES
     offsets = SHIFTS // LANES
     tiles = blocks // GROUPS
     records = shards[0].shape[0] - num_query * blocks
@@ -321,11 +340,13 @@
         scratch_shapes=[
             pltpu.VMEM((NEAR, *shards[0].shape), jnp.bfloat16),
             pltpu.VMEM((records, LANES), jnp.float32),
+            pltpu.VMEM(table, jnp.float32),
             pltpu.VMEM(table, jnp.int32),
             pltpu.SMEM(table, jnp.int32),
             pltpu.VMEM((answers, SHIFTS), jnp.bfloat16),
-            pltpu.VMEM(((blocks + offsets + 1) * 16, LANES), jnp.float32),
-            pltpu.VMEM(((blocks + offsets + 1) * 16, LANES), jnp.bfloat16),
+            pltpu.VMEM((answers, library.shape[0]), jnp.bfloat16),
+            pltpu.VMEM((answers, library.shape[1]), jnp.bfloat16),
+            pltpu.VMEM((answers, LANES), jnp.float32),
             pltpu.VMEM((2, blocks, LANES), jnp.float32),
             pltpu.VMEM((GROUPS, (tiles + offsets + 1) * 16, LANES), jnp.bfloat16),
             pltpu.VMEM(((tiles + 1) * LANES, 2 * LANES), jnp.bfloat16),
@@ -402,8 +423,7 @@
     devices = lax.axis_size("lib")
     num_query, num_bins = spectra.shape
     touches, per_touch = cand_local.shape[1], cand_local.shape[2]
-    depth = rounded(depth_of(num_query, touches, devices), 2)
-    blocks = num_bins // LANES
+    depth = rounded(depth_of(num_query, touches, devices), ROW_SLOTS)
     records = rounded(devices * (rounded(depth, ROW_SLOTS) // ROW_SLOTS), 16)
     me = lax.axis_index("lib").astype(jnp.int32).reshape(1)
 
@@ -422,10 +442,9 @@
     shards = {
         part: [across(heads[part], e) for e in range(NEAR)] for part in order
     }
-    rows = library.reshape(-1, blocks, LANES)
     got = {}
     for part in order:
-        answers = profile(part, depth, num_query, touches, me, shards[part], rows)
+        answers = profile(part, depth, num_query, touches, me, shards[part], library)
         got[part] = [across(answers[e], NEAR * part + e) for e in range(NEAR)]
     out = None
     for part in order:

time: 180 us -> 193 us (1.072)
  Pallas kernels: 68.4 us -> 131 us
  starting transfers between devices: 84.7 us -> 36.7 us
    pallas_call x4, Pallas kernels: 56.3 us -> 119 us  [profile(): pl.pallas_call(functools.partial(profile_kernel, depth, num_query, touche...]
    ppermute x30, starting transfers between devices: 84.7 us -> 36.7 us  [across(): return lax.ppermute(value, 'lib', pairs)]
    unnamed x5 -> x8, local copies, waits for them, and re-layouts: 5.95 us -> 4.7 us
  transfers between devices with their start and end apart: 30 -> 30, of which waited for: 6 -> 7; matrix products, arithmetic and copies ran while one was open for 2% -> 0% of each run, Pallas kernels for 36% -> 66%
where the time goes in v2:
time: 193 us
  Pallas kernels  131 us (68%)
  starting transfers between devices  36.7 us (19%)
  waiting for transfers between devices  20.5 us (11%)
  local copies, waits for them, and re-layouts  4.7 us (2%)
    pallas_call x4, Pallas kernels, profile(): pl.pallas_call(functools.partial(profile_kernel, depth, num_query, touche...  119 us
    ppermute x30, starting transfers between devices, across(): return lax.ppermute(value, 'lib', pairs)  36.7 us
    ppermute x30, waiting for transfers between devices, across(): return lax.ppermute(value, 'lib', pairs)  20.5 us
    pallas_call x4, Pallas kernels, unpack(): pl.pallas_call(functools.partial(unpack_kernel, part, depth), out_shape=j...  10.3 us
    unnamed x8, local copies, waits for them, and re-layouts  4.7 us
  transfers between devices with their start and end apart: 30, of which 7 were waited for; matrix products, arithmetic and copies ran while one was open for 0% of the time, Pallas kernels for 66%

profile of v2, /device:TPU:0, one launch (start us, length us, event | category | flops | bytes accessed | tf_op | source)
XLA Modules:
  0.0 193.4 jit_solution(6717838072770423368)
XLA Ops:
  0.0 0.8 copy.8
  1.6 0.9 copy-done
  2.5 1.7 prepare.1
  4.7 4.7 %collective-permute-start.16 = (bf16[560,128]{1,0:T(8,128)(2,1)S(1)}, bf16[560,128]{1,0:T(8,128)(2,1)S(1)}, u32[]{:S(2)}, u32[]{:S(2)}) collective-permute-start(bf16[560,128]{1,0:T(8,128)(2,1)S(1)} %get-tuple-element.24.refs_0_), channel_id=1, source_target_pairs={{0,12},{1,13},{2,14},{3,15},{4,8},{5,9},{6,10},{7,11},{8,4},{9,5},... | collective-permute-start | bytes 430088 | tf_op jit(solution)/shard_map/ppermute | solution.py:434
  9.4 1.6 collective-permute-start.25
  11.8 2.1 %collective-permute-done.16.refs_0_ = bf16[560,128]{1,0:T(8,128)(2,1)S(1)} collective-permute-done((bf16[560,128]{1,0:T(8,128)(2,1)S(1)}, bf16[560,128]{1,0:T(8,128)(2,1)S(1)}, u32[]{:S(2)}, u32[]{:S(2)}) %collective-permute-start.16) | collective-permute-done | bytes 143392 | tf_op jit(solution)/shard_map/ppermute | solution.py:434
  13.9 2.1 %collective-permute-done.25.refs_2_ = bf16[560,128]{1,0:T(8,128)(2,1)S(1)} collective-permute-done((bf16[560,128]{1,0:T(8,128)(2,1)S(1)}, bf16[560,128]{1,0:T(8,128)(2,1)S(1)}, u32[]{:S(2)}, u32[]{:S(2)}) %collective-permute-start.25) | collective-permute-done | bytes 143392 | tf_op jit(solution)/shard_map/ppermute | solution.py:434
  16.0 1.6 collective-permute-start.18
  18.2 1.9 collective-permute-start.19
  20.1 2.1 %collective-permute-done.8.refs_0_ = bf16[560,128]{1,0:T(8,128)(2,1)S(1)} collective-permute-done((bf16[560,128]{1,0:T(8,128)(2,1)S(1)}, bf16[560,128]{1,0:T(8,128)(2,1)S(1)}, u32[]{:S(2)}, u32[]{:S(2)}) %collective-permute-start.8) | collective-permute-done | bytes 143392 | tf_op jit(solution)/shard_map/ppermute | solution.py:434
  22.1 1.5 collective-permute-start.10
  23.7 2.2 %copy-done.1 = bf16[512,4096]{1,0:T(8,128)(2,1)S(1)} copy-done((bf16[512,4096]{1,0:T(8,128)(2,1)S(1)}, bf16[512,4096]{1,0:T(8,128)(2,1)}, u32[]{:S(2)}) %copy-start.1) | copy-done | bytes 4194328
  25.9 30.8 %profile_0.1 = (bf16[96,1024]{1,0:T(8,128)(2,1)S(1)}, bf16[96,1024]{1,0:T(8,128)(2,1)S(1)}, bf16[96,1024]{1,0:T(8,128)(2,1)S(1)}, bf16[96,1024]{1,0:T(8,128)(2,1)S(1)}) custom-call(s32[1]{0:T(128)} %bitcast.me_ref, bf16[560,128]{1,0:T(8,128)(2,1)S(1)} %get-tuple-element.24.refs_0_, bf16[560,128]{1,0:T(8,128)(2,1)S(1)} %collective-permute-done.24.refs_1_, ...), custom_call_target="tpu_custom_call" | custom-call | flops 32614907904 | bytes 8388608 | tf_op jit(solution)/shard_map/profile_0/pallas_call | solution.py:332
  57.4 1.5 collective-permute-start.2
  59.2 28.9 %profile_3.1 = (bf16[96,1024]{1,0:T(8,128)(2,1)S(1)}, bf16[96,1024]{1,0:T(8,128)(2,1)S(1)}, bf16[96,1024]{1,0:T(8,128)(2,1)S(1)}, bf16[96,1024]{1,0:T(8,128)(2,1)S(1)}) custom-call(s32[1]{0:T(128)} %bitcast.me_ref, bf16[560,128]{1,0:T(8,128)(2,1)S(1)} %collective-permute-done.16.refs_0_, bf16[560,128]{1,0:T(8,128)(2,1)S(1)} %collective-permute-done.17.refs_1_, ...), custom_call_target="tpu_custom_call" | custom-call | flops 32614907904 | bytes 8388608 | tf_op jit(solution)/shard_map/profile_3/pallas_call | solution.py:332
  88.2 2.5 %collective-permute-start.28 = (bf16[96,1024]{1,0:T(8,128)(2,1)S(1)}, bf16[96,1024]{1,0:T(8,128)(2,1)S(1)}, u32[]{:S(2)}, u32[]{:S(2)}) collective-permute-start(bf16[96,1024]{1,0:T(8,128)(2,1)S(1)} %get-tuple-element.39), channel_id=1, source_target_pairs={{0,2},{1,3},{2,0},{3,1},{4,6},{5,7},{6,4},{7,5},{8,10},{9,11},{10,... | collective-permute-start | bytes 589832 | tf_op jit(solution)/shard_map/ppermute | solution.py:434
  90.9 3.4 %collective-permute-start.20 = (bf16[96,1024]{1,0:T(8,128)(2,1)S(1)}, bf16[96,1024]{1,0:T(8,128)(2,1)S(1)}, u32[]{:S(2)}, u32[]{:S(2)}) collective-permute-start(bf16[96,1024]{1,0:T(8,128)(2,1)S(1)} %get-tuple-element.33), channel_id=1, source_target_pairs={{0,12},{1,13},{2,14},{3,15},{4,8},{5,9},{6,10},{7,11},{8,4},{9,5},... | collective-permute-start | bytes 589832 | tf_op jit(solution)/shard_map/ppermute | solution.py:434
  94.3 30.8 %profile_2.1 = (bf16[96,1024]{1,0:T(8,128)(2,1)S(1)}, bf16[96,1024]{1,0:T(8,128)(2,1)S(1)}, bf16[96,1024]{1,0:T(8,128)(2,1)S(1)}, bf16[96,1024]{1,0:T(8,128)(2,1)S(1)}) custom-call(s32[1]{0:T(128)} %bitcast.me_ref, bf16[560,128]{1,0:T(8,128)(2,1)S(1)} %collective-permute-done.8.refs_0_, bf16[560,128]{1,0:T(8,128)(2,1)S(1)} %collective-permute-done.9.refs_1_, ...), custom_call_target="tpu_custom_call" | custom-call | flops 32614907904 | bytes 8388608 | tf_op jit(solution)/shard_map/profile_2/pallas_call | solution.py:332
  125.2 0.8 collective-permute-start.23
  126.0 6.3 %collective-permute-start.13 = (bf16[96,1024]{1,0:T(8,128)(2,1)S(1)}, bf16[96,1024]{1,0:T(8,128)(2,1)S(1)}, u32[]{:S(2)}, u32[]{:S(2)}) collective-permute-start(bf16[96,1024]{1,0:T(8,128)(2,1)S(1)} %get-tuple-element.30), channel_id=1, source_target_pairs={{0,9},{1,8},{2,11},{3,10},{4,13},{5,12},{6,15},{7,14},{8,1},{9,0},... | collective-permute-start | bytes 589832 | tf_op jit(solution)/shard_map/ppermute | solution.py:434
  132.3 1.5 collective-permute-start.14
  133.8 28.9 %profile_1.1 = (bf16[96,1024]{1,0:T(8,128)(2,1)S(1)}, bf16[96,1024]{1,0:T(8,128)(2,1)S(1)}, bf16[96,1024]{1,0:T(8,128)(2,1)S(1)}, bf16[96,1024]{1,0:T(8,128)(2,1)S(1)}) custom-call(s32[1]{0:T(128)} %bitcast.me_ref, bf16[560,128]{1,0:T(8,128)(2,1)S(1)} %collective-permute-done.refs_0_, bf16[560,128]{1,0:T(8,128)(2,1)S(1)} %collective-permute-done.1.refs_1_, ...), custom_call_target="tpu_custom_call" | custom-call | flops 32614907904 | bytes 8388608 | tf_op jit(solution)/shard_map/profile_1/pallas_call | solution.py:332
  162.8 1.0 collective-permute-start.4
  163.7 3.7 %collective-permute-start.5 = (bf16[96,1024]{1,0:T(8,128)(2,1)S(1)}, bf16[96,1024]{1,0:T(8,128)(2,1)S(1)}, u32[]{:S(2)}, u32[]{:S(2)}) collective-permute-start(bf16[96,1024]{1,0:T(8,128)(2,1)S(1)} %get-tuple-element.26), channel_id=1, source_target_pairs={{0,5},{1,4},{2,7},{3,6},{4,1},{5,0},{6,3},{7,2},{8,13},{9,12},{10,... | collective-permute-start | bytes 589832 | tf_op jit(solution)/shard_map/ppermute | solution.py:434
  167.5 2.1 %collective-permute-start.6 = (bf16[96,1024]{1,0:T(8,128)(2,1)S(1)}, bf16[96,1024]{1,0:T(8,128)(2,1)S(1)}, u32[]{:S(2)}, u32[]{:S(2)}) collective-permute-start(bf16[96,1024]{1,0:T(8,128)(2,1)S(1)} %get-tuple-element.27), channel_id=1, source_target_pairs={{0,6},{1,7},{2,4},{3,5},{4,2},{5,3},{6,0},{7,1},{8,14},{9,15},{10,... | collective-permute-start | bytes 589832 | tf_op jit(solution)/shard_map/ppermute | solution.py:434
  169.5 3.1 %collective-permute-done.14.refs_2_ = bf16[96,1024]{1,0:T(8,128)(2,1)S(1)} collective-permute-done((bf16[96,1024]{1,0:T(8,128)(2,1)S(1)}, bf16[96,1024]{1,0:T(8,128)(2,1)S(1)}, u32[]{:S(2)}, u32[]{:S(2)}) %collective-permute-start.14) | collective-permute-done | bytes 196640 | tf_op jit(solution)/shard_map/ppermute | solution.py:434
  172.6 2.6 %unpack_0.1.refs_4_ = f32[128,8,1024]{2,1,0:T(8,128)} custom-call(s32[1]{0:T(128)} %bitcast.me_ref, s32[48,128]{1,0:T(8,128)S(1)} %get-tuple-element.23.table_ref, bf16[96,1024]{1,0:T(8,128)(2,1)S(1)} %get-tuple-element.37.refs_0_, bf16[96,1024]{1,0:T(8,128)(2,1)S(1)} %collective-permute-done.27.refs_1_, ...), custom_call_target="tpu_custom_call" | custom-call | bytes 2359296 | tf_op jit(solution)/shard_map/unpack_0/pallas_call | solution.py:404
  175.2 2.6 %unpack_3.1.refs_4_ = f32[128,8,1024]{2,1,0:T(8,128)} custom-call(s32[1]{0:T(128)} %bitcast.me_ref, s32[48,128]{1,0:T(8,128)S(1)} %get-tuple-element.23.table_ref, bf16[96,1024]{1,0:T(8,128)(2,1)S(1)} %collective-permute-done.20.refs_0_, bf16[96,1024]{1,0:T(8,128)(2,1)S(1)} %collective-permute-done.21.refs_1_, ...), custom_call_target="tpu_custom_call", output_to_operand_aliasing={{}: (6, {})} | custom-call | bytes 2359296 | tf_op jit(solution)/shard_map/unpack_3/pallas_call | solution.py:404
  177.8 2.6 %unpack_2.1.refs_4_ = f32[128,8,1024]{2,1,0:T(8,128)} custom-call(s32[1]{0:T(128)} %bitcast.me_ref, s32[48,128]{1,0:T(8,128)S(1)} %get-tuple-element.23.table_ref, bf16[96,1024]{1,0:T(8,128)(2,1)S(1)} %collective-permute-done.12.refs_0_, bf16[96,1024]{1,0:T(8,128)(2,1)S(1)} %collective-permute-done.13.refs_1_, ...), custom_call_target="tpu_custom_call", output_to_operand_aliasing={{}: (6, {})} | custom-call | bytes 2359296 | tf_op jit(solution)/shard_map/unpack_2/pallas_call | solution.py:404
  180.4 5.9 %collective-permute-done.6.refs_2_ = bf16[96,1024]{1,0:T(8,128)(2,1)S(1)} collective-permute-done((bf16[96,1024]{1,0:T(8,128)(2,1)S(1)}, bf16[96,1024]{1,0:T(8,128)(2,1)S(1)}, u32[]{:S(2)}, u32[]{:S(2)}) %collective-permute-start.6) | collective-permute-done | bytes 196640 | tf_op jit(solution)/shard_map/ppermute | solution.py:434
  186.3 4.5 %collective-permute-done.7.refs_3_ = bf16[96,1024]{1,0:T(8,128)(2,1)S(1)} collective-permute-done((bf16[96,1024]{1,0:T(8,128)(2,1)S(1)}, bf16[96,1024]{1,0:T(8,128)(2,1)S(1)}, u32[]{:S(2)}, u32[]{:S(2)}) %collective-permute-start.7) | collective-permute-done | bytes 196640 | tf_op jit(solution)/shard_map/ppermute | solution.py:434
  190.9 2.6 %unpack_1.1 = f32[128,8,1024]{2,1,0:T(8,128)} custom-call(s32[1]{0:T(128)} %bitcast.me_ref, s32[48,128]{1,0:T(8,128)S(1)} %get-tuple-element.23.table_ref, bf16[96,1024]{1,0:T(8,128)(2,1)S(1)} %collective-permute-done.4.refs_0_, bf16[96,1024]{1,0:T(8,128)(2,1)S(1)} %collective-permute-done.5.refs_1_, ...), custom_call_target="tpu_custom_call", output_to_operand_aliasing={{}: (6, {})} | custom-call | bytes 2359296 | tf_op jit(solution)/shard_map/unpack_1/pallas_call | solution.py:404
  (45 shorter events, 4.1 us)
Async XLA Ops:
  4.2 6.8 %collective-permute-start.24 = (bf16[560,128]{1,0:T(8,128)(2,1)S(1)}, bf16[560,128]{1,0:T(8,128)(2,1)S(1)}, u32[]{:S(2)}, u32[]{:S(2)}) collective-permute-start(bf16[560,128]{1,0:T(8,128)(2,1)S(1)} %get-tuple-element.24.refs_0_), channel_id=1, source_target_pairs={{0,1},{1,0},{2,3},{3,2},{4,5},{5,4},{6,7},{7,6},{8,9},{9,8},{10,11... | collective-permute-start | bytes 430088 | tf_op jit(solution)/shard_map/ppermute | solution.py:434
  4.7 9.1 %collective-permute-start.16 = (bf16[560,128]{1,0:T(8,128)(2,1)S(1)}, bf16[560,128]{1,0:T(8,128)(2,1)S(1)}, u32[]{:S(2)}, u32[]{:S(2)}) collective-permute-start(bf16[560,128]{1,0:T(8,128)(2,1)S(1)} %get-tuple-element.24.refs_0_), channel_id=1, source_target_pairs={{0,12},{1,13},{2,14},{3,15},{4,8},{5,9},{6,10},{7,11},{8,4},{9,5},... | collective-permute-start | bytes 430088 | tf_op jit(solution)/shard_map/ppermute | solution.py:434
  9.4 6.6 %collective-permute-start.25 = (bf16[560,128]{1,0:T(8,128)(2,1)S(1)}, bf16[560,128]{1,0:T(8,128)(2,1)S(1)}, u32[]{:S(2)}, u32[]{:S(2)}) collective-permute-start(bf16[560,128]{1,0:T(8,128)(2,1)S(1)} %get-tuple-element.24.refs_0_), channel_id=1, source_target_pairs={{0,2},{1,3},{2,0},{3,1},{4,6},{5,7},{6,4},{7,5},{8,10},{9,11},{10,... | collective-permute-start | bytes 430088 | tf_op jit(solution)/shard_map/ppermute | solution.py:434
  11.0 7.2 %collective-permute-start.26 = (bf16[560,128]{1,0:T(8,128)(2,1)S(1)}, bf16[560,128]{1,0:T(8,128)(2,1)S(1)}, u32[]{:S(2)}, u32[]{:S(2)}) collective-permute-start(bf16[560,128]{1,0:T(8,128)(2,1)S(1)} %get-tuple-element.24.refs_0_), channel_id=1, source_target_pairs={{0,3},{1,2},{2,1},{3,0},{4,7},{5,6},{6,5},{7,4},{8,11},{9,10},{10,... | collective-permute-start | bytes 430088 | tf_op jit(solution)/shard_map/ppermute | solution.py:434
  11.0 11.2 %collective-permute-start.8 = (bf16[560,128]{1,0:T(8,128)(2,1)S(1)}, bf16[560,128]{1,0:T(8,128)(2,1)S(1)}, u32[]{:S(2)}, u32[]{:S(2)}) collective-permute-start(bf16[560,128]{1,0:T(8,128)(2,1)S(1)} %get-tuple-element.24.refs_0_), channel_id=1, source_target_pairs={{0,8},{1,9},{2,10},{3,11},{4,12},{5,13},{6,14},{7,15},{8,0},{9,1},... | collective-permute-start | bytes 430088 | tf_op jit(solution)/shard_map/ppermute | solution.py:434
  11.0 45.7 %collective-permute-start = (bf16[560,128]{1,0:T(8,128)(2,1)S(1)}, bf16[560,128]{1,0:T(8,128)(2,1)S(1)}, u32[]{:S(2)}, u32[]{:S(2)}) collective-permute-start(bf16[560,128]{1,0:T(8,128)(2,1)S(1)} %get-tuple-element.24.refs_0_), channel_id=1, source_target_pairs={{0,4},{1,5},{2,6},{3,7},{4,0},{5,1},{6,2},{7,3},{8,12},{9,13},{10,... | collective-permute-start | bytes 430088 | tf_op jit(solution)/shard_map/ppermute | solution.py:434
  13.9 42.9 %collective-permute-start.17 = (bf16[560,128]{1,0:T(8,128)(2,1)S(1)}, bf16[560,128]{1,0:T(8,128)(2,1)S(1)}, u32[]{:S(2)}, u32[]{:S(2)}) collective-permute-start(bf16[560,128]{1,0:T(8,128)(2,1)S(1)} %collective-permute-done.16.refs_0_), channel_id=1, source_target_pairs={{0,1},{1,0},{2,3},{3,2},{4,5},{5,4},{6,7},{7,6},{8,9},{9,8},{10,11... | collective-permute-start | bytes 430088 | tf_op jit(solution)/shard_map/ppermute | solution.py:434
  16.0 41.3 %collective-permute-start.18 = (bf16[560,128]{1,0:T(8,128)(2,1)S(1)}, bf16[560,128]{1,0:T(8,128)(2,1)S(1)}, u32[]{:S(2)}, u32[]{:S(2)}) collective-permute-start(bf16[560,128]{1,0:T(8,128)(2,1)S(1)} %collective-permute-done.16.refs_0_), channel_id=1, source_target_pairs={{0,2},{1,3},{2,0},{3,1},{4,6},{5,7},{6,4},{7,5},{8,10},{9,11},{10,... | collective-permute-start | bytes 430088 | tf_op jit(solution)/shard_map/ppermute | solution.py:434
  18.2 39.3 %collective-permute-start.19 = (bf16[560,128]{1,0:T(8,128)(2,1)S(1)}, bf16[560,128]{1,0:T(8,128)(2,1)S(1)}, u32[]{:S(2)}, u32[]{:S(2)}) collective-permute-start(bf16[560,128]{1,0:T(8,128)(2,1)S(1)} %collective-permute-done.16.refs_0_), channel_id=1, source_target_pairs={{0,3},{1,2},{2,1},{3,0},{4,7},{5,6},{6,5},{7,4},{8,11},{9,10},{10,... | collective-permute-start | bytes 430088 | tf_op jit(solution)/shard_map/ppermute | solution.py:434
  22.1 36.8 %collective-permute-start.10 = (bf16[560,128]{1,0:T(8,128)(2,1)S(1)}, bf16[560,128]{1,0:T(8,128)(2,1)S(1)}, u32[]{:S(2)}, u32[]{:S(2)}) collective-permute-start(bf16[560,128]{1,0:T(8,128)(2,1)S(1)} %collective-permute-done.8.refs_0_), channel_id=1, source_target_pairs={{0,2},{1,3},{2,0},{3,1},{4,6},{5,7},{6,4},{7,5},{8,10},{9,11},{10,... | collective-permute-start | bytes 430088 | tf_op jit(solution)/shard_map/ppermute | solution.py:434
  23.7 2.2 %copy-start.1 = (bf16[512,4096]{1,0:T(8,128)(2,1)S(1)}, bf16[512,4096]{1,0:T(8,128)(2,1)}, u32[]{:S(2)}) copy-start(bf16[512,4096]{1,0:T(8,128)(2,1)} %refs_4_.7) | copy-start | bytes 12582916
  25.9 33.4 %copy-start.2 = (bf16[512,4096]{1,0:T(8,128)(2,1)S(1)}, bf16[512,4096]{1,0:T(8,128)(2,1)}, u32[]{:S(2)}) copy-start(bf16[512,4096]{1,0:T(8,128)(2,1)} %refs_4_.7) | copy-start | bytes 12582916
  56.6 31.5 %collective-permute-start.11 = (bf16[560,128]{1,0:T(8,128)(2,1)S(1)}, bf16[560,128]{1,0:T(8,128)(2,1)S(1)}, u32[]{:S(2)}, u32[]{:S(2)}) collective-permute-start(bf16[560,128]{1,0:T(8,128)(2,1)S(1)} %collective-permute-done.8.refs_0_), channel_id=1, source_target_pairs={{0,3},{1,2},{2,1},{3,0},{4,7},{5,6},{6,5},{7,4},{8,11},{9,10},{10,... | collective-permute-start | bytes 430088 | tf_op jit(solution)/shard_map/ppermute | solution.py:434
  56.7 31.5 %collective-permute-start.9 = (bf16[560,128]{1,0:T(8,128)(2,1)S(1)}, bf16[560,128]{1,0:T(8,128)(2,1)S(1)}, u32[]{:S(2)}, u32[]{:S(2)}) collective-permute-start(bf16[560,128]{1,0:T(8,128)(2,1)S(1)} %collective-permute-done.8.refs_0_), channel_id=1, source_target_pairs={{0,1},{1,0},{2,3},{3,2},{4,5},{5,4},{6,7},{7,6},{8,9},{9,8},{10,11... | collective-permute-start | bytes 430088 | tf_op jit(solution)/shard_map/ppermute | solution.py:434
  57.3 33.4 %collective-permute-start.1 = (bf16[560,128]{1,0:T(8,128)(2,1)S(1)}, bf16[560,128]{1,0:T(8,128)(2,1)S(1)}, u32[]{:S(2)}, u32[]{:S(2)}) collective-permute-start(bf16[560,128]{1,0:T(8,128)(2,1)S(1)} %collective-permute-done.refs_0_), channel_id=1, source_target_pairs={{0,1},{1,0},{2,3},{3,2},{4,5},{5,4},{6,7},{7,6},{8,9},{9,8},{10,11... | collective-permute-start | bytes 430088 | tf_op jit(solution)/shard_map/ppermute | solution.py:434
  57.4 33.5 %collective-permute-start.2 = (bf16[560,128]{1,0:T(8,128)(2,1)S(1)}, bf16[560,128]{1,0:T(8,128)(2,1)S(1)}, u32[]{:S(2)}, u32[]{:S(2)}) collective-permute-start(bf16[560,128]{1,0:T(8,128)(2,1)S(1)} %collective-permute-done.refs_0_), channel_id=1, source_target_pairs={{0,2},{1,3},{2,0},{3,1},{4,6},{5,7},{6,4},{7,5},{8,10},{9,11},{10,... | collective-permute-start | bytes 430088 | tf_op jit(solution)/shard_map/ppermute | solution.py:434
  58.9 35.3 %collective-permute-start.3 = (bf16[560,128]{1,0:T(8,128)(2,1)S(1)}, bf16[560,128]{1,0:T(8,128)(2,1)S(1)}, u32[]{:S(2)}, u32[]{:S(2)}) collective-permute-start(bf16[560,128]{1,0:T(8,128)(2,1)S(1)} %collective-permute-done.refs_0_), channel_id=1, source_target_pairs={{0,3},{1,2},{2,1},{3,0},{4,7},{5,6},{6,5},{7,4},{8,11},{9,10},{10,... | collective-permute-start | bytes 430088 | tf_op jit(solution)/shard_map/ppermute | solution.py:434
  88.1 37.0 %collective-permute-start.27 = (bf16[96,1024]{1,0:T(8,128)(2,1)S(1)}, bf16[96,1024]{1,0:T(8,128)(2,1)S(1)}, u32[]{:S(2)}, u32[]{:S(2)}) collective-permute-start(bf16[96,1024]{1,0:T(8,128)(2,1)S(1)} %get-tuple-element.38), channel_id=1, source_target_pairs={{0,1},{1,0},{2,3},{3,2},{4,5},{5,4},{6,7},{7,6},{8,9},{9,8},{10,11... | collective-permute-start | bytes 589832 | tf_op jit(solution)/shard_map/ppermute | solution.py:434
  88.2 37.0 %collective-permute-start.28 = (bf16[96,1024]{1,0:T(8,128)(2,1)S(1)}, bf16[96,1024]{1,0:T(8,128)(2,1)S(1)}, u32[]{:S(2)}, u32[]{:S(2)}) collective-permute-start(bf16[96,1024]{1,0:T(8,128)(2,1)S(1)} %get-tuple-element.39), channel_id=1, source_target_pairs={{0,2},{1,3},{2,0},{3,1},{4,6},{5,7},{6,4},{7,5},{8,10},{9,11},{10,... | collective-permute-start | bytes 589832 | tf_op jit(solution)/shard_map/ppermute | solution.py:434
  90.7 35.2 %collective-permute-start.29 = (bf16[96,1024]{1,0:T(8,128)(2,1)S(1)}, bf16[96,1024]{1,0:T(8,128)(2,1)S(1)}, u32[]{:S(2)}, u32[]{:S(2)}) collective-permute-start(bf16[96,1024]{1,0:T(8,128)(2,1)S(1)} %get-tuple-element.40), channel_id=1, source_target_pairs={{0,3},{1,2},{2,1},{3,0},{4,7},{5,6},{6,5},{7,4},{8,11},{9,10},{10,... | collective-permute-start | bytes 589832 | tf_op jit(solution)/shard_map/ppermute | solution.py:434
  90.9 35.1 %collective-permute-start.20 = (bf16[96,1024]{1,0:T(8,128)(2,1)S(1)}, bf16[96,1024]{1,0:T(8,128)(2,1)S(1)}, u32[]{:S(2)}, u32[]{:S(2)}) collective-permute-start(bf16[96,1024]{1,0:T(8,128)(2,1)S(1)} %get-tuple-element.33), channel_id=1, source_target_pairs={{0,12},{1,13},{2,14},{3,15},{4,8},{5,9},{6,10},{7,11},{8,4},{9,5},... | collective-permute-start | bytes 589832 | tf_op jit(solution)/shard_map/ppermute | solution.py:434
  94.3 38.0 %collective-permute-start.21 = (bf16[96,1024]{1,0:T(8,128)(2,1)S(1)}, bf16[96,1024]{1,0:T(8,128)(2,1)S(1)}, u32[]{:S(2)}, u32[]{:S(2)}) collective-permute-start(bf16[96,1024]{1,0:T(8,128)(2,1)S(1)} %get-tuple-element.34), channel_id=1, source_target_pairs={{0,13},{1,12},{2,15},{3,14},{4,9},{5,8},{6,11},{7,10},{8,5},{9,4},... | collective-permute-start | bytes 589832 | tf_op jit(solution)/shard_map/ppermute | solution.py:434
  125.1 37.6 %collective-permute-start.22 = (bf16[96,1024]{1,0:T(8,128)(2,1)S(1)}, bf16[96,1024]{1,0:T(8,128)(2,1)S(1)}, u32[]{:S(2)}, u32[]{:S(2)}) collective-permute-start(bf16[96,1024]{1,0:T(8,128)(2,1)S(1)} %get-tuple-element.35), channel_id=1, source_target_pairs={{0,14},{1,15},{2,12},{3,13},{4,10},{5,11},{6,8},{7,9},{8,6},{9,7},... | collective-permute-start | bytes 589832 | tf_op jit(solution)/shard_map/ppermute | solution.py:434
  125.2 37.6 %collective-permute-start.23 = (bf16[96,1024]{1,0:T(8,128)(2,1)S(1)}, bf16[96,1024]{1,0:T(8,128)(2,1)S(1)}, u32[]{:S(2)}, u32[]{:S(2)}) collective-permute-start(bf16[96,1024]{1,0:T(8,128)(2,1)S(1)} %get-tuple-element.36), channel_id=1, source_target_pairs={{0,15},{1,14},{2,13},{3,12},{4,11},{5,10},{6,9},{7,8},{8,7},{9,6},... | collective-permute-start | bytes 589832 | tf_op jit(solution)/shard_map/ppermute | solution.py:434
  126.0 37.8 %collective-permute-start.12 = (bf16[96,1024]{1,0:T(8,128)(2,1)S(1)}, bf16[96,1024]{1,0:T(8,128)(2,1)S(1)}, u32[]{:S(2)}, u32[]{:S(2)}) collective-permute-start(bf16[96,1024]{1,0:T(8,128)(2,1)S(1)} %get-tuple-element.29), channel_id=1, source_target_pairs={{0,8},{1,9},{2,10},{3,11},{4,12},{5,13},{6,14},{7,15},{8,0},{9,1},... | collective-permute-start | bytes 589832 | tf_op jit(solution)/shard_map/ppermute | solution.py:434
  126.0 41.5 %collective-permute-start.13 = (bf16[96,1024]{1,0:T(8,128)(2,1)S(1)}, bf16[96,1024]{1,0:T(8,128)(2,1)S(1)}, u32[]{:S(2)}, u32[]{:S(2)}) collective-permute-start(bf16[96,1024]{1,0:T(8,128)(2,1)S(1)} %get-tuple-element.30), channel_id=1, source_target_pairs={{0,9},{1,8},{2,11},{3,10},{4,13},{5,12},{6,15},{7,14},{8,1},{9,0},... | collective-permute-start | bytes 589832 | tf_op jit(solution)/shard_map/ppermute | solution.py:434
  132.3 40.4 %collective-permute-start.14 = (bf16[96,1024]{1,0:T(8,128)(2,1)S(1)}, bf16[96,1024]{1,0:T(8,128)(2,1)S(1)}, u32[]{:S(2)}, u32[]{:S(2)}) collective-permute-start(bf16[96,1024]{1,0:T(8,128)(2,1)S(1)} %get-tuple-element.31), channel_id=1, source_target_pairs={{0,10},{1,11},{2,8},{3,9},{4,14},{5,15},{6,12},{7,13},{8,2},{9,3},... | collective-permute-start | bytes 589832 | tf_op jit(solution)/shard_map/ppermute | solution.py:434
  162.7 15.1 %collective-permute-start.15 = (bf16[96,1024]{1,0:T(8,128)(2,1)S(1)}, bf16[96,1024]{1,0:T(8,128)(2,1)S(1)}, u32[]{:S(2)}, u32[]{:S(2)}) collective-permute-start(bf16[96,1024]{1,0:T(8,128)(2,1)S(1)} %get-tuple-element.32), channel_id=1, source_target_pairs={{0,11},{1,10},{2,9},{3,8},{4,15},{5,14},{6,13},{7,12},{8,3},{9,2},... | collective-permute-start | bytes 589832 | tf_op jit(solution)/shard_map/ppermute | solution.py:434
  162.8 17.6 %collective-permute-start.4 = (bf16[96,1024]{1,0:T(8,128)(2,1)S(1)}, bf16[96,1024]{1,0:T(8,128)(2,1)S(1)}, u32[]{:S(2)}, u32[]{:S(2)}) collective-permute-start(bf16[96,1024]{1,0:T(8,128)(2,1)S(1)} %get-tuple-element.25), channel_id=1, source_target_pairs={{0,4},{1,5},{2,6},{3,7},{4,0},{5,1},{6,2},{7,3},{8,12},{9,13},{10,... | collective-permute-start | bytes 589832 | tf_op jit(solution)/shard_map/ppermute | solution.py:434
  163.7 16.7 %collective-permute-start.5 = (bf16[96,1024]{1,0:T(8,128)(2,1)S(1)}, bf16[96,1024]{1,0:T(8,128)(2,1)S(1)}, u32[]{:S(2)}, u32[]{:S(2)}) collective-permute-start(bf16[96,1024]{1,0:T(8,128)(2,1)S(1)} %get-tuple-element.26), channel_id=1, source_target_pairs={{0,5},{1,4},{2,7},{3,6},{4,1},{5,0},{6,3},{7,2},{8,13},{9,12},{10,... | collective-permute-start | bytes 589832 | tf_op jit(solution)/shard_map/ppermute | solution.py:434
  167.5 18.9 %collective-permute-start.6 = (bf16[96,1024]{1,0:T(8,128)(2,1)S(1)}, bf16[96,1024]{1,0:T(8,128)(2,1)S(1)}, u32[]{:S(2)}, u32[]{:S(2)}) collective-permute-start(bf16[96,1024]{1,0:T(8,128)(2,1)S(1)} %get-tuple-element.27), channel_id=1, source_target_pairs={{0,6},{1,7},{2,4},{3,5},{4,2},{5,3},{6,0},{7,1},{8,14},{9,15},{10,... | collective-permute-start | bytes 589832 | tf_op jit(solution)/shard_map/ppermute | solution.py:434
  172.6 18.2 %collective-permute-start.7 = (bf16[96,1024]{1,0:T(8,128)(2,1)S(1)}, bf16[96,1024]{1,0:T(8,128)(2,1)S(1)}, u32[]{:S(2)}, u32[]{:S(2)}) collective-permute-start(bf16[96,1024]{1,0:T(8,128)(2,1)S(1)} %get-tuple-element.28), channel_id=1, source_target_pairs={{0,7},{1,6},{2,5},{3,4},{4,3},{5,2},{6,1},{7,0},{8,15},{9,14},{10,... | collective-permute-start | bytes 589832 | tf_op jit(solution)/shard_map/ppermute | solution.py:434
  (1 other events, 0.9 us)

commit v3 on v0

--- a/solution.py
+++ b/solution.py
@@ -120,9 +120,9 @@
     )(spectra, named, wanted)
 
 
-def profile_kernel(depth, num_query, touches, me_ref, *refs):
-    shards, library_ref, refs = refs[:NEAR], refs[NEAR], refs[NEAR + 1 :]
-    outs, refs = refs[:NEAR], refs[NEAR:]
+def profile_kernel(near, depth, num_query, touches, me_ref, *refs):
+    shards, library_ref, refs = refs[:near], refs[near], refs[near + 1 :]
+    outs, refs = refs[:near], refs[near:]
     (
         query_ref, record_ref, found_ref, table_ref, answer_ref,
         cand_ref, packed_ref, spectrum_ref, left_ref, right_ref, product_ref, sem_ref,
@@ -140,20 +140,20 @@
     lane16 = lax.broadcasted_iota(jnp.int32, (rows, LANES), 1)
 
     copies = [
-        pltpu.make_async_copy(shards[e], query_ref.at[e], sem_ref.at[e]) for e in range(NEAR)
+        pltpu.make_async_copy(shards[e], query_ref.at[e], sem_ref.at[e]) for e in range(near)
     ]
     for copy in copies:
         copy.start()
     cand_ref[...] = jnp.zeros(cand_ref.shape, cand_ref.dtype)
     right_ref[...] = jnp.zeros(right_ref.shape, right_ref.dtype)
     found_ref[...] = jnp.zeros(found_ref.shape, found_ref.dtype)
-    for e in range(NEAR):
+    for e in range(near):
         copies[e].wait()
         record_ref[...] = query_ref[e, query_rows:, :].astype(jnp.float32)
         found_ref[e * per_block : (e + 1) * per_block, :] = record_values(
             record_ref[pl.ds(me_ref[0] * per_block, per_block), :]
         )
-    to_scalars = pltpu.make_async_copy(found_ref, table_ref, sem_ref.at[NEAR])
+    to_scalars = pltpu.make_async_copy(found_ref, table_ref, sem_ref.at[near])
     to_scalars.start()
     to_scalars.wait()
 
@@ -247,7 +247,7 @@
         )
         return jnp.dot(left, right_ref[...], preferred_element_type=jnp.float32)
 
-    slots = NEAR * depth
+    slots = near * depth
     height = GROUPS // CHAINS * (offsets + 1) * rows
 
     @pl.loop(0, slots // 2)
@@ -290,7 +290,7 @@
             outs[e],
             sem_ref.at[e],
         )
-        for e in range(NEAR)
+        for e in range(near)
     ]
     for copy in back:
         copy.start()
@@ -299,27 +299,28 @@
 
 
 def profile(part, depth, num_query, touches, me, shards, library):
+    near = len(shards)
     blocks = library.shape[1]
     offsets = SHIFTS // LANES
     tiles = blocks // GROUPS
     records = shards[0].shape[0] - num_query * blocks
     per_block = rounded(depth, ROW_SLOTS) // ROW_SLOTS
-    table = (rounded(NEAR * per_block, 8), LANES)
+    table = (rounded(near * per_block, 8), LANES)
     smem = pl.BlockSpec(memory_space=pltpu.SMEM)
     vmem = pl.BlockSpec(memory_space=pltpu.VMEM)
     hbm = pl.BlockSpec(memory_space=pl.ANY)
-    answers = NEAR * depth * PER_TOUCH
+    answers = near * depth * PER_TOUCH
     flops = answers * 2 * (offsets + 1) * (blocks + 4) * LANES * LANES
     return pl.pallas_call(
-        functools.partial(profile_kernel, depth, num_query, touches),
+        functools.partial(profile_kernel, near, depth, num_query, touches),
         out_shape=[
             jax.ShapeDtypeStruct((depth * PER_TOUCH, SHIFTS), jnp.bfloat16)
-            for _ in range(NEAR)
+            for _ in range(near)
         ],
-        in_specs=[smem] + [hbm] * NEAR + [vmem],
-        out_specs=[hbm] * NEAR,
+        in_specs=[smem] + [hbm] * near + [vmem],
+        out_specs=[hbm] * near,
         scratch_shapes=[
-            pltpu.VMEM((NEAR, *shards[0].shape), jnp.bfloat16),
+            pltpu.VMEM((near, *shards[0].shape), jnp.bfloat16),
             pltpu.VMEM((records, LANES), jnp.float32),
             pltpu.VMEM(table, jnp.int32),
             pltpu.SMEM(table, jnp.int32),
@@ -330,7 +331,7 @@
             pltpu.VMEM((GROUPS, (tiles + offsets + 1) * 16, LANES), jnp.bfloat16),
             pltpu.VMEM(((tiles + 1) * LANES, 2 * LANES), jnp.bfloat16),
             pltpu.VMEM((GROUPS * (offsets + 1) * 16, 2 * LANES), jnp.float32),
-            pltpu.SemaphoreType.DMA((NEAR + 1,)),
+            pltpu.SemaphoreType.DMA((near + 1,)),
         ],
         compiler_params=pltpu.CompilerParams(vmem_limit_bytes=VMEM_LIMIT),
         cost_estimate=pl.CostEstimate(
@@ -340,8 +341,8 @@
     )(me, *shards, library)
 
 
-def unpack_kernel(part, depth, me_ref, table_ref, *refs):
-    got, refs = refs[:NEAR], refs[-3:]
+def unpack_kernel(distance, near, depth, me_ref, table_ref, *refs):
+    got, refs = refs[:near], refs[-3:]
     out_ref, stage_ref, sem_ref = refs
     per_block = rounded(depth, ROW_SLOTS) // ROW_SLOTS
 
@@ -349,11 +350,11 @@
         return pltpu.make_async_copy(stage_ref.at[slot], out_ref.at[touch], sem_ref.at[slot])
 
     def touch_of(e, s):
-        block = jnp.bitwise_xor(me_ref[0], NEAR * part + e)
+        block = jnp.bitwise_xor(me_ref[0], distance + e)
         line = block * per_block + s // ROW_SLOTS
         return table_ref[line, s % ROW_SLOTS * SLOT_LANES + 2 * PER_TOUCH] - 1
 
-    for e in range(NEAR):
+    for e in range(near):
         for s in range(depth):
             touch = touch_of(e, s)
             slot = e * depth + s
@@ -365,7 +366,7 @@
                 )
                 copy(slot, touch).start()
 
-    for e in range(NEAR):
+    for e in range(near):
         for s in range(depth):
             touch = touch_of(e, s)
 
@@ -374,27 +375,28 @@
                 copy(e * depth + s, touch).wait()
 
 
-def unpack(part, depth, touched, me, table, got, out):
+def unpack(distance, depth, touched, me, table, got, out):
     shifts = got[0].shape[1]
+    near = len(got)
     smem = pl.BlockSpec(memory_space=pltpu.SMEM)
     vmem = pl.BlockSpec(memory_space=pltpu.VMEM)
     hbm = pl.BlockSpec(memory_space=pl.ANY)
     more = () if out is None else (out,)
     return pl.pallas_call(
-        functools.partial(unpack_kernel, part, depth),
+        functools.partial(unpack_kernel, distance, near, depth),
         out_shape=jax.ShapeDtypeStruct((touched, PER_TOUCH, shifts), jnp.float32),
-        in_specs=[smem] * 2 + [vmem] * NEAR + [hbm] * len(more),
+        in_specs=[smem] * 2 + [vmem] * near + [hbm] * len(more),
         out_specs=hbm,
         scratch_shapes=[
-            pltpu.VMEM((NEAR * depth, PER_TOUCH, shifts), jnp.float32),
-            pltpu.SemaphoreType.DMA((NEAR * depth,)),
+            pltpu.VMEM((near * depth, PER_TOUCH, shifts), jnp.float32),
+            pltpu.SemaphoreType.DMA((near * depth,)),
         ],
-        input_output_aliases={2 + NEAR: 0} if more else {},
+        input_output_aliases={2 + near: 0} if more else {},
         compiler_params=pltpu.CompilerParams(vmem_limit_bytes=VMEM_LIMIT),
         cost_estimate=pl.CostEstimate(
-            flops=0, bytes_accessed=NEAR * got[0].size * 6, transcendentals=0
+            flops=0, bytes_accessed=near * got[0].size * 6, transcendentals=0
         ),
-        name=f"unpack_{part}",
+        name=f"unpack_{distance}",
     )(me, table, *got, *more)
 
 
@@ -423,13 +425,19 @@
         part: [across(heads[part], e) for e in range(NEAR)] for part in order
     }
     rows = library.reshape(-1, blocks, LANES)
+    steps = [(part, 0, NEAR) for part in order[:-1]]
+    half = NEAR // 2
+    steps += [(order[-1], first, half) for first in (0, half)]
     got = {}
-    for part in order:
-        answers = profile(part, depth, num_query, touches, me, shards[part], rows)
-        got[part] = [across(answers[e], NEAR * part + e) for e in range(NEAR)]
+    for part, first, count in steps:
+        distance = NEAR * part + first
+        answers = profile(
+            distance, depth, num_query, touches, me, shards[part][first : first + count], rows
+        )
+        got[distance] = [across(answer, distance + e) for e, answer in enumerate(answers)]
     out = None
-    for part in order:
-        out = unpack(part, depth, num_query * touches, me, table, got[part], out)
+    for distance, answers in got.items():
+        out = unpack(distance, depth, num_query * touches, me, table, answers, out)
     return out.reshape(num_query, touches * per_touch, SHIFTS)
 
 

time: 180 us -> 192 us (1.067)
  starting transfers between devices: 84.7 us -> 95 us
  Pallas kernels: 68.4 us -> 76.6 us
  waiting for transfers between devices: 19.3 us -> 13.4 us
    ppermute x30, starting transfers between devices: 84.7 us -> 95 us  [across(): return lax.ppermute(value, 'lib', pairs)]
    pallas_call x8 -> x10, Pallas kernels: 66.7 us -> 74.9 us  [the longest x5 62.9 us: profile(): pl.pallas_call(functools.partial(profile_kernel, near, depth, num_query,...]
    ppermute x30, waiting for transfers between devices: 19.3 us -> 13.4 us  [across(): return lax.ppermute(value, 'lib', pairs)]
  transfers between devices with their start and end apart: 30 -> 30, of which waited for: 6 -> 6; matrix products, arithmetic and copies ran while one was open for 2% -> 2% of each run, Pallas kernels for 36% -> 38%
where the time goes in v3:
time: 192 us; the launch traced here: 191 us
  starting transfers between devices  95 us (49%)
  Pallas kernels  76.6 us (40%)
  waiting for transfers between devices  13.4 us (7%)
  local copies, waits for them, and re-layouts  5.95 us (3%)
    ppermute x30, starting transfers between devices, across(): return lax.ppermute(value, 'lib', pairs)  95 us
    pallas_call x5, Pallas kernels, profile(): pl.pallas_call(functools.partial(profile_kernel, near, depth, num_query,...  62.9 us
    ppermute x30, waiting for transfers between devices, across(): return lax.ppermute(value, 'lib', pairs)  13.4 us
    pallas_call x5, Pallas kernels, unpack(): pl.pallas_call(functools.partial(unpack_kernel, distance, near, depth), o...  12 us
    unnamed x5, local copies, waits for them, and re-layouts  5.95 us
  transfers between devices with their start and end apart: 30, of which 6 were waited for; matrix products, arithmetic and copies ran while one was open for 2% of the time, Pallas kernels for 38%

profile of v3, /device:TPU:0, one launch (start us, length us, event | category | flops | bytes accessed | tf_op | source)
XLA Modules:
  0.0 191.2 jit_solution(12865277517090992913)
XLA Ops:
  1.6 0.9 copy-done
  2.5 1.7 prepare.1
  4.2 2.5 %collective-permute-start.26 = (bf16[560,128]{1,0:T(8,128)(2,1)S(1)}, bf16[560,128]{1,0:T(8,128)(2,1)S(1)}, u32[]{:S(2)}, u32[]{:S(2)}) collective-permute-start(bf16[560,128]{1,0:T(8,128)(2,1)S(1)} %get-tuple-element.24.refs_0_), channel_id=1, source_target_pairs={{0,3},{1,2},{2,1},{3,0},{4,7},{5,6},{6,5},{7,4},{8,11},{9,10},{10,... | collective-permute-start | bytes 430088 | tf_op jit(solution)/shard_map/ppermute | solution.py:416
  6.7 3.6 %collective-permute-start.16 = (bf16[560,128]{1,0:T(8,128)(2,1)S(1)}, bf16[560,128]{1,0:T(8,128)(2,1)S(1)}, u32[]{:S(2)}, u32[]{:S(2)}) collective-permute-start(bf16[560,128]{1,0:T(8,128)(2,1)S(1)} %get-tuple-element.24.refs_0_), channel_id=1, source_target_pairs={{0,12},{1,13},{2,14},{3,15},{4,8},{5,9},{6,10},{7,11},{8,4},{9,5},... | collective-permute-start | bytes 430088 | tf_op jit(solution)/shard_map/ppermute | solution.py:416
  10.9 3.5 %copy.11 = bf16[64,8,32,128]{3,2,1,0:T(8,128)(2,1)S(1)} copy(bf16[64,8,32,128]{3,1,2,0:T(8,128)(2,1)} %bitcast.11) | data formatting | bytes 8388608
  15.3 0.9 collective-permute-start.19
  17.2 15.8 %profile_0.1 = (bf16[96,1024]{1,0:T(8,128)(2,1)S(1)}, bf16[96,1024]{1,0:T(8,128)(2,1)S(1)}, bf16[96,1024]{1,0:T(8,128)(2,1)S(1)}, bf16[96,1024]{1,0:T(8,128)(2,1)S(1)}) custom-call(s32[1]{0:T(128)} %bitcast.me_ref, bf16[560,128]{1,0:T(8,128)(2,1)S(1)} %get-tuple-element.24.refs_0_, bf16[560,128]{1,0:T(8,128)(2,1)S(1)} %collective-permute-done.24.refs_1_, ...), custom_call_target="tpu_custom_call" | custom-call | flops 32614907904 | bytes 8388608 | tf_op jit(solution)/shard_map/profile_0/pallas_call | solution.py:314
  33.0 5.3 %collective-permute-start.27 = (bf16[96,1024]{1,0:T(8,128)(2,1)S(1)}, bf16[96,1024]{1,0:T(8,128)(2,1)S(1)}, u32[]{:S(2)}, u32[]{:S(2)}) collective-permute-start(bf16[96,1024]{1,0:T(8,128)(2,1)S(1)} %get-tuple-element.38), channel_id=1, source_target_pairs={{0,1},{1,0},{2,3},{3,2},{4,5},{5,4},{6,7},{7,6},{8,9},{9,8},{10,11... | collective-permute-start | bytes 589832 | tf_op jit(solution)/shard_map/ppermute | solution.py:416
  38.3 8.2 %collective-permute-start.11 = (bf16[560,128]{1,0:T(8,128)(2,1)S(1)}, bf16[560,128]{1,0:T(8,128)(2,1)S(1)}, u32[]{:S(2)}, u32[]{:S(2)}) collective-permute-start(bf16[560,128]{1,0:T(8,128)(2,1)S(1)} %collective-permute-done.8.refs_0_), channel_id=1, source_target_pairs={{0,3},{1,2},{2,1},{3,0},{4,7},{5,6},{6,5},{7,4},{8,11},{9,10},{10,... | collective-permute-start | bytes 430088 | tf_op jit(solution)/shard_map/ppermute | solution.py:416
  47.0 14.8 %profile_12.1 = (bf16[96,1024]{1,0:T(8,128)(2,1)S(1)}, bf16[96,1024]{1,0:T(8,128)(2,1)S(1)}, bf16[96,1024]{1,0:T(8,128)(2,1)S(1)}, bf16[96,1024]{1,0:T(8,128)(2,1)S(1)}) custom-call(s32[1]{0:T(128)} %bitcast.me_ref, bf16[560,128]{1,0:T(8,128)(2,1)S(1)} %collective-permute-done.16.refs_0_, bf16[560,128]{1,0:T(8,128)(2,1)S(1)} %collective-permute-done.17.refs_1_, ...), custom_call_target="tpu_custom_call" | custom-call | flops 32614907904 | bytes 8388608 | tf_op jit(solution)/shard_map/profile_12/pallas_call | solution.py:314
  61.9 6.8 %collective-permute-start.28 = (bf16[96,1024]{1,0:T(8,128)(2,1)S(1)}, bf16[96,1024]{1,0:T(8,128)(2,1)S(1)}, u32[]{:S(2)}, u32[]{:S(2)}) collective-permute-start(bf16[96,1024]{1,0:T(8,128)(2,1)S(1)} %get-tuple-element.39), channel_id=1, source_target_pairs={{0,2},{1,3},{2,0},{3,1},{4,6},{5,7},{6,4},{7,5},{8,10},{9,11},{10,... | collective-permute-start | bytes 589832 | tf_op jit(solution)/shard_map/ppermute | solution.py:416
  68.6 8.1 %collective-permute-start.5 = (bf16[560,128]{1,0:T(8,128)(2,1)S(1)}, bf16[560,128]{1,0:T(8,128)(2,1)S(1)}, u32[]{:S(2)}, u32[]{:S(2)}) collective-permute-start(bf16[560,128]{1,0:T(8,128)(2,1)S(1)} %collective-permute-done.refs_0_), channel_id=1, source_target_pairs={{0,1},{1,0},{2,3},{3,2},{4,5},{5,4},{6,7},{7,6},{8,9},{9,8},{10,11... | collective-permute-start | bytes 430088 | tf_op jit(solution)/shard_map/ppermute | solution.py:416
  76.7 1.6 collective-permute-start.1
  78.4 14.8 %profile_8.1 = (bf16[96,1024]{1,0:T(8,128)(2,1)S(1)}, bf16[96,1024]{1,0:T(8,128)(2,1)S(1)}, bf16[96,1024]{1,0:T(8,128)(2,1)S(1)}, bf16[96,1024]{1,0:T(8,128)(2,1)S(1)}) custom-call(s32[1]{0:T(128)} %bitcast.me_ref, bf16[560,128]{1,0:T(8,128)(2,1)S(1)} %collective-permute-done.8.refs_0_, bf16[560,128]{1,0:T(8,128)(2,1)S(1)} %collective-permute-done.9.refs_1_, ...), custom_call_target="tpu_custom_call" | custom-call | flops 32614907904 | bytes 8388608 | tf_op jit(solution)/shard_map/profile_8/pallas_call | solution.py:314
  93.2 13.2 %collective-permute-start.29 = (bf16[96,1024]{1,0:T(8,128)(2,1)S(1)}, bf16[96,1024]{1,0:T(8,128)(2,1)S(1)}, u32[]{:S(2)}, u32[]{:S(2)}) collective-permute-start(bf16[96,1024]{1,0:T(8,128)(2,1)S(1)} %get-tuple-element.40), channel_id=1, source_target_pairs={{0,3},{1,2},{2,1},{3,0},{4,7},{5,6},{6,5},{7,4},{8,11},{9,10},{10,... | collective-permute-start | bytes 589832 | tf_op jit(solution)/shard_map/ppermute | solution.py:416
  106.4 3.4 %collective-permute-start.20 = (bf16[96,1024]{1,0:T(8,128)(2,1)S(1)}, bf16[96,1024]{1,0:T(8,128)(2,1)S(1)}, u32[]{:S(2)}, u32[]{:S(2)}) collective-permute-start(bf16[96,1024]{1,0:T(8,128)(2,1)S(1)} %get-tuple-element.33), channel_id=1, source_target_pairs={{0,12},{1,13},{2,14},{3,15},{4,8},{5,9},{6,10},{7,11},{8,4},{9,5},... | collective-permute-start | bytes 589832 | tf_op jit(solution)/shard_map/ppermute | solution.py:416
  109.9 8.2 %profile_4.1 = (bf16[96,1024]{1,0:T(8,128)(2,1)S(1)}, bf16[96,1024]{1,0:T(8,128)(2,1)S(1)}) custom-call(s32[1]{0:T(128)} %bitcast.me_ref, bf16[560,128]{1,0:T(8,128)(2,1)S(1)} %collective-permute-done.refs_0_, bf16[560,128]{1,0:T(8,128)(2,1)S(1)} %collective-permute-done.5.refs_1_, bf16[512,32,128]{2,1,0:T(8,128)(2,1)S(1)} %bitcast.8), custom_call_target="tpu_custom_call" | custom-call | flops 16307453952 | bytes 8388608 | tf_op jit(solution)/shard_map/profile_4/pallas_call | solution.py:314
  118.1 8.1 %collective-permute-start.22 = (bf16[96,1024]{1,0:T(8,128)(2,1)S(1)}, bf16[96,1024]{1,0:T(8,128)(2,1)S(1)}, u32[]{:S(2)}, u32[]{:S(2)}) collective-permute-start(bf16[96,1024]{1,0:T(8,128)(2,1)S(1)} %get-tuple-element.35), channel_id=1, source_target_pairs={{0,14},{1,15},{2,12},{3,13},{4,10},{5,11},{6,8},{7,9},{8,6},{9,7},... | collective-permute-start | bytes 589832 | tf_op jit(solution)/shard_map/ppermute | solution.py:416
  126.2 4.0 %collective-permute-start.12 = (bf16[96,1024]{1,0:T(8,128)(2,1)S(1)}, bf16[96,1024]{1,0:T(8,128)(2,1)S(1)}, u32[]{:S(2)}, u32[]{:S(2)}) collective-permute-start(bf16[96,1024]{1,0:T(8,128)(2,1)S(1)} %get-tuple-element.29), channel_id=1, source_target_pairs={{0,8},{1,9},{2,10},{3,11},{4,12},{5,13},{6,14},{7,15},{8,0},{9,1},... | collective-permute-start | bytes 589832 | tf_op jit(solution)/shard_map/ppermute | solution.py:416
  130.2 17.7 %collective-permute-start.14 = (bf16[96,1024]{1,0:T(8,128)(2,1)S(1)}, bf16[96,1024]{1,0:T(8,128)(2,1)S(1)}, u32[]{:S(2)}, u32[]{:S(2)}) collective-permute-start(bf16[96,1024]{1,0:T(8,128)(2,1)S(1)} %get-tuple-element.31), channel_id=1, source_target_pairs={{0,10},{1,11},{2,8},{3,9},{4,14},{5,15},{6,12},{7,13},{8,2},{9,3},... | collective-permute-start | bytes 589832 | tf_op jit(solution)/shard_map/ppermute | solution.py:416
  147.9 9.2 %profile_6.1 = (bf16[96,1024]{1,0:T(8,128)(2,1)S(1)}, bf16[96,1024]{1,0:T(8,128)(2,1)S(1)}) custom-call(s32[1]{0:T(128)} %bitcast.me_ref, bf16[560,128]{1,0:T(8,128)(2,1)S(1)} %collective-permute-done.1.refs_0_, bf16[560,128]{1,0:T(8,128)(2,1)S(1)} %collective-permute-done.2.refs_1_, bf16[512,32,128]{2,1,0:T(8,128)(2,1)S(1)} %bitcast.9), custom_call_target="tpu_custom_call" | custom-call | flops 16307453952 | bytes 8388608 | tf_op jit(solution)/shard_map/profile_6/pallas_call | solution.py:314
  157.6 2.8 %collective-permute-done.12.refs_0_ = bf16[96,1024]{1,0:T(8,128)(2,1)S(1)} collective-permute-done((bf16[96,1024]{1,0:T(8,128)(2,1)S(1)}, bf16[96,1024]{1,0:T(8,128)(2,1)S(1)}, u32[]{:S(2)}, u32[]{:S(2)}) %collective-permute-start.12) | collective-permute-done | bytes 196640 | tf_op jit(solution)/shard_map/ppermute | solution.py:416
  160.4 1.8 collective-permute-start.15
  162.3 2.2 %collective-permute-done.13.refs_1_ = bf16[96,1024]{1,0:T(8,128)(2,1)S(1)} collective-permute-done((bf16[96,1024]{1,0:T(8,128)(2,1)S(1)}, bf16[96,1024]{1,0:T(8,128)(2,1)S(1)}, u32[]{:S(2)}, u32[]{:S(2)}) %collective-permute-start.13) | collective-permute-done | bytes 196640 | tf_op jit(solution)/shard_map/ppermute | solution.py:416
  165.3 2.1 %collective-permute-done.14.refs_2_ = bf16[96,1024]{1,0:T(8,128)(2,1)S(1)} collective-permute-done((bf16[96,1024]{1,0:T(8,128)(2,1)S(1)}, bf16[96,1024]{1,0:T(8,128)(2,1)S(1)}, u32[]{:S(2)}, u32[]{:S(2)}) %collective-permute-start.14) | collective-permute-done | bytes 196640 | tf_op jit(solution)/shard_map/ppermute | solution.py:416
  167.5 5.7 %collective-permute-start.4 = (bf16[96,1024]{1,0:T(8,128)(2,1)S(1)}, bf16[96,1024]{1,0:T(8,128)(2,1)S(1)}, u32[]{:S(2)}, u32[]{:S(2)}) collective-permute-start(bf16[96,1024]{1,0:T(8,128)(2,1)S(1)} %get-tuple-element.26), channel_id=1, source_target_pairs={{0,7},{1,6},{2,5},{3,4},{4,3},{5,2},{6,1},{7,0},{8,15},{9,14},{10,... | collective-permute-start | bytes 589832 | tf_op jit(solution)/shard_map/ppermute | solution.py:416
  173.2 2.7 %unpack_0.1.refs_4_ = f32[128,8,1024]{2,1,0:T(8,128)} custom-call(s32[1]{0:T(128)} %bitcast.me_ref, s32[48,128]{1,0:T(8,128)S(1)} %get-tuple-element.23.table_ref, bf16[96,1024]{1,0:T(8,128)(2,1)S(1)} %get-tuple-element.37.refs_0_, bf16[96,1024]{1,0:T(8,128)(2,1)S(1)} %collective-permute-done.27.refs_1_, ...), custom_call_target="tpu_custom_call" | custom-call | bytes 2359296 | tf_op jit(solution)/shard_map/unpack_0/pallas_call | solution.py:385
  175.9 2.6 %unpack_12.1.refs_4_ = f32[128,8,1024]{2,1,0:T(8,128)} custom-call(s32[1]{0:T(128)} %bitcast.me_ref, s32[48,128]{1,0:T(8,128)S(1)} %get-tuple-element.23.table_ref, bf16[96,1024]{1,0:T(8,128)(2,1)S(1)} %collective-permute-done.20.refs_0_, bf16[96,1024]{1,0:T(8,128)(2,1)S(1)} %collective-permute-done.21.refs_1_, ...), custom_call_target="tpu_custom_call", output_to_operand_aliasing={{}: (6, {})} | custom-call | bytes 2359296 | tf_op jit(solution)/shard_map/unpack_12/pallas_call | solution.py:385
  178.5 2.7 %unpack_8.1.refs_2_ = f32[128,8,1024]{2,1,0:T(8,128)} custom-call(s32[1]{0:T(128)} %bitcast.me_ref, s32[48,128]{1,0:T(8,128)S(1)} %get-tuple-element.23.table_ref, bf16[96,1024]{1,0:T(8,128)(2,1)S(1)} %collective-permute-done.12.refs_0_, bf16[96,1024]{1,0:T(8,128)(2,1)S(1)} %collective-permute-done.13.refs_1_, ...), custom_call_target="tpu_custom_call", output_to_operand_aliasing={{}: (6, {})} | custom-call | bytes 2359296 | tf_op jit(solution)/shard_map/unpack_8/pallas_call | solution.py:385
  181.4 2.0 %unpack_4.1.refs_2_ = f32[128,8,1024]{2,1,0:T(8,128)} custom-call(s32[1]{0:T(128)} %bitcast.me_ref, s32[48,128]{1,0:T(8,128)S(1)} %get-tuple-element.23.table_ref, bf16[96,1024]{1,0:T(8,128)(2,1)S(1)} %collective-permute-done.6.refs_0_, bf16[96,1024]{1,0:T(8,128)(2,1)S(1)} %collective-permute-done.7.refs_1_, ...), custom_call_target="tpu_custom_call", output_to_operand_aliasing={{}: (4, {})} | custom-call | bytes 1179648 | tf_op jit(solution)/shard_map/unpack_4/pallas_call | solution.py:385
  183.5 5.7 %collective-permute-done.4.refs_1_ = bf16[96,1024]{1,0:T(8,128)(2,1)S(1)} collective-permute-done((bf16[96,1024]{1,0:T(8,128)(2,1)S(1)}, bf16[96,1024]{1,0:T(8,128)(2,1)S(1)}, u32[]{:S(2)}, u32[]{:S(2)}) %collective-permute-start.4) | collective-permute-done | bytes 196640 | tf_op jit(solution)/shard_map/ppermute | solution.py:416
  189.2 2.0 %unpack_6.1 = f32[128,8,1024]{2,1,0:T(8,128)} custom-call(s32[1]{0:T(128)} %bitcast.me_ref, s32[48,128]{1,0:T(8,128)S(1)} %get-tuple-element.23.table_ref, bf16[96,1024]{1,0:T(8,128)(2,1)S(1)} %collective-permute-done.3.refs_0_, bf16[96,1024]{1,0:T(8,128)(2,1)S(1)} %collective-permute-done.4.refs_1_, ...), custom_call_target="tpu_custom_call", output_to_operand_aliasing={{}: (4, {})} | custom-call | bytes 1179648 | tf_op jit(solution)/shard_map/unpack_6/pallas_call | solution.py:385
  (44 shorter events, 6.3 us)
Async XLA Ops:
  1.6 0.9 copy-start
  4.2 10.2 %collective-permute-start.26 = (bf16[560,128]{1,0:T(8,128)(2,1)S(1)}, bf16[560,128]{1,0:T(8,128)(2,1)S(1)}, u32[]{:S(2)}, u32[]{:S(2)}) collective-permute-start(bf16[560,128]{1,0:T(8,128)(2,1)S(1)} %get-tuple-element.24.refs_0_), channel_id=1, source_target_pairs={{0,3},{1,2},{2,1},{3,0},{4,7},{5,6},{6,5},{7,4},{8,11},{9,10},{10,... | collective-permute-start | bytes 430088 | tf_op jit(solution)/shard_map/ppermute | solution.py:416
  6.7 8.6 %collective-permute-start.16 = (bf16[560,128]{1,0:T(8,128)(2,1)S(1)}, bf16[560,128]{1,0:T(8,128)(2,1)S(1)}, u32[]{:S(2)}, u32[]{:S(2)}) collective-permute-start(bf16[560,128]{1,0:T(8,128)(2,1)S(1)} %get-tuple-element.24.refs_0_), channel_id=1, source_target_pairs={{0,12},{1,13},{2,14},{3,15},{4,8},{5,9},{6,10},{7,11},{8,4},{9,5},... | collective-permute-start | bytes 430088 | tf_op jit(solution)/shard_map/ppermute | solution.py:416
  10.3 6.1 %collective-permute-start.25 = (bf16[560,128]{1,0:T(8,128)(2,1)S(1)}, bf16[560,128]{1,0:T(8,128)(2,1)S(1)}, u32[]{:S(2)}, u32[]{:S(2)}) collective-permute-start(bf16[560,128]{1,0:T(8,128)(2,1)S(1)} %get-tuple-element.24.refs_0_), channel_id=1, source_target_pairs={{0,2},{1,3},{2,0},{3,1},{4,6},{5,7},{6,4},{7,5},{8,10},{9,11},{10,... | collective-permute-start | bytes 430088 | tf_op jit(solution)/shard_map/ppermute | solution.py:416
  10.9 6.0 %collective-permute-start.24 = (bf16[560,128]{1,0:T(8,128)(2,1)S(1)}, bf16[560,128]{1,0:T(8,128)(2,1)S(1)}, u32[]{:S(2)}, u32[]{:S(2)}) collective-permute-start(bf16[560,128]{1,0:T(8,128)(2,1)S(1)} %get-tuple-element.24.refs_0_), channel_id=1, source_target_pairs={{0,1},{1,0},{2,3},{3,2},{4,5},{5,4},{6,7},{7,6},{8,9},{9,8},{10,11... | collective-permute-start | bytes 430088 | tf_op jit(solution)/shard_map/ppermute | solution.py:416
  10.9 22.1 %collective-permute-start.8 = (bf16[560,128]{1,0:T(8,128)(2,1)S(1)}, bf16[560,128]{1,0:T(8,128)(2,1)S(1)}, u32[]{:S(2)}, u32[]{:S(2)}) collective-permute-start(bf16[560,128]{1,0:T(8,128)(2,1)S(1)} %get-tuple-element.24.refs_0_), channel_id=1, source_target_pairs={{0,8},{1,9},{2,10},{3,11},{4,12},{5,13},{6,14},{7,15},{8,0},{9,1},... | collective-permute-start | bytes 430088 | tf_op jit(solution)/shard_map/ppermute | solution.py:416
  14.4 47.4 %collective-permute-start = (bf16[560,128]{1,0:T(8,128)(2,1)S(1)}, bf16[560,128]{1,0:T(8,128)(2,1)S(1)}, u32[]{:S(2)}, u32[]{:S(2)}) collective-permute-start(bf16[560,128]{1,0:T(8,128)(2,1)S(1)} %get-tuple-element.24.refs_0_), channel_id=1, source_target_pairs={{0,4},{1,5},{2,6},{3,7},{4,0},{5,1},{6,2},{7,3},{8,12},{9,13},{10,... | collective-permute-start | bytes 430088 | tf_op jit(solution)/shard_map/ppermute | solution.py:416
  15.3 23.0 %collective-permute-start.19 = (bf16[560,128]{1,0:T(8,128)(2,1)S(1)}, bf16[560,128]{1,0:T(8,128)(2,1)S(1)}, u32[]{:S(2)}, u32[]{:S(2)}) collective-permute-start(bf16[560,128]{1,0:T(8,128)(2,1)S(1)} %collective-permute-done.16.refs_0_), channel_id=1, source_target_pairs={{0,3},{1,2},{2,1},{3,0},{4,7},{5,6},{6,5},{7,4},{8,11},{9,10},{10,... | collective-permute-start | bytes 430088 | tf_op jit(solution)/shard_map/ppermute | solution.py:416
  16.4 30.1 %collective-permute-start.18 = (bf16[560,128]{1,0:T(8,128)(2,1)S(1)}, bf16[560,128]{1,0:T(8,128)(2,1)S(1)}, u32[]{:S(2)}, u32[]{:S(2)}) collective-permute-start(bf16[560,128]{1,0:T(8,128)(2,1)S(1)} %collective-permute-done.16.refs_0_), channel_id=1, source_target_pairs={{0,2},{1,3},{2,0},{3,1},{4,6},{5,7},{6,4},{7,5},{8,10},{9,11},{10,... | collective-permute-start | bytes 430088 | tf_op jit(solution)/shard_map/ppermute | solution.py:416
  16.9 30.0 %collective-permute-start.17 = (bf16[560,128]{1,0:T(8,128)(2,1)S(1)}, bf16[560,128]{1,0:T(8,128)(2,1)S(1)}, u32[]{:S(2)}, u32[]{:S(2)}) collective-permute-start(bf16[560,128]{1,0:T(8,128)(2,1)S(1)} %collective-permute-done.16.refs_0_), channel_id=1, source_target_pairs={{0,1},{1,0},{2,3},{3,2},{4,5},{5,4},{6,7},{7,6},{8,9},{9,8},{10,11... | collective-permute-start | bytes 430088 | tf_op jit(solution)/shard_map/ppermute | solution.py:416
  33.0 85.1 %collective-permute-start.27 = (bf16[96,1024]{1,0:T(8,128)(2,1)S(1)}, bf16[96,1024]{1,0:T(8,128)(2,1)S(1)}, u32[]{:S(2)}, u32[]{:S(2)}) collective-permute-start(bf16[96,1024]{1,0:T(8,128)(2,1)S(1)} %get-tuple-element.38), channel_id=1, source_target_pairs={{0,1},{1,0},{2,3},{3,2},{4,5},{5,4},{6,7},{7,6},{8,9},{9,8},{10,11... | collective-permute-start | bytes 589832 | tf_op jit(solution)/shard_map/ppermute | solution.py:416
  38.3 30.3 %collective-permute-start.11 = (bf16[560,128]{1,0:T(8,128)(2,1)S(1)}, bf16[560,128]{1,0:T(8,128)(2,1)S(1)}, u32[]{:S(2)}, u32[]{:S(2)}) collective-permute-start(bf16[560,128]{1,0:T(8,128)(2,1)S(1)} %collective-permute-done.8.refs_0_), channel_id=1, source_target_pairs={{0,3},{1,2},{2,1},{3,0},{4,7},{5,6},{6,5},{7,4},{8,11},{9,10},{10,... | collective-permute-start | bytes 430088 | tf_op jit(solution)/shard_map/ppermute | solution.py:416
  46.5 30.2 %collective-permute-start.10 = (bf16[560,128]{1,0:T(8,128)(2,1)S(1)}, bf16[560,128]{1,0:T(8,128)(2,1)S(1)}, u32[]{:S(2)}, u32[]{:S(2)}) collective-permute-start(bf16[560,128]{1,0:T(8,128)(2,1)S(1)} %collective-permute-done.8.refs_0_), channel_id=1, source_target_pairs={{0,2},{1,3},{2,0},{3,1},{4,6},{5,7},{6,4},{7,5},{8,10},{9,11},{10,... | collective-permute-start | bytes 430088 | tf_op jit(solution)/shard_map/ppermute | solution.py:416
  46.9 29.8 %collective-permute-start.9 = (bf16[560,128]{1,0:T(8,128)(2,1)S(1)}, bf16[560,128]{1,0:T(8,128)(2,1)S(1)}, u32[]{:S(2)}, u32[]{:S(2)}) collective-permute-start(bf16[560,128]{1,0:T(8,128)(2,1)S(1)} %collective-permute-done.8.refs_0_), channel_id=1, source_target_pairs={{0,1},{1,0},{2,3},{3,2},{4,5},{5,4},{6,7},{7,6},{8,9},{9,8},{10,11... | collective-permute-start | bytes 430088 | tf_op jit(solution)/shard_map/ppermute | solution.py:416
  61.9 64.4 %collective-permute-start.28 = (bf16[96,1024]{1,0:T(8,128)(2,1)S(1)}, bf16[96,1024]{1,0:T(8,128)(2,1)S(1)}, u32[]{:S(2)}, u32[]{:S(2)}) collective-permute-start(bf16[96,1024]{1,0:T(8,128)(2,1)S(1)} %get-tuple-element.39), channel_id=1, source_target_pairs={{0,2},{1,3},{2,0},{3,1},{4,6},{5,7},{6,4},{7,5},{8,10},{9,11},{10,... | collective-permute-start | bytes 589832 | tf_op jit(solution)/shard_map/ppermute | solution.py:416
  68.6 24.6 %collective-permute-start.5 = (bf16[560,128]{1,0:T(8,128)(2,1)S(1)}, bf16[560,128]{1,0:T(8,128)(2,1)S(1)}, u32[]{:S(2)}, u32[]{:S(2)}) collective-permute-start(bf16[560,128]{1,0:T(8,128)(2,1)S(1)} %collective-permute-done.refs_0_), channel_id=1, source_target_pairs={{0,1},{1,0},{2,3},{3,2},{4,5},{5,4},{6,7},{7,6},{8,9},{9,8},{10,11... | collective-permute-start | bytes 430088 | tf_op jit(solution)/shard_map/ppermute | solution.py:416
  76.7 29.8 %collective-permute-start.2 = (bf16[560,128]{1,0:T(8,128)(2,1)S(1)}, bf16[560,128]{1,0:T(8,128)(2,1)S(1)}, u32[]{:S(2)}, u32[]{:S(2)}) collective-permute-start(bf16[560,128]{1,0:T(8,128)(2,1)S(1)} %collective-permute-done.refs_0_), channel_id=1, source_target_pairs={{0,3},{1,2},{2,1},{3,0},{4,7},{5,6},{6,5},{7,4},{8,11},{9,10},{10,... | collective-permute-start | bytes 430088 | tf_op jit(solution)/shard_map/ppermute | solution.py:416
  76.7 33.1 %collective-permute-start.1 = (bf16[560,128]{1,0:T(8,128)(2,1)S(1)}, bf16[560,128]{1,0:T(8,128)(2,1)S(1)}, u32[]{:S(2)}, u32[]{:S(2)}) collective-permute-start(bf16[560,128]{1,0:T(8,128)(2,1)S(1)} %collective-permute-done.refs_0_), channel_id=1, source_target_pairs={{0,2},{1,3},{2,0},{3,1},{4,6},{5,7},{6,4},{7,5},{8,10},{9,11},{10,... | collective-permute-start | bytes 430088 | tf_op jit(solution)/shard_map/ppermute | solution.py:416
  93.2 33.0 %collective-permute-start.29 = (bf16[96,1024]{1,0:T(8,128)(2,1)S(1)}, bf16[96,1024]{1,0:T(8,128)(2,1)S(1)}, u32[]{:S(2)}, u32[]{:S(2)}) collective-permute-start(bf16[96,1024]{1,0:T(8,128)(2,1)S(1)} %get-tuple-element.40), channel_id=1, source_target_pairs={{0,3},{1,2},{2,1},{3,0},{4,7},{5,6},{6,5},{7,4},{8,11},{9,10},{10,... | collective-permute-start | bytes 589832 | tf_op jit(solution)/shard_map/ppermute | solution.py:416
  106.4 23.8 %collective-permute-start.20 = (bf16[96,1024]{1,0:T(8,128)(2,1)S(1)}, bf16[96,1024]{1,0:T(8,128)(2,1)S(1)}, u32[]{:S(2)}, u32[]{:S(2)}) collective-permute-start(bf16[96,1024]{1,0:T(8,128)(2,1)S(1)} %get-tuple-element.33), channel_id=1, source_target_pairs={{0,12},{1,13},{2,14},{3,15},{4,8},{5,9},{6,10},{7,11},{8,4},{9,5},... | collective-permute-start | bytes 589832 | tf_op jit(solution)/shard_map/ppermute | solution.py:416
  109.9 20.3 %collective-permute-start.21 = (bf16[96,1024]{1,0:T(8,128)(2,1)S(1)}, bf16[96,1024]{1,0:T(8,128)(2,1)S(1)}, u32[]{:S(2)}, u32[]{:S(2)}) collective-permute-start(bf16[96,1024]{1,0:T(8,128)(2,1)S(1)} %get-tuple-element.34), channel_id=1, source_target_pairs={{0,13},{1,12},{2,15},{3,14},{4,9},{5,8},{6,11},{7,10},{8,5},{9,4},... | collective-permute-start | bytes 589832 | tf_op jit(solution)/shard_map/ppermute | solution.py:416
  118.1 39.0 %collective-permute-start.22 = (bf16[96,1024]{1,0:T(8,128)(2,1)S(1)}, bf16[96,1024]{1,0:T(8,128)(2,1)S(1)}, u32[]{:S(2)}, u32[]{:S(2)}) collective-permute-start(bf16[96,1024]{1,0:T(8,128)(2,1)S(1)} %get-tuple-element.35), channel_id=1, source_target_pairs={{0,14},{1,15},{2,12},{3,13},{4,10},{5,11},{6,8},{7,9},{8,6},{9,7},... | collective-permute-start | bytes 589832 | tf_op jit(solution)/shard_map/ppermute | solution.py:416
  126.2 31.0 %collective-permute-start.23 = (bf16[96,1024]{1,0:T(8,128)(2,1)S(1)}, bf16[96,1024]{1,0:T(8,128)(2,1)S(1)}, u32[]{:S(2)}, u32[]{:S(2)}) collective-permute-start(bf16[96,1024]{1,0:T(8,128)(2,1)S(1)} %get-tuple-element.36), channel_id=1, source_target_pairs={{0,15},{1,14},{2,13},{3,12},{4,11},{5,10},{6,9},{7,8},{8,7},{9,6},... | collective-permute-start | bytes 589832 | tf_op jit(solution)/shard_map/ppermute | solution.py:416
  126.2 34.2 %collective-permute-start.12 = (bf16[96,1024]{1,0:T(8,128)(2,1)S(1)}, bf16[96,1024]{1,0:T(8,128)(2,1)S(1)}, u32[]{:S(2)}, u32[]{:S(2)}) collective-permute-start(bf16[96,1024]{1,0:T(8,128)(2,1)S(1)} %get-tuple-element.29), channel_id=1, source_target_pairs={{0,8},{1,9},{2,10},{3,11},{4,12},{5,13},{6,14},{7,15},{8,0},{9,1},... | collective-permute-start | bytes 589832 | tf_op jit(solution)/shard_map/ppermute | solution.py:416
  130.2 34.3 %collective-permute-start.13 = (bf16[96,1024]{1,0:T(8,128)(2,1)S(1)}, bf16[96,1024]{1,0:T(8,128)(2,1)S(1)}, u32[]{:S(2)}, u32[]{:S(2)}) collective-permute-start(bf16[96,1024]{1,0:T(8,128)(2,1)S(1)} %get-tuple-element.30), channel_id=1, source_target_pairs={{0,9},{1,8},{2,11},{3,10},{4,13},{5,12},{6,15},{7,14},{8,1},{9,0},... | collective-permute-start | bytes 589832 | tf_op jit(solution)/shard_map/ppermute | solution.py:416
  130.2 37.3 %collective-permute-start.14 = (bf16[96,1024]{1,0:T(8,128)(2,1)S(1)}, bf16[96,1024]{1,0:T(8,128)(2,1)S(1)}, u32[]{:S(2)}, u32[]{:S(2)}) collective-permute-start(bf16[96,1024]{1,0:T(8,128)(2,1)S(1)} %get-tuple-element.31), channel_id=1, source_target_pairs={{0,10},{1,11},{2,8},{3,9},{4,14},{5,15},{6,12},{7,13},{8,2},{9,3},... | collective-permute-start | bytes 589832 | tf_op jit(solution)/shard_map/ppermute | solution.py:416
  157.1 26.3 %collective-permute-start.3 = (bf16[96,1024]{1,0:T(8,128)(2,1)S(1)}, bf16[96,1024]{1,0:T(8,128)(2,1)S(1)}, u32[]{:S(2)}, u32[]{:S(2)}) collective-permute-start(bf16[96,1024]{1,0:T(8,128)(2,1)S(1)} %get-tuple-element.25), channel_id=1, source_target_pairs={{0,6},{1,7},{2,4},{3,5},{4,2},{5,3},{6,0},{7,1},{8,14},{9,15},{10,... | collective-permute-start | bytes 589832 | tf_op jit(solution)/shard_map/ppermute | solution.py:416
  157.2 24.0 %collective-permute-start.6 = (bf16[96,1024]{1,0:T(8,128)(2,1)S(1)}, bf16[96,1024]{1,0:T(8,128)(2,1)S(1)}, u32[]{:S(2)}, u32[]{:S(2)}) collective-permute-start(bf16[96,1024]{1,0:T(8,128)(2,1)S(1)} %get-tuple-element.27), channel_id=1, source_target_pairs={{0,4},{1,5},{2,6},{3,7},{4,0},{5,1},{6,2},{7,3},{8,12},{9,13},{10,... | collective-permute-start | bytes 589832 | tf_op jit(solution)/shard_map/ppermute | solution.py:416
  160.4 18.1 %collective-permute-start.15 = (bf16[96,1024]{1,0:T(8,128)(2,1)S(1)}, bf16[96,1024]{1,0:T(8,128)(2,1)S(1)}, u32[]{:S(2)}, u32[]{:S(2)}) collective-permute-start(bf16[96,1024]{1,0:T(8,128)(2,1)S(1)} %get-tuple-element.32), channel_id=1, source_target_pairs={{0,11},{1,10},{2,9},{3,8},{4,15},{5,14},{6,13},{7,12},{8,3},{9,2},... | collective-permute-start | bytes 589832 | tf_op jit(solution)/shard_map/ppermute | solution.py:416
  164.5 17.0 %collective-permute-start.7 = (bf16[96,1024]{1,0:T(8,128)(2,1)S(1)}, bf16[96,1024]{1,0:T(8,128)(2,1)S(1)}, u32[]{:S(2)}, u32[]{:S(2)}) collective-permute-start(bf16[96,1024]{1,0:T(8,128)(2,1)S(1)} %get-tuple-element.28), channel_id=1, source_target_pairs={{0,5},{1,4},{2,7},{3,6},{4,1},{5,0},{6,3},{7,2},{8,13},{9,12},{10,... | collective-permute-start | bytes 589832 | tf_op jit(solution)/shard_map/ppermute | solution.py:416
  167.5 21.7 %collective-permute-start.4 = (bf16[96,1024]{1,0:T(8,128)(2,1)S(1)}, bf16[96,1024]{1,0:T(8,128)(2,1)S(1)}, u32[]{:S(2)}, u32[]{:S(2)}) collective-permute-start(bf16[96,1024]{1,0:T(8,128)(2,1)S(1)} %get-tuple-element.26), channel_id=1, source_target_pairs={{0,7},{1,6},{2,5},{3,4},{4,3},{5,2},{6,1},{7,0},{8,15},{9,14},{10,... | collective-permute-start | bytes 589832 | tf_op jit(solution)/shard_map/ppermute | solution.py:416

commit v4 on v0

--- a/solution.py
+++ b/solution.py
@@ -208,28 +208,39 @@
             entry(slot)[0], pl.ds(pl.multiple_of(query * blocks, blocks), blocks), :
         ].astype(jnp.float32)
         zero = jnp.zeros((8, LANES), jnp.float32)
-        before = (zero, zero)
+        columns = slice(half * LANES, (half + 1) * LANES)
+
+        def joined(top, bottom):
+            return jnp.concatenate([top, bottom], axis=0).astype(jnp.bfloat16)
+
+        before = last = zero
         before_shifted = jnp.zeros((16, LANES), jnp.bfloat16)
-        columns = slice(half * LANES, (half + 1) * LANES)
-        for b in range(blocks + 1):
-            if b < blocks:
-                wide = jnp.broadcast_to(spectrum_ref[half, pl.ds(b, 1), :], (8, LANES))
-                now = tuple(
-                    pltpu.roll(wide, 1 + 8 * h, 1, stride=1, stride_axis=0) for h in range(2)
-                )
-            else:
-                now = (zero, zero)
-            shifted = jnp.concatenate(
-                [jnp.where(lane > row + 8 * h, now[h], before[h]) for h in range(2)], axis=0
-            ).astype(jnp.bfloat16)
-            j = blocks - 1 - b
-            place = 0 if j < 0 else (j % tiles + 1) * LANES + j // tiles * WIDTH
-            right_ref[pl.ds(place, 16), columns] = shifted
-            for c in range(16, WIDTH, 16):
-                right_ref[pl.ds(place + c, 16), columns] = pltpu.roll(
-                    jnp.where(lane16 < LANES - c, shifted, before_shifted), c, 1
-                )
-            before, before_shifted = now, shifted
+        for first_b in range(0, blocks + 2, 2):
+            low = []
+            for b in (first_b, first_b + 1):
+                if b < blocks:
+                    wide = jnp.broadcast_to(spectrum_ref[half, pl.ds(b, 1), :], (8, LANES))
+                    now = pltpu.roll(wide, 1, 1, stride=1, stride_axis=0)
+                else:
+                    now = zero
+                low.append(jnp.where(lane > row, now, before))
+                before = now
+            more = pltpu.roll(
+                jnp.where(lane16 < LANES - 8, joined(low[0], low[1]), joined(last, low[0])), 8, 1
+            ).astype(jnp.float32)
+            last = low[1]
+            for side, b in enumerate((first_b, first_b + 1)):
+                if b > blocks:
+                    continue
+                shifted = joined(low[side], more[8 * side : 8 * side + 8])
+                j = blocks - 1 - b
+                place = 0 if j < 0 else (j % tiles + 1) * LANES + j // tiles * WIDTH
+                right_ref[pl.ds(place, 16), columns] = shifted
+                for c in range(16, WIDTH, 16):
+                    right_ref[pl.ds(place + c, 16), columns] = pltpu.roll(
+                        jnp.where(lane16 < LANES - c, shifted, before_shifted), c, 1
+                    )
+                before_shifted = shifted
 
     def sums(low, high):
         left = jnp.concatenate(

time: 180 us -> 183 us (1.017)
  Pallas kernels: 68.4 us -> 83.9 us
  starting transfers between devices: 84.7 us -> 73.4 us
    pallas_call x4, Pallas kernels: 56.3 us -> 71.8 us  [profile(): pl.pallas_call(functools.partial(profile_kernel, depth, num_query, touche...]
    ppermute x30, starting transfers between devices: 84.7 us -> 73.4 us  [across(): return lax.ppermute(value, 'lib', pairs)]
  transfers between devices with their start and end apart: 30 -> 30, of which waited for: 6 -> 6; matrix products, arithmetic and copies ran while one was open for 2% -> 2% of each run, Pallas kernels for 36% -> 43%
where the time goes in v4:
time: 183 us
  Pallas kernels  83.9 us (46%)
  starting transfers between devices  73.4 us (40%)
  waiting for transfers between devices  19.8 us (11%)
  local copies, waits for them, and re-layouts  5.95 us (3%)
    ppermute x30, starting transfers between devices, across(): return lax.ppermute(value, 'lib', pairs)  73.4 us
    pallas_call x4, Pallas kernels, profile(): pl.pallas_call(functools.partial(profile_kernel, depth, num_query, touche...  71.8 us
    ppermute x30, waiting for transfers between devices, across(): return lax.ppermute(value, 'lib', pairs)  19.8 us
    pallas_call x4, Pallas kernels, unpack(): pl.pallas_call(functools.partial(unpack_kernel, part, depth), out_shape=j...  10.4 us
    unnamed x5, local copies, waits for them, and re-layouts  5.95 us
  transfers between devices with their start and end apart: 30, of which 6 were waited for; matrix products, arithmetic and copies ran while one was open for 2% of the time, Pallas kernels for 43%

profile of v4, /device:TPU:0, one launch (start us, length us, event | category | flops | bytes accessed | tf_op | source)
XLA Modules:
  0.0 183.2 jit_solution(10667741538058390046)
XLA Ops:
  0.0 0.8 copy.9.named_ref
  0.8 0.8 copy.8
  1.6 0.9 copy-done
  2.5 1.7 prepare.1
  4.2 2.5 %collective-permute-start.26 = (bf16[560,128]{1,0:T(8,128)(2,1)S(1)}, bf16[560,128]{1,0:T(8,128)(2,1)S(1)}, u32[]{:S(2)}, u32[]{:S(2)}) collective-permute-start(bf16[560,128]{1,0:T(8,128)(2,1)S(1)} %get-tuple-element.24.refs_0_), channel_id=1, source_target_pairs={{0,3},{1,2},{2,1},{3,0},{4,7},{5,6},{6,5},{7,4},{8,11},{9,10},{10,... | collective-permute-start | bytes 430088 | tf_op jit(solution)/shard_map/ppermute | solution.py:425
  6.7 3.6 %collective-permute-start.16 = (bf16[560,128]{1,0:T(8,128)(2,1)S(1)}, bf16[560,128]{1,0:T(8,128)(2,1)S(1)}, u32[]{:S(2)}, u32[]{:S(2)}) collective-permute-start(bf16[560,128]{1,0:T(8,128)(2,1)S(1)} %get-tuple-element.24.refs_0_), channel_id=1, source_target_pairs={{0,12},{1,13},{2,14},{3,15},{4,8},{5,9},{6,10},{7,11},{8,4},{9,5},... | collective-permute-start | bytes 430088 | tf_op jit(solution)/shard_map/ppermute | solution.py:425
  10.9 3.5 %copy.10 = bf16[64,8,32,128]{3,2,1,0:T(8,128)(2,1)S(1)} copy(bf16[64,8,32,128]{3,1,2,0:T(8,128)(2,1)} %bitcast.10) | data formatting | bytes 8388608
  14.4 0.9 collective-permute-start
  15.3 0.9 collective-permute-start.19
  17.2 6.2 %collective-permute-done.8.refs_0_ = bf16[560,128]{1,0:T(8,128)(2,1)S(1)} collective-permute-done((bf16[560,128]{1,0:T(8,128)(2,1)S(1)}, bf16[560,128]{1,0:T(8,128)(2,1)S(1)}, u32[]{:S(2)}, u32[]{:S(2)}) %collective-permute-start.8) | collective-permute-done | bytes 143392 | tf_op jit(solution)/shard_map/ppermute | solution.py:425
  23.4 22.3 %profile_0.1 = (bf16[96,1024]{1,0:T(8,128)(2,1)S(1)}, bf16[96,1024]{1,0:T(8,128)(2,1)S(1)}, bf16[96,1024]{1,0:T(8,128)(2,1)S(1)}, bf16[96,1024]{1,0:T(8,128)(2,1)S(1)}) custom-call(s32[1]{0:T(128)} %bitcast.me_ref, bf16[560,128]{1,0:T(8,128)(2,1)S(1)} %get-tuple-element.24.refs_0_, bf16[560,128]{1,0:T(8,128)(2,1)S(1)} %collective-permute-done.24.refs_1_, ...), custom_call_target="tpu_custom_call" | custom-call | flops 32614907904 | bytes 8388608 | tf_op jit(solution)/shard_map/profile_0/pallas_call | solution.py:324
  45.7 7.6 %collective-permute-start.10 = (bf16[560,128]{1,0:T(8,128)(2,1)S(1)}, bf16[560,128]{1,0:T(8,128)(2,1)S(1)}, u32[]{:S(2)}, u32[]{:S(2)}) collective-permute-start(bf16[560,128]{1,0:T(8,128)(2,1)S(1)} %collective-permute-done.8.refs_0_), channel_id=1, source_target_pairs={{0,2},{1,3},{2,0},{3,1},{4,6},{5,7},{6,4},{7,5},{8,10},{9,11},{10,... | collective-permute-start | bytes 430088 | tf_op jit(solution)/shard_map/ppermute | solution.py:425
  53.3 0.6 collective-permute-start.3
  54.0 1.5 collective-permute-start.2
  55.5 17.2 %profile_3.1 = (bf16[96,1024]{1,0:T(8,128)(2,1)S(1)}, bf16[96,1024]{1,0:T(8,128)(2,1)S(1)}, bf16[96,1024]{1,0:T(8,128)(2,1)S(1)}, bf16[96,1024]{1,0:T(8,128)(2,1)S(1)}) custom-call(s32[1]{0:T(128)} %bitcast.me_ref, bf16[560,128]{1,0:T(8,128)(2,1)S(1)} %collective-permute-done.16.refs_0_, bf16[560,128]{1,0:T(8,128)(2,1)S(1)} %collective-permute-done.17.refs_1_, ...), custom_call_target="tpu_custom_call" | custom-call | flops 32614907904 | bytes 8388608 | tf_op jit(solution)/shard_map/profile_3/pallas_call | solution.py:324
  72.7 11.8 %collective-permute-start.27 = (bf16[96,1024]{1,0:T(8,128)(2,1)S(1)}, bf16[96,1024]{1,0:T(8,128)(2,1)S(1)}, u32[]{:S(2)}, u32[]{:S(2)}) collective-permute-start(bf16[96,1024]{1,0:T(8,128)(2,1)S(1)} %get-tuple-element.38), channel_id=1, source_target_pairs={{0,1},{1,0},{2,3},{3,2},{4,5},{5,4},{6,7},{7,6},{8,9},{9,8},{10,11... | collective-permute-start | bytes 589832 | tf_op jit(solution)/shard_map/ppermute | solution.py:425
  84.5 1.4 collective-permute-start.29
  86.4 3.4 %collective-permute-start.21 = (bf16[96,1024]{1,0:T(8,128)(2,1)S(1)}, bf16[96,1024]{1,0:T(8,128)(2,1)S(1)}, u32[]{:S(2)}, u32[]{:S(2)}) collective-permute-start(bf16[96,1024]{1,0:T(8,128)(2,1)S(1)} %get-tuple-element.34), channel_id=1, source_target_pairs={{0,13},{1,12},{2,15},{3,14},{4,9},{5,8},{6,11},{7,10},{8,5},{9,4},... | collective-permute-start | bytes 589832 | tf_op jit(solution)/shard_map/ppermute | solution.py:425
  89.8 17.2 %profile_2.1 = (bf16[96,1024]{1,0:T(8,128)(2,1)S(1)}, bf16[96,1024]{1,0:T(8,128)(2,1)S(1)}, bf16[96,1024]{1,0:T(8,128)(2,1)S(1)}, bf16[96,1024]{1,0:T(8,128)(2,1)S(1)}) custom-call(s32[1]{0:T(128)} %bitcast.me_ref, bf16[560,128]{1,0:T(8,128)(2,1)S(1)} %collective-permute-done.8.refs_0_, bf16[560,128]{1,0:T(8,128)(2,1)S(1)} %collective-permute-done.9.refs_1_, ...), custom_call_target="tpu_custom_call" | custom-call | flops 32614907904 | bytes 8388608 | tf_op jit(solution)/shard_map/profile_2/pallas_call | solution.py:324
  107.1 15.4 %collective-permute-start.23 = (bf16[96,1024]{1,0:T(8,128)(2,1)S(1)}, bf16[96,1024]{1,0:T(8,128)(2,1)S(1)}, u32[]{:S(2)}, u32[]{:S(2)}) collective-permute-start(bf16[96,1024]{1,0:T(8,128)(2,1)S(1)} %get-tuple-element.36), channel_id=1, source_target_pairs={{0,15},{1,14},{2,13},{3,12},{4,11},{5,10},{6,9},{7,8},{8,7},{9,6},... | collective-permute-start | bytes 589832 | tf_op jit(solution)/shard_map/ppermute | solution.py:425
  122.6 0.7 collective-permute-start.14
  123.2 15.1 %profile_1.1 = (bf16[96,1024]{1,0:T(8,128)(2,1)S(1)}, bf16[96,1024]{1,0:T(8,128)(2,1)S(1)}, bf16[96,1024]{1,0:T(8,128)(2,1)S(1)}, bf16[96,1024]{1,0:T(8,128)(2,1)S(1)}) custom-call(s32[1]{0:T(128)} %bitcast.me_ref, bf16[560,128]{1,0:T(8,128)(2,1)S(1)} %collective-permute-done.refs_0_, bf16[560,128]{1,0:T(8,128)(2,1)S(1)} %collective-permute-done.1.refs_1_, ...), custom_call_target="tpu_custom_call" | custom-call | flops 32614907904 | bytes 8388608 | tf_op jit(solution)/shard_map/profile_1/pallas_call | solution.py:324
  138.4 18.8 %collective-permute-start.15 = (bf16[96,1024]{1,0:T(8,128)(2,1)S(1)}, bf16[96,1024]{1,0:T(8,128)(2,1)S(1)}, u32[]{:S(2)}, u32[]{:S(2)}) collective-permute-start(bf16[96,1024]{1,0:T(8,128)(2,1)S(1)} %get-tuple-element.32), channel_id=1, source_target_pairs={{0,11},{1,10},{2,9},{3,8},{4,15},{5,14},{6,13},{7,12},{8,3},{9,2},... | collective-permute-start | bytes 589832 | tf_op jit(solution)/shard_map/ppermute | solution.py:425
  157.4 2.2 %collective-permute-done.14.refs_2_ = bf16[96,1024]{1,0:T(8,128)(2,1)S(1)} collective-permute-done((bf16[96,1024]{1,0:T(8,128)(2,1)S(1)}, bf16[96,1024]{1,0:T(8,128)(2,1)S(1)}, u32[]{:S(2)}, u32[]{:S(2)}) %collective-permute-start.14) | collective-permute-done | bytes 196640 | tf_op jit(solution)/shard_map/ppermute | solution.py:425
  159.6 2.0 %collective-permute-start.7 = (bf16[96,1024]{1,0:T(8,128)(2,1)S(1)}, bf16[96,1024]{1,0:T(8,128)(2,1)S(1)}, u32[]{:S(2)}, u32[]{:S(2)}) collective-permute-start(bf16[96,1024]{1,0:T(8,128)(2,1)S(1)} %get-tuple-element.28), channel_id=1, source_target_pairs={{0,7},{1,6},{2,5},{3,4},{4,3},{5,2},{6,1},{7,0},{8,15},{9,14},{10,... | collective-permute-start | bytes 589832 | tf_op jit(solution)/shard_map/ppermute | solution.py:425
  161.6 2.5 %unpack_0.1.refs_4_ = f32[128,8,1024]{2,1,0:T(8,128)} custom-call(s32[1]{0:T(128)} %bitcast.me_ref, s32[48,128]{1,0:T(8,128)S(1)} %get-tuple-element.23.table_ref, bf16[96,1024]{1,0:T(8,128)(2,1)S(1)} %get-tuple-element.37.refs_0_, bf16[96,1024]{1,0:T(8,128)(2,1)S(1)} %collective-permute-done.27.refs_1_, ...), custom_call_target="tpu_custom_call" | custom-call | bytes 2359296 | tf_op jit(solution)/shard_map/unpack_0/pallas_call | solution.py:394
  164.2 2.6 %unpack_3.1.refs_4_ = f32[128,8,1024]{2,1,0:T(8,128)} custom-call(s32[1]{0:T(128)} %bitcast.me_ref, s32[48,128]{1,0:T(8,128)S(1)} %get-tuple-element.23.table_ref, bf16[96,1024]{1,0:T(8,128)(2,1)S(1)} %collective-permute-done.20.refs_0_, bf16[96,1024]{1,0:T(8,128)(2,1)S(1)} %collective-permute-done.21.refs_1_, ...), custom_call_target="tpu_custom_call", output_to_operand_aliasing={{}: (6, {})} | custom-call | bytes 2359296 | tf_op jit(solution)/shard_map/unpack_3/pallas_call | solution.py:394
  166.8 2.7 %unpack_2.1.refs_4_ = f32[128,8,1024]{2,1,0:T(8,128)} custom-call(s32[1]{0:T(128)} %bitcast.me_ref, s32[48,128]{1,0:T(8,128)S(1)} %get-tuple-element.23.table_ref, bf16[96,1024]{1,0:T(8,128)(2,1)S(1)} %collective-permute-done.12.refs_0_, bf16[96,1024]{1,0:T(8,128)(2,1)S(1)} %collective-permute-done.13.refs_1_, ...), custom_call_target="tpu_custom_call", output_to_operand_aliasing={{}: (6, {})} | custom-call | bytes 2359296 | tf_op jit(solution)/shard_map/unpack_2/pallas_call | solution.py:394
  169.5 0.8 collective-permute-done.5.refs_1_
  170.3 6.1 %collective-permute-done.6.refs_2_ = bf16[96,1024]{1,0:T(8,128)(2,1)S(1)} collective-permute-done((bf16[96,1024]{1,0:T(8,128)(2,1)S(1)}, bf16[96,1024]{1,0:T(8,128)(2,1)S(1)}, u32[]{:S(2)}, u32[]{:S(2)}) %collective-permute-start.6) | collective-permute-done | bytes 196640 | tf_op jit(solution)/shard_map/ppermute | solution.py:425
  176.4 4.2 %collective-permute-done.7.refs_3_ = bf16[96,1024]{1,0:T(8,128)(2,1)S(1)} collective-permute-done((bf16[96,1024]{1,0:T(8,128)(2,1)S(1)}, bf16[96,1024]{1,0:T(8,128)(2,1)S(1)}, u32[]{:S(2)}, u32[]{:S(2)}) %collective-permute-start.7) | collective-permute-done | bytes 196640 | tf_op jit(solution)/shard_map/ppermute | solution.py:425
  180.6 2.6 %unpack_1.1 = f32[128,8,1024]{2,1,0:T(8,128)} custom-call(s32[1]{0:T(128)} %bitcast.me_ref, s32[48,128]{1,0:T(8,128)S(1)} %get-tuple-element.23.table_ref, bf16[96,1024]{1,0:T(8,128)(2,1)S(1)} %collective-permute-done.4.refs_0_, bf16[96,1024]{1,0:T(8,128)(2,1)S(1)} %collective-permute-done.5.refs_1_, ...), custom_call_target="tpu_custom_call", output_to_operand_aliasing={{}: (6, {})} | custom-call | bytes 2359296 | tf_op jit(solution)/shard_map/unpack_1/pallas_call | solution.py:394
  (42 shorter events, 2.4 us)
Async XLA Ops:
  1.6 0.9 copy-start
  4.2 10.2 %collective-permute-start.26 = (bf16[560,128]{1,0:T(8,128)(2,1)S(1)}, bf16[560,128]{1,0:T(8,128)(2,1)S(1)}, u32[]{:S(2)}, u32[]{:S(2)}) collective-permute-start(bf16[560,128]{1,0:T(8,128)(2,1)S(1)} %get-tuple-element.24.refs_0_), channel_id=1, source_target_pairs={{0,3},{1,2},{2,1},{3,0},{4,7},{5,6},{6,5},{7,4},{8,11},{9,10},{10,... | collective-permute-start | bytes 430088 | tf_op jit(solution)/shard_map/ppermute | solution.py:425
  6.7 8.6 %collective-permute-start.16 = (bf16[560,128]{1,0:T(8,128)(2,1)S(1)}, bf16[560,128]{1,0:T(8,128)(2,1)S(1)}, u32[]{:S(2)}, u32[]{:S(2)}) collective-permute-start(bf16[560,128]{1,0:T(8,128)(2,1)S(1)} %get-tuple-element.24.refs_0_), channel_id=1, source_target_pairs={{0,12},{1,13},{2,14},{3,15},{4,8},{5,9},{6,10},{7,11},{8,4},{9,5},... | collective-permute-start | bytes 430088 | tf_op jit(solution)/shard_map/ppermute | solution.py:425
  10.3 6.1 %collective-permute-start.25 = (bf16[560,128]{1,0:T(8,128)(2,1)S(1)}, bf16[560,128]{1,0:T(8,128)(2,1)S(1)}, u32[]{:S(2)}, u32[]{:S(2)}) collective-permute-start(bf16[560,128]{1,0:T(8,128)(2,1)S(1)} %get-tuple-element.24.refs_0_), channel_id=1, source_target_pairs={{0,2},{1,3},{2,0},{3,1},{4,6},{5,7},{6,4},{7,5},{8,10},{9,11},{10,... | collective-permute-start | bytes 430088 | tf_op jit(solution)/shard_map/ppermute | solution.py:425
  10.9 6.0 %collective-permute-start.24 = (bf16[560,128]{1,0:T(8,128)(2,1)S(1)}, bf16[560,128]{1,0:T(8,128)(2,1)S(1)}, u32[]{:S(2)}, u32[]{:S(2)}) collective-permute-start(bf16[560,128]{1,0:T(8,128)(2,1)S(1)} %get-tuple-element.24.refs_0_), channel_id=1, source_target_pairs={{0,1},{1,0},{2,3},{3,2},{4,5},{5,4},{6,7},{7,6},{8,9},{9,8},{10,11... | collective-permute-start | bytes 430088 | tf_op jit(solution)/shard_map/ppermute | solution.py:425
  10.9 12.4 %collective-permute-start.8 = (bf16[560,128]{1,0:T(8,128)(2,1)S(1)}, bf16[560,128]{1,0:T(8,128)(2,1)S(1)}, u32[]{:S(2)}, u32[]{:S(2)}) collective-permute-start(bf16[560,128]{1,0:T(8,128)(2,1)S(1)} %get-tuple-element.24.refs_0_), channel_id=1, source_target_pairs={{0,8},{1,9},{2,10},{3,11},{4,12},{5,13},{6,14},{7,15},{8,0},{9,1},... | collective-permute-start | bytes 430088 | tf_op jit(solution)/shard_map/ppermute | solution.py:425
  14.4 31.3 %collective-permute-start = (bf16[560,128]{1,0:T(8,128)(2,1)S(1)}, bf16[560,128]{1,0:T(8,128)(2,1)S(1)}, u32[]{:S(2)}, u32[]{:S(2)}) collective-permute-start(bf16[560,128]{1,0:T(8,128)(2,1)S(1)} %get-tuple-element.24.refs_0_), channel_id=1, source_target_pairs={{0,4},{1,5},{2,6},{3,7},{4,0},{5,1},{6,2},{7,3},{8,12},{9,13},{10,... | collective-permute-start | bytes 430088 | tf_op jit(solution)/shard_map/ppermute | solution.py:425
  15.3 38.0 %collective-permute-start.19 = (bf16[560,128]{1,0:T(8,128)(2,1)S(1)}, bf16[560,128]{1,0:T(8,128)(2,1)S(1)}, u32[]{:S(2)}, u32[]{:S(2)}) collective-permute-start(bf16[560,128]{1,0:T(8,128)(2,1)S(1)} %collective-permute-done.16.refs_0_), channel_id=1, source_target_pairs={{0,3},{1,2},{2,1},{3,0},{4,7},{5,6},{6,5},{7,4},{8,11},{9,10},{10,... | collective-permute-start | bytes 430088 | tf_op jit(solution)/shard_map/ppermute | solution.py:425
  16.4 36.9 %collective-permute-start.18 = (bf16[560,128]{1,0:T(8,128)(2,1)S(1)}, bf16[560,128]{1,0:T(8,128)(2,1)S(1)}, u32[]{:S(2)}, u32[]{:S(2)}) collective-permute-start(bf16[560,128]{1,0:T(8,128)(2,1)S(1)} %collective-permute-done.16.refs_0_), channel_id=1, source_target_pairs={{0,2},{1,3},{2,0},{3,1},{4,6},{5,7},{6,4},{7,5},{8,10},{9,11},{10,... | collective-permute-start | bytes 430088 | tf_op jit(solution)/shard_map/ppermute | solution.py:425
  16.9 37.1 %collective-permute-start.17 = (bf16[560,128]{1,0:T(8,128)(2,1)S(1)}, bf16[560,128]{1,0:T(8,128)(2,1)S(1)}, u32[]{:S(2)}, u32[]{:S(2)}) collective-permute-start(bf16[560,128]{1,0:T(8,128)(2,1)S(1)} %collective-permute-done.16.refs_0_), channel_id=1, source_target_pairs={{0,1},{1,0},{2,3},{3,2},{4,5},{5,4},{6,7},{7,6},{8,9},{9,8},{10,11... | collective-permute-start | bytes 430088 | tf_op jit(solution)/shard_map/ppermute | solution.py:425
  23.4 32.1 %collective-permute-start.11 = (bf16[560,128]{1,0:T(8,128)(2,1)S(1)}, bf16[560,128]{1,0:T(8,128)(2,1)S(1)}, u32[]{:S(2)}, u32[]{:S(2)}) collective-permute-start(bf16[560,128]{1,0:T(8,128)(2,1)S(1)} %collective-permute-done.8.refs_0_), channel_id=1, source_target_pairs={{0,3},{1,2},{2,1},{3,0},{4,7},{5,6},{6,5},{7,4},{8,11},{9,10},{10,... | collective-permute-start | bytes 430088 | tf_op jit(solution)/shard_map/ppermute | solution.py:425
  45.7 27.0 %collective-permute-start.10 = (bf16[560,128]{1,0:T(8,128)(2,1)S(1)}, bf16[560,128]{1,0:T(8,128)(2,1)S(1)}, u32[]{:S(2)}, u32[]{:S(2)}) collective-permute-start(bf16[560,128]{1,0:T(8,128)(2,1)S(1)} %collective-permute-done.8.refs_0_), channel_id=1, source_target_pairs={{0,2},{1,3},{2,0},{3,1},{4,6},{5,7},{6,4},{7,5},{8,10},{9,11},{10,... | collective-permute-start | bytes 430088 | tf_op jit(solution)/shard_map/ppermute | solution.py:425
  53.3 31.2 %collective-permute-start.9 = (bf16[560,128]{1,0:T(8,128)(2,1)S(1)}, bf16[560,128]{1,0:T(8,128)(2,1)S(1)}, u32[]{:S(2)}, u32[]{:S(2)}) collective-permute-start(bf16[560,128]{1,0:T(8,128)(2,1)S(1)} %collective-permute-done.8.refs_0_), channel_id=1, source_target_pairs={{0,1},{1,0},{2,3},{3,2},{4,5},{5,4},{6,7},{7,6},{8,9},{9,8},{10,11... | collective-permute-start | bytes 430088 | tf_op jit(solution)/shard_map/ppermute | solution.py:425
  53.3 31.2 %collective-permute-start.3 = (bf16[560,128]{1,0:T(8,128)(2,1)S(1)}, bf16[560,128]{1,0:T(8,128)(2,1)S(1)}, u32[]{:S(2)}, u32[]{:S(2)}) collective-permute-start(bf16[560,128]{1,0:T(8,128)(2,1)S(1)} %collective-permute-done.refs_0_), channel_id=1, source_target_pairs={{0,3},{1,2},{2,1},{3,0},{4,7},{5,6},{6,5},{7,4},{8,11},{9,10},{10,... | collective-permute-start | bytes 430088 | tf_op jit(solution)/shard_map/ppermute | solution.py:425
  54.0 32.0 %collective-permute-start.2 = (bf16[560,128]{1,0:T(8,128)(2,1)S(1)}, bf16[560,128]{1,0:T(8,128)(2,1)S(1)}, u32[]{:S(2)}, u32[]{:S(2)}) collective-permute-start(bf16[560,128]{1,0:T(8,128)(2,1)S(1)} %collective-permute-done.refs_0_), channel_id=1, source_target_pairs={{0,2},{1,3},{2,0},{3,1},{4,6},{5,7},{6,4},{7,5},{8,10},{9,11},{10,... | collective-permute-start | bytes 430088 | tf_op jit(solution)/shard_map/ppermute | solution.py:425
  55.5 30.9 %collective-permute-start.1 = (bf16[560,128]{1,0:T(8,128)(2,1)S(1)}, bf16[560,128]{1,0:T(8,128)(2,1)S(1)}, u32[]{:S(2)}, u32[]{:S(2)}) collective-permute-start(bf16[560,128]{1,0:T(8,128)(2,1)S(1)} %collective-permute-done.refs_0_), channel_id=1, source_target_pairs={{0,1},{1,0},{2,3},{3,2},{4,5},{5,4},{6,7},{7,6},{8,9},{9,8},{10,11... | collective-permute-start | bytes 430088 | tf_op jit(solution)/shard_map/ppermute | solution.py:425
  72.7 34.3 %collective-permute-start.27 = (bf16[96,1024]{1,0:T(8,128)(2,1)S(1)}, bf16[96,1024]{1,0:T(8,128)(2,1)S(1)}, u32[]{:S(2)}, u32[]{:S(2)}) collective-permute-start(bf16[96,1024]{1,0:T(8,128)(2,1)S(1)} %get-tuple-element.38), channel_id=1, source_target_pairs={{0,1},{1,0},{2,3},{3,2},{4,5},{5,4},{6,7},{7,6},{8,9},{9,8},{10,11... | collective-permute-start | bytes 589832 | tf_op jit(solution)/shard_map/ppermute | solution.py:425
  84.5 22.6 %collective-permute-start.28 = (bf16[96,1024]{1,0:T(8,128)(2,1)S(1)}, bf16[96,1024]{1,0:T(8,128)(2,1)S(1)}, u32[]{:S(2)}, u32[]{:S(2)}) collective-permute-start(bf16[96,1024]{1,0:T(8,128)(2,1)S(1)} %get-tuple-element.39), channel_id=1, source_target_pairs={{0,2},{1,3},{2,0},{3,1},{4,6},{5,7},{6,4},{7,5},{8,10},{9,11},{10,... | collective-permute-start | bytes 589832 | tf_op jit(solution)/shard_map/ppermute | solution.py:425
  84.5 38.0 %collective-permute-start.29 = (bf16[96,1024]{1,0:T(8,128)(2,1)S(1)}, bf16[96,1024]{1,0:T(8,128)(2,1)S(1)}, u32[]{:S(2)}, u32[]{:S(2)}) collective-permute-start(bf16[96,1024]{1,0:T(8,128)(2,1)S(1)} %get-tuple-element.40), channel_id=1, source_target_pairs={{0,3},{1,2},{2,1},{3,0},{4,7},{5,6},{6,5},{7,4},{8,11},{9,10},{10,... | collective-permute-start | bytes 589832 | tf_op jit(solution)/shard_map/ppermute | solution.py:425
  85.9 36.5 %collective-permute-start.20 = (bf16[96,1024]{1,0:T(8,128)(2,1)S(1)}, bf16[96,1024]{1,0:T(8,128)(2,1)S(1)}, u32[]{:S(2)}, u32[]{:S(2)}) collective-permute-start(bf16[96,1024]{1,0:T(8,128)(2,1)S(1)} %get-tuple-element.33), channel_id=1, source_target_pairs={{0,12},{1,13},{2,14},{3,15},{4,8},{5,9},{6,10},{7,11},{8,4},{9,5},... | collective-permute-start | bytes 589832 | tf_op jit(solution)/shard_map/ppermute | solution.py:425
  86.4 36.2 %collective-permute-start.21 = (bf16[96,1024]{1,0:T(8,128)(2,1)S(1)}, bf16[96,1024]{1,0:T(8,128)(2,1)S(1)}, u32[]{:S(2)}, u32[]{:S(2)}) collective-permute-start(bf16[96,1024]{1,0:T(8,128)(2,1)S(1)} %get-tuple-element.34), channel_id=1, source_target_pairs={{0,13},{1,12},{2,15},{3,14},{4,9},{5,8},{6,11},{7,10},{8,5},{9,4},... | collective-permute-start | bytes 589832 | tf_op jit(solution)/shard_map/ppermute | solution.py:425
  107.0 31.4 %collective-permute-start.22 = (bf16[96,1024]{1,0:T(8,128)(2,1)S(1)}, bf16[96,1024]{1,0:T(8,128)(2,1)S(1)}, u32[]{:S(2)}, u32[]{:S(2)}) collective-permute-start(bf16[96,1024]{1,0:T(8,128)(2,1)S(1)} %get-tuple-element.35), channel_id=1, source_target_pairs={{0,14},{1,15},{2,12},{3,13},{4,10},{5,11},{6,8},{7,9},{8,6},{9,7},... | collective-permute-start | bytes 589832 | tf_op jit(solution)/shard_map/ppermute | solution.py:425
  107.1 50.1 %collective-permute-start.23 = (bf16[96,1024]{1,0:T(8,128)(2,1)S(1)}, bf16[96,1024]{1,0:T(8,128)(2,1)S(1)}, u32[]{:S(2)}, u32[]{:S(2)}) collective-permute-start(bf16[96,1024]{1,0:T(8,128)(2,1)S(1)} %get-tuple-element.36), channel_id=1, source_target_pairs={{0,15},{1,14},{2,13},{3,12},{4,11},{5,10},{6,9},{7,8},{8,7},{9,6},... | collective-permute-start | bytes 589832 | tf_op jit(solution)/shard_map/ppermute | solution.py:425
  122.5 34.8 %collective-permute-start.12 = (bf16[96,1024]{1,0:T(8,128)(2,1)S(1)}, bf16[96,1024]{1,0:T(8,128)(2,1)S(1)}, u32[]{:S(2)}, u32[]{:S(2)}) collective-permute-start(bf16[96,1024]{1,0:T(8,128)(2,1)S(1)} %get-tuple-element.29), channel_id=1, source_target_pairs={{0,8},{1,9},{2,10},{3,11},{4,12},{5,13},{6,14},{7,15},{8,0},{9,1},... | collective-permute-start | bytes 589832 | tf_op jit(solution)/shard_map/ppermute | solution.py:425
  122.5 34.8 %collective-permute-start.13 = (bf16[96,1024]{1,0:T(8,128)(2,1)S(1)}, bf16[96,1024]{1,0:T(8,128)(2,1)S(1)}, u32[]{:S(2)}, u32[]{:S(2)}) collective-permute-start(bf16[96,1024]{1,0:T(8,128)(2,1)S(1)} %get-tuple-element.30), channel_id=1, source_target_pairs={{0,9},{1,8},{2,11},{3,10},{4,13},{5,12},{6,15},{7,14},{8,1},{9,0},... | collective-permute-start | bytes 589832 | tf_op jit(solution)/shard_map/ppermute | solution.py:425
  122.6 37.0 %collective-permute-start.14 = (bf16[96,1024]{1,0:T(8,128)(2,1)S(1)}, bf16[96,1024]{1,0:T(8,128)(2,1)S(1)}, u32[]{:S(2)}, u32[]{:S(2)}) collective-permute-start(bf16[96,1024]{1,0:T(8,128)(2,1)S(1)} %get-tuple-element.31), channel_id=1, source_target_pairs={{0,10},{1,11},{2,8},{3,9},{4,14},{5,15},{6,12},{7,13},{8,2},{9,3},... | collective-permute-start | bytes 589832 | tf_op jit(solution)/shard_map/ppermute | solution.py:425
  138.4 28.4 %collective-permute-start.15 = (bf16[96,1024]{1,0:T(8,128)(2,1)S(1)}, bf16[96,1024]{1,0:T(8,128)(2,1)S(1)}, u32[]{:S(2)}, u32[]{:S(2)}) collective-permute-start(bf16[96,1024]{1,0:T(8,128)(2,1)S(1)} %get-tuple-element.32), channel_id=1, source_target_pairs={{0,11},{1,10},{2,9},{3,8},{4,15},{5,14},{6,13},{7,12},{8,3},{9,2},... | collective-permute-start | bytes 589832 | tf_op jit(solution)/shard_map/ppermute | solution.py:425
  157.2 12.2 %collective-permute-start.4 = (bf16[96,1024]{1,0:T(8,128)(2,1)S(1)}, bf16[96,1024]{1,0:T(8,128)(2,1)S(1)}, u32[]{:S(2)}, u32[]{:S(2)}) collective-permute-start(bf16[96,1024]{1,0:T(8,128)(2,1)S(1)} %get-tuple-element.25), channel_id=1, source_target_pairs={{0,4},{1,5},{2,6},{3,7},{4,0},{5,1},{6,2},{7,3},{8,12},{9,13},{10,... | collective-permute-start | bytes 589832 | tf_op jit(solution)/shard_map/ppermute | solution.py:425
  157.2 13.1 %collective-permute-start.5 = (bf16[96,1024]{1,0:T(8,128)(2,1)S(1)}, bf16[96,1024]{1,0:T(8,128)(2,1)S(1)}, u32[]{:S(2)}, u32[]{:S(2)}) collective-permute-start(bf16[96,1024]{1,0:T(8,128)(2,1)S(1)} %get-tuple-element.26), channel_id=1, source_target_pairs={{0,5},{1,4},{2,7},{3,6},{4,1},{5,0},{6,3},{7,2},{8,13},{9,12},{10,... | collective-permute-start | bytes 589832 | tf_op jit(solution)/shard_map/ppermute | solution.py:425
  157.3 19.1 %collective-permute-start.6 = (bf16[96,1024]{1,0:T(8,128)(2,1)S(1)}, bf16[96,1024]{1,0:T(8,128)(2,1)S(1)}, u32[]{:S(2)}, u32[]{:S(2)}) collective-permute-start(bf16[96,1024]{1,0:T(8,128)(2,1)S(1)} %get-tuple-element.27), channel_id=1, source_target_pairs={{0,6},{1,7},{2,4},{3,5},{4,2},{5,3},{6,0},{7,1},{8,14},{9,15},{10,... | collective-permute-start | bytes 589832 | tf_op jit(solution)/shard_map/ppermute | solution.py:425
  159.6 21.0 %collective-permute-start.7 = (bf16[96,1024]{1,0:T(8,128)(2,1)S(1)}, bf16[96,1024]{1,0:T(8,128)(2,1)S(1)}, u32[]{:S(2)}, u32[]{:S(2)}) collective-permute-start(bf16[96,1024]{1,0:T(8,128)(2,1)S(1)} %get-tuple-element.28), channel_id=1, source_target_pairs={{0,7},{1,6},{2,5},{3,4},{4,3},{5,2},{6,1},{7,0},{8,15},{9,14},{10,... | collective-permute-start | bytes 589832 | tf_op jit(solution)/shard_map/ppermute | solution.py:425
